TPU v7x, 32 devices: a whole 2x2x4 slice. The times are simulated.
32 devices in a mesh: seq: 8 (over z, core), rows: 4 (over y, x).
Axes of the slice: x: 2, y: 2, z: 4, core: 2. Of those that a mesh axis runs over, the one named last changes fastest.
Arguments:
- tokens: bfloat16 [2, 4, 1024, 2048], P(None, 'rows', 'seq'), may hold values from -6 to 6
- w_query: bfloat16 [2048, 2048], P(('seq', 'rows')), may hold values from -0.125 to 0.125
- w_key: bfloat16 [2048, 256], P(('seq', 'rows')), may hold values from -0.125 to 0.125
- w_value: bfloat16 [2048, 256], P(('seq', 'rows')), may hold values from -0.125 to 0.125
- w_out: bfloat16 [2048, 2048], P(('seq', 'rows')), may hold values from -0.75 to 0.75
- w_gate: bfloat16 [2048, 5632], P(('seq', 'rows')), may hold values from -0.125 to 0.125
- w_up: bfloat16 [2048, 5632], P(('seq', 'rows')), may hold values from -0.125 to 0.125
- w_down: bfloat16 [5632, 2048], P(('seq', 'rows')), may hold values from -0.078125 to 0.078125
- gain_attn: bfloat16 [2048], P(('seq', 'rows')), may hold values from 0.5 to 1.5
- gain_ffn: bfloat16 [2048], P(('seq', 'rows')), may hold values from 0.5 to 1.5
- lengths: int32 [2, 4, 2], P(None, 'rows'), may hold values from 512 to 512, as said below
- order: int32 [16], replicated, may hold values from 0 to 15, each once
- cotangent: bfloat16 [2, 4, 1024, 2048], P(None, 'rows', 'seq'), may hold values from -6 to 6
Outputs:
- output: bfloat16 [2, 4, 1024, 2048], P(None, 'rows', 'seq')
- x_grad: bfloat16 [2, 4, 1024, 2048], P(None, 'rows', 'seq')
- w_query_grad: float32 [2048, 2048], P(('seq', 'rows'))
- w_key_grad: float32 [2048, 256], P(('seq', 'rows'))
- w_value_grad: float32 [2048, 256], P(('seq', 'rows'))
- w_out_grad: float32 [2048, 2048], P(('seq', 'rows'))
- w_gate_grad: float32 [2048, 5632], P(('seq', 'rows'))
- w_up_grad: float32 [2048, 5632], P(('seq', 'rows'))
- w_down_grad: float32 [5632, 2048], P(('seq', 'rows'))
- gain_attn_grad: float32 [2048], P(('seq', 'rows'))
- gain_ffn_grad: float32 [2048], P(('seq', 'rows'))
Inputs may be any that keep to these rules, and one draw needn't show every extreme that they name: lengths[m, r] holds the first then the second sequence of row r of micro-batch m; the two add up to 1024. `order`: each block number appears once; index i of seq holds slot blocks 2 i and 2 i + 1.
All inputs are finite; a program needn't handle non-finite values.
Results may differ from a plain program's by a relative error of at most 0.022.
Values may be sent and summed in bfloat16 or wider, within the bound.
A program may use at most 384 MiB of HBM per device.

v0:
```python
import math

import jax
import jax.numpy as jnp
from jax import lax
from jax.sharding import PartitionSpec as P

D = 2048
HEADS = 32
KV_HEADS = 4
HEAD_DIM = 64
GROUP = 8
KVW = 256


EPSILON = 1e-05
NEG_LARGE = -1e30


def rms_scaled(values, gain_vec):
    return (
        values * lax.rsqrt(jnp.mean(values * values, axis=-1, keepdims=True) + EPSILON) * gain_vec
    )


def angle_tables(position):
    width_half = HEAD_DIM // 2
    inverse = 10000.0 ** (-jnp.arange(width_half, dtype=jnp.float32) / width_half)
    angles = position[..., None] * inverse
    return (jnp.cos(angles), jnp.sin(angles))


def rotate_pairs(tensor, cosine, sine):
    width_half = tensor.shape[-1] // 2
    first_half = tensor[..., :width_half]
    second_half = tensor[..., width_half:]
    return jnp.concatenate(
        [first_half * cosine - second_half * sine, second_half * cosine + first_half * sine],
        axis=-1,
    )


def product(left, right):
    return jnp.dot(left, right, preferred_element_type=jnp.float32)


def slot_places(order, half_len, slot_ids):
    matches = (slot_ids // half_len)[:, None] == jnp.arange(order.shape[0], dtype=jnp.int32)[
        None, :
    ]
    return jnp.sum(jnp.where(matches, order[None, :], 0), axis=1) * half_len + slot_ids % half_len


def one_row(full, row_tokens, row_cot, first_len, mine, order, half_len):
    query_w, key_w, value_w, out_w, gate_w, up_w, down_w, gain_one, gain_two = full
    span = row_tokens.shape[0]
    scale = 1.0 / math.sqrt(HEAD_DIM)
    gain_first = gain_one.astype(jnp.float32)
    gain_second = gain_two.astype(jnp.float32)
    seq_start = jnp.where(mine >= first_len, first_len, 0)
    cosine, sine = angle_tables((mine - seq_start).astype(jnp.float32))
    cos_heads = cosine[:, None, :]
    sin_heads = sine[:, None, :]

    def rotate_heads(tensor):
        return rotate_pairs(tensor, cos_heads, sin_heads)

    x_float = row_tokens.astype(jnp.float32)
    attn_in = rms_scaled(x_float, gain_first).astype(jnp.bfloat16)
    q_lin = product(attn_in, query_w).reshape(span, HEADS, HEAD_DIM)
    k_lin = product(attn_in, key_w).reshape(span, KV_HEADS, HEAD_DIM)
    values_own = product(attn_in, value_w).astype(jnp.bfloat16)
    queries = rotate_heads(q_lin).astype(jnp.bfloat16).reshape(span, KV_HEADS, GROUP, HEAD_DIM)
    keys_own = rotate_heads(k_lin).astype(jnp.bfloat16).reshape(span, KVW)

    def key_view(fetched):
        key_block, value_block = fetched
        count = key_block.shape[0]
        key_place = slot_places(order, half_len, jnp.arange(count, dtype=jnp.int32))
        allowed = (key_place[None, :] <= mine[:, None]) & (key_place[None, :] >= seq_start[:, None])
        key_heads = key_block.reshape(count, KV_HEADS, HEAD_DIM)
        value_heads = value_block.reshape(count, KV_HEADS, HEAD_DIM)
        scores = (
            jnp.einsum("tkgd,skd->kgts", queries, key_heads, preferred_element_type=jnp.float32)
            * scale
        )
        return (key_heads, value_heads, allowed[None, None], scores)

    top_now = jnp.full((KV_HEADS, GROUP, span), NEG_LARGE, jnp.float32)
    key_heads, value_heads, allowed, scores = key_view(
        (
            lax.all_gather(keys_own, "seq", axis=0, tiled=True),
            lax.all_gather(values_own, "seq", axis=0, tiled=True),
        )
    )
    scores = jnp.where(allowed, scores, NEG_LARGE)
    top_next = jnp.maximum(top_now, jnp.max(scores, axis=-1))
    exps = jnp.where(allowed, jnp.exp(scores - top_next[..., None]), 0.0)
    total_next = jnp.sum(exps, axis=-1)
    summed = jnp.einsum(
        "kgts,skd->kgtd", exps.astype(jnp.bfloat16), value_heads, preferred_element_type=jnp.float32
    )
    log_total = top_next + jnp.log(total_next)
    attn_float = jnp.transpose(summed / total_next[..., None], (2, 0, 1, 3)).reshape(span, D)
    attended = attn_float.astype(jnp.bfloat16)
    middle = x_float + product(attended, out_w)
    ffn_in = rms_scaled(middle, gain_second).astype(jnp.bfloat16)
    gate = product(ffn_in, gate_w)
    upper = product(ffn_in, up_w)
    hidden = (gate * jax.nn.sigmoid(gate) * upper).astype(jnp.bfloat16)
    result = (middle + product(hidden, down_w)).astype(jnp.bfloat16)
    d_hidden = product(row_cot, down_w.T)
    grad_down = product(hidden.T, row_cot)

    def swiglu(gate_in, upper_in):
        return gate_in * jax.nn.sigmoid(gate_in) * upper_in

    unused_one, swiglu_back = jax.vjp(swiglu, gate, upper)
    d_gate, d_upper = swiglu_back(d_hidden)
    d_gate = d_gate.astype(jnp.bfloat16)
    d_upper = d_upper.astype(jnp.bfloat16)
    grad_gate = product(ffn_in.T, d_gate)
    grad_up = product(ffn_in.T, d_upper)
    d_ffn_in = product(d_gate, gate_w.T) + product(d_upper, up_w.T)
    unused_two, norm_two_back = jax.vjp(rms_scaled, middle, gain_second)
    d_middle_part, grad_gain_two = norm_two_back(d_ffn_in)
    d_middle = row_cot.astype(jnp.float32) + d_middle_part
    d_mid_low = d_middle.astype(jnp.bfloat16)
    grad_out = product(attended.T, d_mid_low)
    d_attended = product(d_mid_low, out_w.T).astype(jnp.bfloat16)
    d_heads = d_attended.reshape(span, KV_HEADS, GROUP, HEAD_DIM)
    delta = jnp.transpose(
        jnp.sum(
            d_heads.astype(jnp.float32) * attn_float.reshape(span, KV_HEADS, GROUP, HEAD_DIM),
            axis=-1,
        ),
        (1, 2, 0),
    )
    key_heads, value_heads, allowed, scores = key_view(
        (
            lax.all_gather(keys_own, "seq", axis=0, tiled=True),
            lax.all_gather(values_own, "seq", axis=0, tiled=True),
        )
    )
    count = key_heads.shape[0]
    probs = jnp.where(allowed, jnp.exp(scores - log_total[..., None]), 0.0)
    d_probs = jnp.einsum("tkgd,skd->kgts", d_heads, value_heads, preferred_element_type=jnp.float32)
    d_scores = (probs * (d_probs - delta[..., None])).astype(jnp.bfloat16)
    d_query = (
        jnp.einsum("kgts,skd->tkgd", d_scores, key_heads, preferred_element_type=jnp.float32)
        * scale
    )
    key_term = (
        jnp.einsum("kgts,tkgd->skd", d_scores, queries, preferred_element_type=jnp.float32) * scale
    ).reshape(count, KVW)
    value_term = jnp.einsum(
        "kgts,tkgd->skd", probs.astype(jnp.bfloat16), d_heads, preferred_element_type=jnp.float32
    ).reshape(count, KVW)
    d_keys_all = key_term
    d_values_all = value_term
    d_query, d_keys_all, d_values_all = (d_query, d_keys_all, d_values_all)
    d_keys, d_values = (
        lax.psum_scatter(
            d_keys_all.astype(jnp.bfloat16), "seq", scatter_dimension=0, tiled=True
        ).astype(jnp.float32),
        lax.psum_scatter(
            d_values_all.astype(jnp.bfloat16), "seq", scatter_dimension=0, tiled=True
        ).astype(jnp.float32),
    )
    unused_three, rotate_query_back = jax.vjp(rotate_heads, q_lin)
    d_q_lin = (
        rotate_query_back(d_query.reshape(span, HEADS, HEAD_DIM))[0]
        .reshape(span, D)
        .astype(jnp.bfloat16)
    )
    unused_four, rotate_key_back = jax.vjp(rotate_heads, k_lin)
    d_k_lin = (
        rotate_key_back(d_keys.reshape(span, KV_HEADS, HEAD_DIM))[0]
        .reshape(span, KVW)
        .astype(jnp.bfloat16)
    )
    d_v_lin = d_values.astype(jnp.bfloat16)
    grad_query = product(attn_in.T, d_q_lin)
    grad_key = product(attn_in.T, d_k_lin)
    grad_value = product(attn_in.T, d_v_lin)
    d_attn_in = (
        product(d_q_lin, query_w.T) + product(d_k_lin, key_w.T) + product(d_v_lin, value_w.T)
    )
    unused_five, norm_one_back = jax.vjp(rms_scaled, x_float, gain_first)
    d_x_part, grad_gain_one = norm_one_back(d_attn_in)
    x_grad = (d_middle + d_x_part).astype(jnp.bfloat16)
    return (
        result,
        x_grad,
        (
            grad_query,
            grad_key,
            grad_value,
            grad_out,
            grad_gate,
            grad_up,
            grad_down,
            grad_gain_one,
            grad_gain_two,
        ),
    )


def on_device(
    tokens,
    w_query,
    w_key,
    w_value,
    w_out,
    w_gate,
    w_up,
    w_down,
    gain_attn,
    gain_ffn,
    lengths,
    order,
    cotangent,
):
    span = tokens.shape[2]
    half_len = span // 2
    mine = slot_places(
        order, half_len, lax.axis_index("seq") * span + jnp.arange(span, dtype=jnp.int32)
    )
    results = []
    x_grads = []
    totals = None
    grads = None
    for micro_step in range(tokens.shape[0]):
        full = (
            lax.all_gather(w_query, ("seq", "rows"), axis=0, tiled=True),
            lax.all_gather(w_key, ("seq", "rows"), axis=0, tiled=True),
            lax.all_gather(w_value, ("seq", "rows"), axis=0, tiled=True),
            lax.all_gather(w_out, ("seq", "rows"), axis=0, tiled=True),
            lax.all_gather(w_gate, ("seq", "rows"), axis=0, tiled=True),
            lax.all_gather(w_up, ("seq", "rows"), axis=0, tiled=True),
            lax.all_gather(w_down, ("seq", "rows"), axis=0, tiled=True),
            lax.all_gather(gain_attn, ("seq", "rows"), axis=0, tiled=True),
            lax.all_gather(gain_ffn, ("seq", "rows"), axis=0, tiled=True),
        )
        micro_totals = None
        result, x_grad, terms = one_row(
            full,
            tokens[micro_step, 0],
            cotangent[micro_step, 0],
            lengths[micro_step, 0, 0],
            mine,
            order,
            half_len,
        )
        results.append(result)
        x_grads.append(x_grad)
        micro_totals = terms
        totals = micro_totals if totals is None else jax.tree.map(jnp.add, totals, micro_totals)
    grads = (
        lax.psum_scatter(totals[0], ("seq", "rows"), scatter_dimension=0, tiled=True),
        lax.psum_scatter(totals[1], ("seq", "rows"), scatter_dimension=0, tiled=True),
        lax.psum_scatter(totals[2], ("seq", "rows"), scatter_dimension=0, tiled=True),
        lax.psum_scatter(totals[3], ("seq", "rows"), scatter_dimension=0, tiled=True),
        lax.psum_scatter(totals[4], ("seq", "rows"), scatter_dimension=0, tiled=True),
        lax.psum_scatter(totals[5], ("seq", "rows"), scatter_dimension=0, tiled=True),
        lax.psum_scatter(totals[6], ("seq", "rows"), scatter_dimension=0, tiled=True),
        lax.psum_scatter(totals[7], ("seq", "rows"), scatter_dimension=0, tiled=True),
        lax.psum_scatter(totals[8], ("seq", "rows"), scatter_dimension=0, tiled=True),
    )
    output = jnp.stack(results).reshape(tokens.shape)
    input_grad = jnp.stack(x_grads).reshape(tokens.shape)
    return (
        output,
        input_grad,
        grads[0],
        grads[1],
        grads[2],
        grads[3],
        grads[4],
        grads[5],
        grads[6],
        grads[7],
        grads[8],
    )


def solution(mesh):
    return jax.shard_map(
        on_device,
        mesh=mesh,
        in_specs=(
            P(None, "rows", "seq", None),
            P(("seq", "rows"), None),
            P(("seq", "rows"), None),
            P(("seq", "rows"), None),
            P(("seq", "rows"), None),
            P(("seq", "rows"), None),
            P(("seq", "rows"), None),
            P(("seq", "rows"), None),
            P(("seq", "rows")),
            P(("seq", "rows")),
            P(None, "rows", None),
            P(),
            P(None, "rows", "seq", None),
        ),
        out_specs=(
            P(None, "rows", "seq", None),
            P(None, "rows", "seq", None),
            P(("seq", "rows"), None),
            P(("seq", "rows"), None),
            P(("seq", "rows"), None),
            P(("seq", "rows"), None),
            P(("seq", "rows"), None),
            P(("seq", "rows"), None),
            P(("seq", "rows"), None),
            P(("seq", "rows")),
            P(("seq", "rows")),
        ),
        check_vma=False,
    )
```

profile of v0, /device:TPU:8, one launch (start us, length us, event | category | flops | bytes accessed | tf_op | source)
XLA Modules:
  0.0 4895.0 jit_solution(5910732682120993875)
XLA Ops:
  13.7 40.7 all-reduce.13
  66.7 54.2 %all-gather.12.cloned.1.call-done = bf16[2048,256]{1,0:T(8,128)(2,1)} async-done(((bf16[64,256]{1,0:T(8,128)(2,1)}), bf16[2048,256]{1,0:T(8,128)(2,1)}) %all-gather.12.cloned.1.call-update) | async-done | bytes 1048592 | tf_op jit(solution)/shard_map/all_gather | solution.py:237
  122.7 14.6 all_gather.57
  139.9 16.0 all_gather.64
  158.1 16.0 all_gather.54
  174.1 17.9 all_gather.63
  192.0 12.9 all-gather.10.cloned.1.call-done
  236.0 49.0 %all-gather.14.cloned.1.call-done = bf16[2048,2048]{1,0:T(8,128)(2,1)} async-done(((bf16[64,2048]{1,0:T(8,128)(2,1)}), bf16[2048,2048]{1,0:T(8,128)(2,1)}) %all-gather.14.cloned.1.call-update) | async-done | bytes 8388624 | tf_op jit(solution)/shard_map/all_gather | solution.py:238
  315.2 114.0 %all-gather.16.cloned.1.call-done = bf16[2048,5632]{1,0:T(8,128)(2,1)} async-done(((bf16[64,5632]{1,0:T(8,128)(2,1)}), bf16[2048,5632]{1,0:T(8,128)(2,1)}) %all-gather.16.cloned.1.call-update) | async-done | bytes 23068688 | tf_op jit(solution)/shard_map/all_gather | solution.py:239
  441.5 133.3 %all-gather.18.cloned.1.call-done = bf16[2048,5632]{1,0:T(8,128)(2,1)} async-done(((bf16[64,5632]{1,0:T(8,128)(2,1)}), bf16[2048,5632]{1,0:T(8,128)(2,1)}) %all-gather.18.cloned.1.call-update) | async-done | bytes 23068688 | tf_op jit(solution)/shard_map/all_gather | solution.py:240
  574.7 12.3 fusion.177
  587.1 133.4 %all-gather.20.cloned.1.call-done = bf16[5632,2048]{1,0:T(8,128)(2,1)} async-done(((bf16[176,2048]{1,0:T(8,128)(2,1)}), bf16[5632,2048]{1,0:T(8,128)(2,1)}) %all-gather.20.cloned.1.call-update) | async-done | bytes 23068688 | tf_op jit(solution)/shard_map/all_gather | solution.py:241
  720.4 15.4 multiply_convert_fusion.1
  735.9 13.3 fusion.180
  749.2 13.9 multiply_reduce_fusion.1
  763.1 12.5 fusion.179
  787.9 15.6 multiply_convert_fusion
  815.7 13.7 multiply_reduce_fusion
  910.6 27.7 reduce-scatter.34.cloned.1.call-done
  939.3 31.1 reduce-scatter.38.cloned.1.call-done
  1010.2 18.0 fusion.185
  1028.2 29.3 convolution_add_fusion.1
  1058.8 18.1 fusion.184
  1076.9 29.3 convolution_add_fusion.2
  1107.9 17.9 fusion.103
  1125.8 29.6 convolution_add_fusion
  1190.2 43.2 all-reduce.12
  1237.8 366.7 %reduce-scatter.26.cloned.1.call-done = f32[64,2048]{1,0:T(8,128)} async-done(((f32[2048,2048]{1,0:T(8,128)}), f32[64,2048]{1,0:T(8,128)}) %reduce-scatter.26.cloned.1.call-update) | async-done | bytes 524304 | tf_op jit(solution)/shard_map/reduce_scatter | solution.py:263
  1604.5 361.8 %reduce-scatter.20.cloned.1.call-done = f32[64,2048]{1,0:T(8,128)} async-done(((f32[2048,2048]{1,0:T(8,128)}), f32[64,2048]{1,0:T(8,128)}) %reduce-scatter.20.cloned.1.call-update) | async-done | bytes 524304 | tf_op jit(solution)/shard_map/reduce_scatter | solution.py:260
  1966.4 974.5 %reduce-scatter.30.cloned.1.call-done = f32[64,5632]{1,0:T(8,128)} async-done(((f32[2048,5632]{1,0:T(8,128)}), f32[64,5632]{1,0:T(8,128)}) %reduce-scatter.30.cloned.1.call-update) | async-done | bytes 1441808 | tf_op jit(solution)/shard_map/reduce_scatter | solution.py:265
  2940.8 973.6 %reduce-scatter.28.cloned.1.call-done = f32[64,5632]{1,0:T(8,128)} async-done(((f32[2048,5632]{1,0:T(8,128)}), f32[64,5632]{1,0:T(8,128)}) %reduce-scatter.28.cloned.1.call-update) | async-done | bytes 1441808 | tf_op jit(solution)/shard_map/reduce_scatter | solution.py:264
  3914.4 973.5 %reduce-scatter.32.cloned.1.call-done = f32[176,2048]{1,0:T(8,128)} async-done(((f32[5632,2048]{1,0:T(8,128)}), f32[176,2048]{1,0:T(8,128)}) %reduce-scatter.32.cloned.1.call-update) | async-done | bytes 1441808 | tf_op jit(solution)/shard_map/reduce_scatter | solution.py:266
  (338 shorter events, 285.9 us)
Async XLA Ops:
  7.2 131.1 %copy-start.2 = (bf16[2,1,128,2048]{3,2,1,0:T(8,128)(2,1)S(1)}, bf16[2,1,128,2048]{3,2,1,0:T(8,128)(2,1)}, u32[]{:S(2)}) copy-start(bf16[2,1,128,2048]{3,2,1,0:T(8,128)(2,1)} %param.13) | copy-start | bytes 3145732
  7.2 58.0 %all-gather.8.cloned.1.call-start = ((), (), s32[]{:S(2)}) async-start(), calls=%async_computation.11 | async-start | bytes 1081344 | tf_op jit(solution)/shard_map/all_gather | solution.py:236
  7.9 113.0 %all-gather.12.cloned.1.call-start = ((), (), s32[]{:S(2)}) async-start(), calls=%async_computation.13 | async-start | bytes 1081344 | tf_op jit(solution)/shard_map/all_gather | solution.py:237
  8.7 196.2 %all-gather.10.cloned.1.call-start = ((), (), s32[]{:S(2)}) async-start(), calls=%async_computation.12 | async-start | bytes 8650752 | tf_op jit(solution)/shard_map/all_gather | solution.py:235
  9.4 275.6 %all-gather.14.cloned.1.call-start = ((), (), s32[]{:S(2)}) async-start(), calls=%async_computation.14 | async-start | bytes 8650752 | tf_op jit(solution)/shard_map/all_gather | solution.py:238
  10.0 419.2 %all-gather.16.cloned.1.call-start = ((), (), s32[]{:S(2)}) async-start(), calls=%async_computation.15 | async-start | bytes 23789568 | tf_op jit(solution)/shard_map/all_gather | solution.py:239
  10.6 564.2 %all-gather.18.cloned.1.call-start = ((), (), s32[]{:S(2)}) async-start(), calls=%async_computation.16 | async-start | bytes 23789568 | tf_op jit(solution)/shard_map/all_gather | solution.py:240
  11.1 709.3 %all-gather.20.cloned.1.call-start = ((), (), s32[]{:S(2)}) async-start(), calls=%async_computation.17 | async-start | bytes 23789568 | tf_op jit(solution)/shard_map/all_gather | solution.py:241
  11.9 888.0 %reduce-scatter.36.cloned.1.call-start = ((), (), s32[]{:S(2)}) async-start(), calls=%async_computation.26 | async-start | bytes 589824
  54.3 235.5 %copy-start.54 = (f32[2048]{0:T(1024)}, f32[2048]{0:T(1024)S(1)}, u32[]{:S(2)}) copy-start(f32[2048]{0:T(1024)S(1)} %convert_element_type.251) | copy-start | bytes 24580
  59.1 157.7 %copy-start.76 = (f32[128]{0:T(128)}, f32[128]{0:T(128)S(1)}, u32[]{:S(2)}) copy-start(f32[128]{0:T(128)S(1)} %fusion.146) | copy-start | bytes 1540
  59.1 230.7 %copy-start.79 = (f32[128]{0:T(128)}, f32[128]{0:T(128)S(1)}, u32[]{:S(2)}) copy-start(f32[128]{0:T(128)S(1)} %fusion.148) | copy-start | bytes 1540
  61.3 161.3 %copy-start.68 = (f32[128,32]{0,1:T(8,128)}, f32[128,32]{0,1:T(8,128)S(1)}, u32[]{:S(2)}) copy-start(f32[128,32]{0,1:T(8,128)S(1)} %get-tuple-element.102) | copy-start | bytes 49156
  61.3 161.3 %copy-start.70 = (f32[128,32]{0,1:T(8,128)}, f32[128,32]{0,1:T(8,128)S(1)}, u32[]{:S(2)}) copy-start(f32[128,32]{0,1:T(8,128)S(1)} %get-tuple-element.103) | copy-start | bytes 49156
  61.3 234.7 %copy-start.64 = (f32[128,32]{0,1:T(8,128)}, f32[128,32]{0,1:T(8,128)S(1)}, u32[]{:S(2)}) copy-start(f32[128,32]{0,1:T(8,128)S(1)} %get-tuple-element.108) | copy-start | bytes 49156
  61.3 234.7 %copy-start.66 = (f32[128,32]{0,1:T(8,128)}, f32[128,32]{0,1:T(8,128)S(1)}, u32[]{:S(2)}) copy-start(f32[128,32]{0,1:T(8,128)S(1)} %get-tuple-element.109) | copy-start | bytes 49156
  62.3 167.3 %copy-start.52 = (pred[128,1024]{0,1:T(8,128)(4,1)}, pred[128,1024]{0,1:T(8,128)(4,1)S(1)}, u32[]{:S(2)}) copy-start(pred[128,1024]{0,1:T(8,128)(4,1)S(1)} %get-tuple-element.100) | copy-start | bytes 393220
  289.7 539.7 %copy-start.7 = (f32[128,2048]{1,0:T(8,128)}, f32[128,2048]{1,0:T(8,128)S(1)}, u32[]{:S(2)}) copy-start(f32[128,2048]{1,0:T(8,128)S(1)} %get-tuple-element.122) | copy-start | bytes 3145732
  314.4 515.1 %copy-start.9 = (f32[128,2048]{1,0:T(8,128)}, f32[128,2048]{1,0:T(8,128)S(1)}, u32[]{:S(2)}) copy-start(f32[128,2048]{1,0:T(8,128)S(1)} %get-tuple-element.124) | copy-start | bytes 3145732
  315.1 259.6 %copy-start.16 = (bf16[128,2048]{1,0:T(8,128)(2,1)}, bf16[128,2048]{1,0:T(8,128)(2,1)S(1)}, u32[]{:S(2)}) copy-start(bf16[128,2048]{1,0:T(8,128)(2,1)S(1)} %multiply_convert_fusion.5) | copy-start | bytes 1572868
  832.0 146.1 %copy-start.11 = (f32[128,2048]{1,0:T(8,128)}, f32[128,2048]{1,0:T(8,128)S(1)}, u32[]{:S(2)}) copy-start(f32[128,2048]{1,0:T(8,128)S(1)} %get-tuple-element.90) | copy-start | bytes 3145732
  848.2 58.8 %reduce-scatter.40.cloned.1.call-start = ((), (), s32[]{:S(2)}) async-start(), calls=%async_computation.28 | async-start | bytes 589824
  866.9 71.4 %reduce-scatter.34.cloned.1.call-start = ((), (), s32[]{:S(2)}) async-start(), calls=%async_computation.25 | async-start | bytes 589824
  883.9 86.6 %reduce-scatter.38.cloned.1.call-start = ((), (), s32[]{:S(2)}) async-start(), calls=%async_computation.27 | async-start | bytes 589824
  896.1 75.3 %copy-start.69 = (f32[128,32]{0,1:T(8,128)S(1)}, f32[128,32]{0,1:T(8,128)}, u32[]{:S(2)}) copy-start(f32[128,32]{0,1:T(8,128)} %copy-done.68) | copy-start | bytes 49156
  899.8 338.0 %reduce-scatter.24.cloned.1.call-start = ((), (), s32[]{:S(2)}) async-start(), calls=%async_computation.20 | async-start | bytes 2162688 | tf_op jit(solution)/shard_map/reduce_scatter | solution.py:262
  910.5 327.3 %reduce-scatter.22.cloned.1.call-start = ((), (), s32[]{:S(2)}) async-start(), calls=%async_computation.19 | async-start | bytes 2162688 | tf_op jit(solution)/shard_map/reduce_scatter | solution.py:261
  974.6 630.0 %reduce-scatter.26.cloned.1.call-start = ((), (), s32[]{:S(2)}) async-start(), calls=%async_computation.21 | async-start | bytes 17301504 | tf_op jit(solution)/shard_map/reduce_scatter | solution.py:263
  986.2 980.1 %reduce-scatter.20.cloned.1.call-start = ((), (), s32[]{:S(2)}) async-start(), calls=%async_computation.18 | async-start | bytes 17301504 | tf_op jit(solution)/shard_map/reduce_scatter | solution.py:260
  1008.7 1932.1 %reduce-scatter.30.cloned.1.call-start = ((), (), s32[]{:S(2)}) async-start(), calls=%async_computation.23 | async-start | bytes 47579136 | tf_op jit(solution)/shard_map/reduce_scatter | solution.py:265
  1057.5 2856.9 %reduce-scatter.28.cloned.1.call-start = ((), (), s32[]{:S(2)}) async-start(), calls=%async_computation.22 | async-start | bytes 47579136 | tf_op jit(solution)/shard_map/reduce_scatter | solution.py:264
  1106.2 3781.7 %reduce-scatter.32.cloned.1.call-start = ((), (), s32[]{:S(2)}) async-start(), calls=%async_computation.24 | async-start | bytes 47579136 | tf_op jit(solution)/shard_map/reduce_scatter | solution.py:266
  (78 other events, 1037.6 us)
Sparse Core Ops, SparseCore 0:
  11.0 54.1 all-gather.7
  68.2 52.6 all-gather.11
  123.8 81.0 all-gather.9
  207.6 77.3 all-gather.13
  287.7 141.4 all-gather.15
  431.9 142.7 all-gather.17
  577.6 142.7 all-gather.19
  848.3 27.3 reduce-scatter.35
  878.1 28.8 reduce-scatter.39
  909.1 29.1 reduce-scatter.33
  941.3 29.1 reduce-scatter.37
  973.1 127.0 reduce-scatter.23
  1103.1 132.8 reduce-scatter.21
  1238.7 365.8 reduce-scatter.25
  1607.3 359.0 reduce-scatter.19
  1969.1 971.6 reduce-scatter.29
  2943.6 970.7 reduce-scatter.27
  3917.1 970.7 reduce-scatter.31
where the time goes:
time: 4900 us; the launch traced here: 4890 us
  waiting for transfers between devices  4220 us (86%)
  matrix products  438 us (9%)
  blocking collectives  148 us (3%)
    reduce_scatter x1, waiting for transfers between devices, on_device(): lax.psum_scatter(totals[5], ('seq', 'rows'), scatter_dimension=0, tiled=T...  974 us
    reduce_scatter x1, waiting for transfers between devices, on_device(): lax.psum_scatter(totals[4], ('seq', 'rows'), scatter_dimension=0, tiled=T...  974 us
    reduce_scatter x1, waiting for transfers between devices, on_device(): lax.psum_scatter(totals[6], ('seq', 'rows'), scatter_dimension=0, tiled=T...  974 us
    dot_general x42, matrix products, product(): return jnp.dot(left, right, preferred_element_type=jnp.float32)  374 us
    reduce_scatter x1, waiting for transfers between devices, on_device(): lax.psum_scatter(totals[3], ('seq', 'rows'), scatter_dimension=0, tiled=T...  367 us
    reduce_scatter x1, waiting for transfers between devices, on_device(): lax.psum_scatter(totals[0], ('seq', 'rows'), scatter_dimension=0, tiled=T...  362 us
    all_gather x1, waiting for transfers between devices, on_device(): lax.all_gather(w_down, ('seq', 'rows'), axis=0, tiled=True)  133 us
    all_gather x1, waiting for transfers between devices, on_device(): lax.all_gather(w_up, ('seq', 'rows'), axis=0, tiled=True)  133 us
  transfers between devices with their start and end apart: 18, of which 15 were waited for; matrix products, arithmetic and copies ran while one was open for 7% of the time, Pallas kernels for 0%

commit v1 on v0

v1 whole, which is shorter than its diff:
```python
import functools
import math

import jax
import jax.numpy as jnp
from jax import lax
from jax.experimental import pallas as pl
from jax.experimental.pallas import tpu as pltpu
from jax.sharding import PartitionSpec as P

D = 2048
HEADS = 32
KV_HEADS = 4
HEAD_DIM = 64
GROUP = 8
KVW = 256
QKV = D + 2 * KVW
PACK = QKV + D + 128

EPSILON = 1e-05
NEG_LARGE = -1e30
MESH = pl.DeviceIdType.MESH
MIB = 1 << 20


def product(left, right):
    return jnp.dot(left, right, preferred_element_type=jnp.float32)


def product_nt(left, right):
    return lax.dot_general(left, right, (((1,), (1,)), ((), ())), preferred_element_type=jnp.float32)


def product_tn(left, right):
    return lax.dot_general(left, right, (((0,), (0,)), ((), ())), preferred_element_type=jnp.float32)


def rms_factor(values):
    return lax.rsqrt(jnp.mean(values * values, axis=-1, keepdims=True) + EPSILON)


def norm_back(d_scaled, normed, factor, gain):
    inner = d_scaled * gain
    mean = jnp.mean(inner * normed, axis=-1, keepdims=True)
    return factor * (inner - normed * mean), jnp.sum(d_scaled * normed, axis=0)


def rotate(tensor, cosine, sine):
    half = tensor.shape[-1] // 2
    one, two = tensor[..., :half], tensor[..., half:]
    return jnp.concatenate([one * cosine - two * sine, two * cosine + one * sine], axis=-1)


def rotate_back(tensor, cosine, sine):
    return rotate(tensor, cosine, -sine)


def slot_places(order, half_len, slot_ids):
    matches = (slot_ids // half_len)[:, None] == jnp.arange(order.shape[0], dtype=jnp.int32)[None, :]
    return jnp.sum(jnp.where(matches, order[None, :], 0), axis=1) * half_len + slot_ids % half_len


def place():
    s, r = lax.axis_index("seq"), lax.axis_index("rows")
    return lax.div(s, 2), lax.rem(s, 2), r


def send(src, dst, ssem, rsem, device):
    return pltpu.make_async_remote_copy(
        src_ref=src, dst_ref=dst, send_sem=ssem, recv_sem=rsem, device_id=device, device_id_type=MESH
    )


def greet(devices):
    barrier = pltpu.get_barrier_semaphore()
    for device in devices:
        pl.semaphore_signal(barrier, inc=1, device_id=device, device_id_type=MESH)
    pl.semaphore_wait(barrier, len(devices))


def corners(r):
    return r, r + 1 - 2 * lax.rem(r, 2), lax.rem(r + 2, 4), 3 - r


def gather_kernel(zs, planes, z_flags, *refs):
    count = len(z_flags)
    own, out = refs[:count], refs[count : 2 * count]
    z_ssem, z_rsem, f_ssem, f_rsem, h_ssem, h_rsem, c_ssem, c_rsem, l_sem = refs[2 * count :]
    z, c, r = place()
    line = corners(r)
    s = z * 2 + c

    def at_z(other):
        return (other * 2 + c, r)

    twin = (z * 2 + 1 - c, r)
    shifts = range(1, zs) if any(z_flags) else ()
    partners = [twin] + ([(s, line[1]), (s, line[2])] if planes else [])
    partners += [at_z(lax.rem(z + k, zs)) for k in shifts]
    greet(partners)

    items = []
    for k in range(zs):
        for a in range(count):
            if k == 0 or z_flags[a]:
                items.append((a, k))
    pending = []

    def slot(a, k, core, row):
        zz = lax.rem(z - k + zs, zs) if z_flags[a] else 0
        return out[a].at[zz, core, row] if planes else out[a].at[zz, core]

    for i, (a, k) in enumerate(items):
        if k == 0:
            local = pltpu.make_async_copy(own[a], slot(a, 0, c, r), l_sem.at[a])
            local.start()
            pending.append(local.wait)
    for i, (a, k) in enumerate(items):
        if k:
            copy = send(own[a], out[a].at[(z, c, r) if planes else (z, c)], z_ssem.at[i], z_rsem.at[i], at_z(lax.rem(z + k, zs)))
            copy.start()
            pending.append(copy.wait_send)

    def to_twin(i, j, src, dst):
        copy = send(src, dst, c_ssem.at[i, j], c_rsem.at[i, j], twin)
        copy.start()
        pending.append(copy.wait_send)

    def begin(i):
        a, k = items[i]
        dst = slot(a, k, c, r)
        src = own[a]
        if k:
            send(dst, dst, z_ssem.at[i], z_rsem.at[i], at_z(lax.rem(z + k, zs))).wait_recv()
            src = dst
        if planes:
            for j in (1, 2):
                copy = send(src, dst, f_ssem.at[i, j - 1], f_rsem.at[i, j - 1], (s, line[j]))
                copy.start()
                pending.append(copy.wait_send)
        to_twin(i, 0, src, dst)

    def forward(i):
        a, k = items[i]
        half = own[a].shape[0] // 2
        for j in (1, 2):
            dst = slot(a, k, c, line[j])
            send(dst, dst, f_ssem.at[i, j - 1], f_rsem.at[i, j - 1], (s, line[j])).wait_recv()
            part = dst.at[pl.ds(half if j == 1 else 0, half)]
            copy = send(part, part, h_ssem.at[i, j - 1], h_rsem.at[i, j - 1], (s, line[3 - j]))
            copy.start()
            pending.append(copy.wait_send)
            to_twin(i, j, dst, dst)

    def finish(i):
        a, k = items[i]
        half = own[a].shape[0] // 2
        dst = slot(a, k, c, line[3])
        for j in (1, 2):
            part = dst.at[pl.ds(half if j == 1 else 0, half)]
            send(part, part, h_ssem.at[i, j - 1], h_rsem.at[i, j - 1], (s, line[3 - j])).wait_recv()
        to_twin(i, 3, dst, dst)

    total = len(items)
    for i in range(total + 2):
        if i < total:
            begin(i)
        if planes and 1 <= i <= total:
            forward(i - 1)
        if planes and i >= 2:
            finish(i - 2)
    for i, (a, k) in enumerate(items):
        for j in range(4 if planes else 1):
            dst = slot(a, k, 1 - c, line[j])
            send(dst, dst, c_ssem.at[i, j], c_rsem.at[i, j], twin).wait_recv()
    for wait in pending:
        wait()


def gather(arrays, z_flags, zs, collective_id, planes=True):
    n = sum(zs if f else 1 for f in z_flags)
    rows = (4,) if planes else ()
    sem = pltpu.SemaphoreType.DMA
    return pl.pallas_call(
        functools.partial(gather_kernel, zs, planes, tuple(z_flags)),
        out_shape=[
            jax.ShapeDtypeStruct((zs if f else 1, 2) + rows + a.shape, a.dtype) for a, f in zip(arrays, z_flags)
        ],
        in_specs=[pl.BlockSpec(memory_space=pl.ANY)] * len(arrays),
        out_specs=[pl.BlockSpec(memory_space=pl.ANY)] * len(arrays),
        scratch_shapes=[
            sem((n,)), sem((n,)), sem((n, 2)), sem((n, 2)), sem((n, 2)), sem((n, 2)), sem((n, 4)), sem((n, 4)),
            sem((len(arrays),)),
        ],
        compiler_params=pltpu.CompilerParams(collective_id=collective_id, has_side_effects=True),
    )(*arrays)


def exchange_kernel(own, out, ssem, rsem, l_sem):
    z, c, r = place()
    line = corners(r)
    others = [(cc, j) for j in (3, 1, 2, 0) for cc in range(2) if (cc, j) != (0, 0)]

    def core(flip):
        return 1 - c if flip else c

    devices = [(z * 2 + core(cc), line[j]) for cc, j in others]
    greet(devices)
    copies = []
    for i, (cc, j) in enumerate(others):
        copy = send(own.at[core(cc), line[j]], out.at[c, r], ssem.at[i], rsem.at[i], devices[i])
        copy.start()
        copies.append(copy)
    local = pltpu.make_async_copy(own.at[c, r], out.at[c, r], l_sem)
    local.start()
    for i, (cc, j) in enumerate(others):
        dst = out.at[core(cc), line[j]]
        send(dst, dst, ssem.at[i], rsem.at[i], devices[i]).wait_recv()
    for copy in copies:
        copy.wait_send()
    local.wait()


def exchange(blocks, collective_id):
    sem = pltpu.SemaphoreType.DMA
    return pl.pallas_call(
        exchange_kernel,
        out_shape=jax.ShapeDtypeStruct(blocks.shape, blocks.dtype),
        in_specs=[pl.BlockSpec(memory_space=pl.ANY)],
        out_specs=pl.BlockSpec(memory_space=pl.ANY),
        scratch_shapes=[sem((7,)), sem((7,)), sem],
        compiler_params=pltpu.CompilerParams(collective_id=collective_id, has_side_effects=True),
    )(blocks)


def scatter_kernel(zs, planes, given, out, own, twin_in, half_in, full_in, z_in, l_sem, c_ssem, c_rsem, h_ssem, h_rsem,
                   f_ssem, f_rsem, z_ssem, z_rsem):
    z, c, r = place()
    line = corners(r)
    s = z * 2 + c
    twin = (z * 2 + 1 - c, r)
    rows = out.shape[0]
    half = rows // 2
    step = 16
    spots = (3, 1, 2, 0) if planes else (0,)

    def at_z(other):
        return (other * 2 + c, r)

    partners = [twin] + ([(s, line[1]), (s, line[2])] if planes else [])
    partners += [at_z(lax.rem(z + k, zs)) for k in range(1, zs)]
    greet(partners)
    pending = []

    def block(k, core, row):
        zz = lax.rem(z + k, zs)
        return given.at[zz, core, row] if planes else given.at[zz, core]

    order = list(range(1, zs)) + [0]
    for k in order:
        for j in spots:
            copy = send(block(k, 1 - c, line[j]), twin_in.at[k, j], c_ssem.at[k, j], c_rsem.at[k, j], twin)
            copy.start()
            pending.append(copy.wait_send)
            pltpu.make_async_copy(block(k, c, line[j]), own.at[k, j], l_sem.at[k, j]).start()

    def settle(k, j):
        pltpu.make_async_copy(block(k, c, line[j]), own.at[k, j], l_sem.at[k, j]).wait()
        send(own.at[k, j], twin_in.at[k, j], c_ssem.at[k, j], c_rsem.at[k, j], twin).wait_recv()

    def add(first, last, k, j, *more):
        def body(n, carry):
            at = pl.ds(pl.multiple_of(first + n * step, step), step)
            value = own[k, j, at, :].astype(jnp.float32) + twin_in[k, j, at, :].astype(jnp.float32)
            for ref, offset in more:
                there = pl.ds(pl.multiple_of(first - offset + n * step, step), step)
                value = value + ref[there, :].astype(jnp.float32)
            own[k, j, at, :] = value.astype(own.dtype)
            return carry

        lax.fori_loop(0, (last - first) // step, body, 0)

    def start(copy):
        copy.start()
        pending.append(copy.wait_send)

    def stage_a(k):
        settle(k, 3)
        add(0, rows, k, 3)
        start(send(own.at[k, 3, pl.ds(half, half)], half_in.at[k, 1], h_ssem.at[k, 1], h_rsem.at[k, 1], (s, line[2])))
        start(send(own.at[k, 3, pl.ds(0, half)], half_in.at[k, 0], h_ssem.at[k, 0], h_rsem.at[k, 0], (s, line[1])))

    def stage_b(k):
        for j in (1, 2):
            settle(k, j)
            n = 1 if j == 1 else 0
            send(half_in.at[k, n], half_in.at[k, n], h_ssem.at[k, n], h_rsem.at[k, n], (s, line[2 - n])).wait_recv()
            if n:
                add(0, half, k, j)
                add(half, rows, k, j, (half_in.at[k, n], half))
            else:
                add(0, half, k, j, (half_in.at[k, n], 0))
                add(half, rows, k, j)
            start(send(own.at[k, j], full_in.at[k, j - 1], f_ssem.at[k, j - 1], f_rsem.at[k, j - 1], (s, line[j])))

    def stage_c(k):
        settle(k, 0)
        more = []
        if planes:
            for j in (1, 2):
                there = full_in.at[k, j - 1]
                send(there, there, f_ssem.at[k, j - 1], f_rsem.at[k, j - 1], (s, line[j])).wait_recv()
                more.append(there)
        if k:
            add(0, rows, k, 0, *[(ref, 0) for ref in more])
            start(send(own.at[k, 0], z_in.at[k], z_ssem.at[k], z_rsem.at[k], at_z(lax.rem(z + k, zs))))
            return
        for k2 in range(1, zs):
            there = z_in.at[k2]
            send(there, there, z_ssem.at[k2], z_rsem.at[k2], at_z(lax.rem(z + k2, zs))).wait_recv()
            more.append(there)

        def body(n, carry):
            at = pl.ds(pl.multiple_of(n * step, step), step)
            value = own[0, 0, at, :].astype(jnp.float32) + twin_in[0, 0, at, :].astype(jnp.float32)
            for ref in more:
                value = value + ref[at, :].astype(jnp.float32)
            out[at, :] = value
            return carry

        lax.fori_loop(0, rows // step, body, 0)

    total = len(order)
    for n in range(total + 2):
        if planes and n < total:
            stage_a(order[n])
        if planes and 1 <= n <= total:
            stage_b(order[n - 1])
        if n >= 2:
            stage_c(order[n - 2])
    for wait in pending:
        wait()


def scatter(blocks, zs, collective_id, planes=True):
    rows, columns = blocks.shape[-2:]
    spots = 4 if planes else 1
    low = blocks.dtype
    sem = pltpu.SemaphoreType.DMA
    size = rows * columns * 2
    used = size * (zs * (2 * spots + (3 if planes else 0) + 1) + 2)
    few = (zs, 2, 1 if planes else 1)
    return pl.pallas_call(
        functools.partial(scatter_kernel, zs, planes),
        out_shape=jax.ShapeDtypeStruct((rows, columns), jnp.float32),
        in_specs=[pl.BlockSpec(memory_space=pl.ANY)],
        out_specs=pl.BlockSpec(memory_space=pltpu.VMEM),
        scratch_shapes=[
            pltpu.VMEM((zs, spots, rows, columns), low),
            pltpu.VMEM((zs, spots, rows, columns), low),
            pltpu.VMEM((zs, 2, rows // 2, columns) if planes else (1, 2, 16, 128), low),
            pltpu.VMEM((zs, 2, rows, columns) if planes else (1, 2, 16, 128), low),
            pltpu.VMEM((zs, rows, columns) if zs > 1 else (1, 16, 128), low),
            sem((zs, 4)), sem((zs, 4)), sem((zs, 4)), sem((zs, 2)), sem((zs, 2)), sem((zs, 2)), sem((zs, 2)),
            sem((zs,)), sem((zs,)),
        ],
        compiler_params=pltpu.CompilerParams(
            collective_id=collective_id, has_side_effects=True, vmem_limit_bytes=used + 6 * MIB
        ),
    )(blocks)


class Links:
    def __init__(self, seq, rows):
        self.zs, self.rows = seq // 2, rows
        self.kernels = rows == 4 and self.zs == 4
        self.z_groups = [[2 * z + c for z in range(self.zs)] for c in range(2)]
        self.core_groups = [[2 * z, 2 * z + 1] for z in range(self.zs)]

    def gather_z(self, block):
        return lax.all_gather(block, "seq", axis=0, tiled=True, axis_index_groups=self.z_groups)

    def scatter_z(self, blocks):
        return lax.psum_scatter(blocks, "seq", scatter_dimension=0, tiled=True, axis_index_groups=self.z_groups)

    def exchange(self, blocks, collective_id):
        if self.kernels:
            return exchange(blocks, collective_id)
        moved = lax.all_to_all(blocks, "rows", split_axis=1, concat_axis=1, tiled=True)
        return lax.all_to_all(moved, "seq", split_axis=0, concat_axis=0, tiled=True, axis_index_groups=self.core_groups)

    def gather(self, arrays, z_flags, collective_id, planes=True):
        if self.kernels:
            return gather(arrays, z_flags, self.zs, collective_id, planes)
        results = []
        for array, flag in zip(arrays, z_flags):
            if planes:
                array = lax.all_gather(array, "rows", axis=0)
            array = lax.all_gather(array, "seq", axis=0, axis_index_groups=self.core_groups)[None]
            results.append(self.gather_z(array) if flag else array)
        return results

    def scatter(self, blocks, zs, collective_id, planes=True):
        if self.kernels:
            return scatter(blocks, zs, collective_id, planes)
        if zs > 1:
            blocks = self.scatter_z(blocks)
        blocks = lax.psum_scatter(
            blocks[0], "seq", scatter_dimension=0, tiled=True, axis_index_groups=self.core_groups
        )[0]
        if planes:
            blocks = lax.psum_scatter(blocks, "rows", scatter_dimension=0, tiled=True)[0]
        return blocks.astype(jnp.float32)


def on_device(seq, rows, tokens, w_query, w_key, w_value, w_out, w_gate, w_up, w_down, gain_attn, gain_ffn, lengths, order, cotangent):
    links = Links(seq, rows)
    zs = links.zs
    micro, _, span, _ = tokens.shape
    half_len = span // 2
    many = micro * span
    low = jnp.bfloat16
    scale = 1.0 / math.sqrt(HEAD_DIM)
    wide, part = w_gate.shape
    unit = w_down.shape[0]
    share = zs * unit

    both = jnp.stack([w_gate, w_up]).reshape(2, wide, zs, 2, rows, unit)
    both = jnp.transpose(both, (3, 4, 0, 1, 2, 5)).reshape(2, rows, 2, wide, share)
    both = links.exchange(both, 0)
    gate_w = links.gather_z(both[:, :, 0].reshape(2 * rows * wide, share))
    up_w = links.gather_z(both[:, :, 1].reshape(2 * rows * wide, share))
    down_w = links.gather_z(w_down)

    dy_own = cotangent.reshape(many, D)
    gains = jnp.pad(jnp.stack([gain_attn, gain_ffn], axis=1), ((0, 0), (0, 126)))
    pack = jnp.concatenate([w_query, w_key, w_value, w_out, gains], axis=1)
    packed, dy = links.gather([pack, dy_own], (True, False), 1)
    packed = packed.reshape(D, PACK)
    dy = dy.reshape(2 * rows * many, D)
    qkv_w, out_w = packed[:, :QKV], packed[:, QKV : QKV + D]
    gain_one = packed[:, QKV + D].astype(jnp.float32)
    gain_two = packed[:, QKV + D + 1].astype(jnp.float32)

    mine = slot_places(order, half_len, lax.axis_index("seq") * span + jnp.arange(span, dtype=jnp.int32))
    first = lengths[:, 0, 0]
    start = jnp.where(mine[None, :] >= first[:, None], first[:, None], 0)
    inverse = 10000.0 ** (-jnp.arange(HEAD_DIM // 2, dtype=jnp.float32) / (HEAD_DIM // 2))
    angles = (mine[None, :] - start).astype(jnp.float32)[..., None] * inverse
    cosine = jnp.cos(angles).reshape(many, 1, HEAD_DIM // 2)
    sine = jnp.sin(angles).reshape(many, 1, HEAD_DIM // 2)

    x = tokens.reshape(many, D).astype(jnp.float32)
    factor_one = rms_factor(x)
    attn_in = (x * factor_one * gain_one).astype(low)
    lin = product(attn_in, qkv_w)
    queries = rotate(lin[:, :D].reshape(many, HEADS, HEAD_DIM), cosine, sine).astype(low)
    queries = queries.reshape(micro, span, KV_HEADS, GROUP, HEAD_DIM)
    keys_own = rotate(lin[:, D : D + KVW].reshape(many, KV_HEADS, HEAD_DIM), cosine, sine).astype(low)
    kv_own = jnp.concatenate([keys_own.reshape(many, KVW), lin[:, D + KVW :].astype(low)], axis=1)
    (kv,) = links.gather([kv_own], (True,), 2, planes=False)
    count = seq * span
    kv = jnp.transpose(kv.reshape(seq, micro, span, 2 * KVW), (1, 0, 2, 3)).reshape(micro, count, 2, KV_HEADS, HEAD_DIM)
    keys, values = kv[:, :, 0], kv[:, :, 1]
    key_place = slot_places(order, half_len, jnp.arange(count, dtype=jnp.int32))
    allowed = (key_place[None, None, :] <= mine[None, :, None]) & (key_place[None, None, :] >= start[:, :, None])
    allowed = allowed[:, None, None]
    scores = jnp.einsum("mtkgd,mskd->mkgts", queries, keys, preferred_element_type=jnp.float32) * scale
    scores = jnp.where(allowed, scores, NEG_LARGE)
    top = jnp.max(scores, axis=-1, keepdims=True)
    exps = jnp.exp(scores - top)
    total = jnp.sum(exps, axis=-1, keepdims=True)
    probs = exps / total
    probs_low = probs.astype(low)
    attn_float = jnp.einsum("mkgts,mskd->mtkgd", probs_low, values, preferred_element_type=jnp.float32)
    attended = attn_float.astype(low).reshape(many, D)
    middle = x + product(attended, out_w)
    factor_two = rms_factor(middle)
    normed_two = middle * factor_two
    ffn_own = (normed_two * gain_two).astype(low)

    (ffn_in,) = links.gather([ffn_own], (False,), 3)
    ffn_in = ffn_in.reshape(2 * rows * many, D)
    gate = product(ffn_in, gate_w)
    upper = product(ffn_in, up_w)
    sig = jax.nn.sigmoid(gate)
    hidden = (gate * sig * upper).astype(low)
    d_hidden = product_nt(dy, down_w)
    d_gate = (d_hidden * upper * (sig * (1.0 + gate * (1.0 - sig)))).astype(low)
    d_upper = (d_hidden * gate * sig).astype(low)
    d_ffn_part = (product_nt(d_gate, gate_w) + product_nt(d_upper, up_w)).astype(low)
    result_part = product(hidden, down_w).astype(low)
    grad_down = product_tn(hidden, dy).astype(low)
    grad_gate = product_tn(ffn_in, d_gate).astype(low)
    grad_up = product_tn(ffn_in, d_upper).astype(low)

    d_ffn_in = links.scatter(d_ffn_part.reshape(1, 2, rows, many, D), 1, 4)
    result = (middle + links.scatter(result_part.reshape(1, 2, rows, many, D), 1, 4)).astype(low)
    grad_down = links.scatter_z(grad_down).astype(jnp.float32)
    grad_gate = links.scatter_z(grad_gate)
    grad_up = links.scatter_z(grad_up)
    grads = jnp.stack([grad_gate.reshape(2, rows, wide, share), grad_up.reshape(2, rows, wide, share)], axis=2)
    grads = links.exchange(grads, 0).reshape(2, rows, 2, wide, zs, unit)
    grads = jnp.transpose(grads, (2, 3, 4, 0, 1, 5)).reshape(2, wide, part).astype(jnp.float32)

    d_part, grad_gain_two = norm_back(d_ffn_in, normed_two, factor_two, gain_two)
    d_middle = dy_own.astype(jnp.float32) + d_part
    d_mid_low = d_middle.astype(low)
    grad_out = product_tn(attended, d_mid_low)
    d_heads = product_nt(d_mid_low, out_w).astype(low).reshape(micro, span, KV_HEADS, GROUP, HEAD_DIM)
    d_probs = jnp.einsum("mtkgd,mskd->mkgts", d_heads, values, preferred_element_type=jnp.float32)
    delta = jnp.sum(probs * d_probs, axis=-1, keepdims=True)
    d_scores = (probs * (d_probs - delta)).astype(low)
    d_query = jnp.einsum("mkgts,mskd->mtkgd", d_scores, keys, preferred_element_type=jnp.float32) * scale
    d_keys = jnp.einsum("mkgts,mtkgd->mskd", d_scores, queries, preferred_element_type=jnp.float32) * scale
    d_values = jnp.einsum("mkgts,mtkgd->mskd", probs_low, d_heads, preferred_element_type=jnp.float32)
    d_kv = jnp.concatenate([d_keys.reshape(micro, count, KVW), d_values.reshape(micro, count, KVW)], axis=-1).astype(low)
    d_kv = jnp.transpose(d_kv.reshape(micro, zs, 2, span, 2 * KVW), (1, 2, 0, 3, 4)).reshape(zs, 2, many, 2 * KVW)
    d_kv = links.scatter(d_kv, zs, 5, planes=False)
    d_lin = jnp.concatenate(
        [
            rotate_back(d_query.reshape(many, HEADS, HEAD_DIM), cosine, sine).reshape(many, D),
            rotate_back(d_kv[:, :KVW].reshape(many, KV_HEADS, HEAD_DIM), cosine, sine).reshape(many, KVW),
            d_kv[:, KVW:],
        ],
        axis=1,
    ).astype(low)
    grad_qkv = product_tn(attn_in, d_lin)
    d_attn_in = product_nt(d_lin, qkv_w)
    d_x, grad_gain_one = norm_back(d_attn_in, x * factor_one, factor_one, gain_one)
    x_grad = (d_middle + d_x).astype(low)
    gains_grad = jnp.pad(jnp.stack([grad_gain_one, grad_gain_two], axis=1), ((0, 0), (0, 126)))
    pack_grad = jnp.concatenate([grad_qkv, grad_out, gains_grad], axis=1).astype(low)
    pack_grad = links.scatter(pack_grad.reshape(zs, 2, rows, wide, PACK), zs, 6)

    return (
        result.reshape(tokens.shape),
        x_grad.reshape(tokens.shape),
        pack_grad[:, :D],
        pack_grad[:, D : D + KVW],
        pack_grad[:, D + KVW : QKV],
        pack_grad[:, QKV : QKV + D],
        grads[0],
        grads[1],
        grad_down,
        pack_grad[:, QKV + D],
        pack_grad[:, QKV + D + 1],
    )


def solution(mesh):
    both = ("seq", "rows")
    row = P(None, "rows", "seq", None)
    weight, gain = P(both, None), P(both)
    return jax.shard_map(
        functools.partial(on_device, mesh.shape["seq"], mesh.shape["rows"]),
        mesh=mesh,
        in_specs=(row,) + (weight,) * 7 + (gain, gain, P(None, "rows", None), P(), row),
        out_specs=(row, row) + (weight,) * 7 + (gain, gain),
        check_vma=False,
    )
```

time: 4900 us -> 884 us (0.18)
  waiting for transfers between devices: 4220 us -> 1.49 us
  Pallas kernels: 0 us -> 500 us
  matrix products: 438 us -> 222 us
  blocking collectives: 148 us -> 0 us
    reduce_scatter x7 -> x3, waiting for transfers between devices: 3650 us -> 0.02 us  [scatter_z(): lax.psum_scatter(blocks, 'seq', scatter_dimension=0, tiled=True, axis_ind...]
    pallas_call x0 -> x9, Pallas kernels: none -> 500 us  [the longest x3 250 us: gather(): pl.pallas_call(functools.partial(gather_kernel, zs, planes, tuple(z_flags...]
    all_gather x7 -> x3, waiting for transfers between devices: 500 us -> 0.02 us  [gather_z(): lax.all_gather(block, 'seq', axis=0, tiled=True, axis_index_groups=self.z...]
    dot_general x42 -> x5, matrix products: 374 us -> 43.7 us  [product(): return jnp.dot(left, right, preferred_element_type=jnp.float32)]
    dot_general x12 -> x15, matrix products: 64.1 us -> 160 us  [the longest x5 52 us: product_nt(): lax.dot_general(left, right, (((1,), (1,)), ((), ())), preferred_element_...]
    unnamed x2 -> x0, blocking collectives: 83.8 us -> none
    unnamed x22 -> x6, waiting for transfers between devices: 67.8 us -> 1.44 us
    all_gather x4 -> x0, blocking collectives: 64.5 us -> none  [the longest x2 33.9 us: one_row(): lax.all_gather(keys_own, 'seq', axis=0, tiled=True)]
  transfers between devices with their start and end apart: 18 -> 6, of which waited for: 15 -> 0; matrix products, arithmetic and copies ran while one was open for 7% -> 34% of each run, Pallas kernels for 0% -> 55%
where the time goes in v1:
time: 884 us; the launch traced here: 874 us
  Pallas kernels  500 us (57%)
  matrix products  222 us (25%)
  local copies, waits for them, and re-layouts  79.2 us (9%)
  other arithmetic  55.6 us (6%)
  between operations  15.5 us (2%)
    pallas_call x3, Pallas kernels, gather(): pl.pallas_call(functools.partial(gather_kernel, zs, planes, tuple(z_flags...  250 us
    pallas_call x4, Pallas kernels, scatter(): pl.pallas_call(functools.partial(scatter_kernel, zs, planes), out_shape=j...  208 us
    dot_general x5, matrix products, product_nt(): lax.dot_general(left, right, (((1,), (1,)), ((), ())), preferred_element_...  52 us
    dot_general x5, matrix products, product(): return jnp.dot(left, right, preferred_element_type=jnp.float32)  43.7 us
    pallas_call x2, Pallas kernels, exchange(): pl.pallas_call(exchange_kernel, out_shape=jax.ShapeDtypeStruct(blocks.sha...  41.9 us
    dot_general x5, matrix products, product_tn(): lax.dot_general(left, right, (((0,), (0,)), ((), ())), preferred_element_...  39.5 us
    convert_element_type x1, other arithmetic, on_device(): d_scores = (probs * (d_probs - delta)).astype(low)  28.2 us
    dot_general x1, matrix products, on_device(): jnp.einsum('mtkgd,mskd->mkgts', d_heads, values, preferred_element_type=j...  21.7 us
  transfers between devices with their start and end apart: 6, of which 0 were waited for; matrix products, arithmetic and copies ran while one was open for 34% of the time, Pallas kernels for 55%

profile of v1, /device:TPU:8, one launch (start us, length us, event | category | flops | bytes accessed | tf_op | source)
XLA Modules:
  0.0 874.0 jit_solution(11946060347401492683)
XLA Ops:
  7.2 4.4 stack.36
  18.9 21.2 %shard_map.215 = bf16[2,4,2,64,704]{4,3,2,1,0:T(8,128)(2,1)} custom-call(bf16[2,4,2,64,704]{4,3,2,1,0:T(8,128)(2,1)} %reshape.453.own), custom_call_target="tpu_custom_call" | custom-call | tf_op jit(solution)/shard_map/pallas_call | solution.py:226
  46.5 138.2 %shard_map.212 = (bf16[4,2,4,64,4736]{4,3,2,1,0:T(8,128)(2,1)}, bf16[1,2,4,256,2048]{4,3,2,1,0:T(8,128)(2,1)}) custom-call(bf16[64,4736]{1,0:T(8,128)(2,1)} %copy-done.16, bf16[256,2048]{1,0:T(8,128)(2,1)} %bitcast.206), custom_call_target="tpu_custom_call" | custom-call | tf_op jit(solution)/shard_map/pallas_call | solution.py:184
  186.8 6.0 fusion.10
  202.8 71.0 %shard_map.213 = bf16[4,2,256,512]{3,2,1,0:T(8,128)(2,1)} custom-call(bf16[256,512]{1,0:T(8,128)(2,1)} %pad_maximum_fusion.7.refs_0_), custom_call_target="tpu_custom_call" | custom-call | tf_op jit(solution)/shard_map/pallas_call | solution.py:184
  280.8 17.6 %fusion.67 = (f32[2,4,8,128]{3,2,1,0:T(8,128)S(1)}, f32[2,4,8,128,1024]{3,4,2,1,0:T(8,128)}) fusion(pred[2,128,1024]{1,2,0:T(8,128)(4,1)S(1)} %compare_and_fusion, bf16[2,128,4,8,64]{1,4,3,2,0:T(8,128)(2,1)S(1)} %copy_dynamic-update-slice_fusion, bf16[2,1024,2,4,64]{1,4,3,2,0:T(8,128)(2,1)} %reshape.449), kind=kOutput, calls=%fused_computation.146 | convolution fusion | flops 1107297280 | bytes 35946496 | tf_op jit(solution)/shard_map/sub | solution.py:471
  298.4 12.9 %fusion.34 = bf16[2,128,4,8,64]{1,4,3,2,0:T(8,128)(2,1)S(1)} fusion(bf16[2,1024,2,4,64]{1,4,3,2,0:T(8,128)(2,1)S(1)} %copy-done.7, f32[2,4,8,128,1024]{3,4,2,1,0:T(8,128)} %get-tuple-element.92, f32[2,4,8,128]{3,2,1,0:T(8,128)S(1)} %get-tuple-element.91), kind=kOutput, calls=%fused_computation.60 | convolution fusion | flops 1091043328 | bytes 35684352 | tf_op jit(solution)/shard_map/mkgts,mskd->mtkgd/dot_general | solution.py:475
  312.4 6.0 multiply_reduce_fusion.4
  323.0 41.3 %shard_map.214 = bf16[1,2,4,256,2048]{4,3,2,1,0:T(8,128)(2,1)} custom-call(bf16[256,2048]{1,0:T(8,128)(2,1)} %multiply_convert_fusion.3.refs_0_), custom_call_target="tpu_custom_call" | custom-call | tf_op jit(solution)/shard_map/pallas_call | solution.py:184
  364.3 11.1 %fusion.69 = f32[2048,704]{0,1:T(8,128)} fusion(bf16[2048,2048]{1,0:T(8,128)(2,1)} %bitcast.199, bf16[2048,704]{1,0:T(8,128)(2,1)} %all-gather.6.cloned.1.call-done), kind=kOutput, calls=%fused_computation.148 | convolution fusion | flops 5905580032 | bytes 17039360 | tf_op jit(solution)/shard_map/dot_general | solution.py:27
  375.4 11.1 %fusion.68 = f32[2048,704]{0,1:T(8,128)} fusion(bf16[2048,2048]{1,0:T(8,128)(2,1)} %bitcast.200, bf16[2048,704]{1,0:T(8,128)(2,1)} %all-gather.4.cloned.1.call-done), kind=kOutput, calls=%fused_computation.147 | convolution fusion | flops 5905580032 | bytes 17039360 | tf_op jit(solution)/shard_map/dot_general | solution.py:27
  386.5 15.7 %multiply_convert_fusion = (bf16[2048,704]{0,1:T(8,128)(2,1)S(1)}, bf16[2048,704]{0,1:T(8,128)(2,1)}, bf16[2048,704]{0,1:T(8,128)(2,1)}) fusion(f32[2048,704]{0,1:T(8,128)} %fusion.68, f32[2048,704]{0,1:T(8,128)} %fusion.69, bf16[2048,2048]{1,0:T(8,128)(2,1)} %bitcast.236, bf16[704,2048]{1,0:T(8,128)(2,1)} %all-gather.8.cloned.1.call-done), kind=kOutput, calls=%fused_computation.29 | convolution fusion | flops 5928648704 | bytes 31457280 | tf_op jit(solution)/shard_map/dot_general | solution.py:31
  403.9 10.9 %convolution_convert_fusion.3 = bf16[2048,704]{0,1:T(8,128)(2,1)} fusion(bf16[2048,704]{0,1:T(8,128)(2,1)S(1)} %get-tuple-element.67, bf16[2048,2048]{1,0:T(8,128)(2,1)} %bitcast.201), kind=kOutput, calls=%fused_computation.35 | convolution fusion | flops 5907021824 | bytes 14155776 | tf_op jit(solution)/shard_map/dot_general | solution.py:35
  414.8 10.6 %convolution_convert_fusion.4 = bf16[2048,704]{0,1:T(8,128)(2,1)} fusion(bf16[2048,704]{0,1:T(8,128)(2,1)} %get-tuple-element.68, bf16[2048,2048]{1,0:T(8,128)(2,1)} %bitcast.202), kind=kOutput, calls=%fused_computation.36 | convolution fusion | flops 5907021824 | bytes 14155776 | tf_op jit(solution)/shard_map/dot_general | solution.py:35
  425.5 9.5 %convolution_convert_fusion.1 = bf16[2048,2048]{1,0:T(8,128)(2,1)S(1)} fusion(bf16[2048,704]{0,1:T(8,128)(2,1)} %get-tuple-element.69, bf16[704,2048]{1,0:T(8,128)(2,1)} %all-gather.8.cloned.1.call-done), kind=kOutput, calls=%fused_computation.24 | convolution fusion | flops 5909774336 | bytes 14155776 | tf_op jit(solution)/shard_map/dot_general | solution.py:27
  435.0 43.4 %shard_map.216 = f32[256,2048]{1,0:T(8,128)S(1)} custom-call(bf16[1,2,4,256,2048]{4,3,2,1,0:T(8,128)(2,1)S(1)} %bitcast.195), custom_call_target="tpu_custom_call" | custom-call | tf_op jit(solution)/shard_map/pallas_call | solution.py:353
  478.3 10.3 %fusion.70 = f32[2048,2048]{1,0:T(8,128)} fusion(bf16[2048,704]{0,1:T(8,128)(2,1)S(1)} %copy-done.40, bf16[2048,704]{1,0:T(8,128)(2,1)S(1)} %copy-done.35), kind=kOutput, calls=%fused_computation.149 | convolution fusion | flops 5905580032 | bytes 22544384 | tf_op jit(solution)/shard_map/dot_general | solution.py:31
  488.6 11.8 %add_convert_fusion = bf16[2048,2048]{1,0:T(8,128)(2,1)S(1)} fusion(f32[2048,2048]{1,0:T(8,128)} %fusion.70, bf16[2048,704]{0,1:T(8,128)(2,1)} %copy-done.39, bf16[2048,704]{1,0:T(8,128)(2,1)} %all-gather.6.cloned.1.call-done), kind=kOutput, calls=%fused_computation.10 | convolution fusion | flops 5913968640 | bytes 30932992 | tf_op jit(solution)/shard_map/dot_general | solution.py:31
  500.4 43.2 %shard_map.217 = f32[256,2048]{1,0:T(8,128)S(1)} custom-call(bf16[1,2,4,256,2048]{4,3,2,1,0:T(8,128)(2,1)S(1)} %bitcast.194), custom_call_target="tpu_custom_call" | custom-call | tf_op jit(solution)/shard_map/pallas_call | solution.py:353
  548.0 5.8 fusion.25
  558.3 21.7 %fusion.1 = (f32[2,4,8,128]{3,2,1,0:T(8,128)S(1)}, f32[2,4,1024,128,8]{3,2,4,1,0:T(8,128)}) fusion(f32[2,4,8,128,1024]{3,4,2,1,0:T(8,128)} %get-tuple-element.92, f32[2,4,8,128]{3,2,1,0:T(8,128)S(1)} %copy-done.27, bf16[2,128,4,8,64]{1,4,3,2,0:T(8,128)(2,1)S(1)} %copy.130, bf16[2,1024,2,4,64]{1,4,3,2,0:T(8,128)(2,1)} %reshape.449), kind=kOutput, calls=%fused_computation.3 | convolution fusion | flops 1098899456 | bytes 69271552 | tf_op jit(solution)/shard_map/mtkgd,mskd->mkgts/dot_general | solution.py:511
  580.1 28.2 %fusion.3 = bf16[2,4,8,128,1024]{3,4,2,1,0:T(8,128)(2,1)} fusion(f32[2,4,1024,128,8]{3,2,4,1,0:T(8,128)} %get-tuple-element.96, f32[2,4,8,128]{3,2,1,0:T(8,128)S(1)} %get-tuple-element.95, f32[2,4,8,128,1024]{3,4,2,1,0:T(8,128)} %get-tuple-element.92, f32[2,4,8,128]{3,2,1,0:T(8,128)S(1)} %copy-done.27), kind=kLoop, calls=%fused_computation.5 | loop fusion | flops 33554432 | bytes 83951616 | tf_op jit(solution)/shard_map/convert_element_type | solution.py:513
  608.3 14.4 %fusion.37 = bf16[2,1024,4,64]{1,3,2,0:T(8,128)(2,1)} fusion(bf16[2,128,4,8,64]{1,4,3,2,0:T(8,128)(2,1)S(1)} %copy.130, f32[2,4,8,128,1024]{3,4,2,1,0:T(8,128)} %get-tuple-element.92, f32[2,4,8,128]{3,2,1,0:T(8,128)S(1)} %copy-done.27), kind=kOutput, calls=%fused_computation.61 | convolution fusion | flops 1091043328 | bytes 35684352 | tf_op jit(solution)/shard_map/mkgts,mtkgd->mskd/dot_general | solution.py:516
  626.1 11.0 %fusion.40 = bf16[2,1024,4,64]{1,3,2,0:T(8,128)(2,1)S(1)} fusion(bf16[2,128,4,8,64]{1,4,3,2,0:T(8,128)(2,1)S(1)} %copy-done.10, bf16[2,4,8,128,1024]{3,4,2,1,0:T(8,128)(2,1)} %fusion.3), kind=kOutput, calls=%fused_computation.62 | convolution fusion | flops 1074790400 | bytes 18874368 | tf_op jit(solution)/shard_map/mkgts,mtkgd->mskd/dot_general | solution.py:515
  639.5 27.3 %shard_map.218 = f32[256,512]{1,0:T(8,128)S(1)} custom-call(bf16[4,2,256,512]{3,2,1,0:T(8,128)(2,1)S(1)} %bitcast.196), custom_call_target="tpu_custom_call" | custom-call | tf_op jit(solution)/shard_map/pallas_call | solution.py:353
  666.8 8.9 %multiply_bitcast_fusion = f32[2,128,4,8,64]{1,4,3,2,0:T(8,128)S(1)} fusion(bf16[2,4,8,128,1024]{3,4,2,1,0:T(8,128)(2,1)} %fusion.3, bf16[2,1024,2,4,64]{1,4,3,2,0:T(8,128)(2,1)S(1)} %copy-done.8), kind=kOutput, calls=%fused_computation.50 | convolution fusion | flops 1074266112 | bytes 19922944 | tf_op jit(solution)/shard_map/mkgts,mskd->mtkgd/dot_general | solution.py:514
  683.3 10.6 %convolution_convert_fusion.5 = bf16[704,2048]{1,0:T(8,128)(2,1)} fusion(bf16[2048,704]{0,1:T(8,128)(2,1)} %get-tuple-element.69, bf16[2048,2048]{1,0:T(8,128)(2,1)} %bitcast.237), kind=kOutput, calls=%fused_computation.37 | convolution fusion | flops 5907021824 | bytes 14155776 | tf_op jit(solution)/shard_map/dot_general | solution.py:35
  695.1 8.3 multiply_reduce_fusion.1
  712.2 7.4 pad_maximum_fusion.given
  719.7 94.2 %shard_map.219 = f32[64,4736]{1,0:T(8,128)S(1)} custom-call(bf16[4,2,4,64,4736]{4,3,2,1,0:T(8,128)(2,1)} %pad_maximum_fusion.given), custom_call_target="tpu_custom_call" | custom-call | tf_op jit(solution)/shard_map/pallas_call | solution.py:353
  822.1 20.7 %shard_map.220 = bf16[2,4,2,64,704]{4,3,2,1,0:T(8,128)(2,1)} custom-call(bf16[2,4,2,64,704]{4,3,2,1,0:T(8,128)(2,1)} %pad_maximum_fusion.2.own), custom_call_target="tpu_custom_call" | custom-call | tf_op jit(solution)/shard_map/pallas_call | solution.py:226
  842.8 5.9 reshape.468
  (197 shorter events, 98.0 us)
Async XLA Ops:
  7.2 4.9 copy-start.19
  7.2 357.1 %all-gather.6.cloned.1.call-start = ((), (), s32[]{:S(2)}) async-start(), calls=%async_computation.4 | async-start | bytes 3932160 | tf_op jit(solution)/shard_map/all_gather | solution.py:381
  40.2 5.0 copy-start.3
  40.2 5.2 copy-start.37
  40.2 5.2 copy-start.38
  40.2 5.4 copy-start.22
  40.2 5.4 copy-start.28
  40.2 5.4 copy-start.29
  40.2 5.4 copy-start.23
  43.0 332.4 %all-gather.4.cloned.1.call-start = ((), (), s32[]{:S(2)}) async-start(), calls=%async_computation.3 | async-start | bytes 3932160 | tf_op jit(solution)/shard_map/all_gather | solution.py:381
  43.8 342.7 %all-gather.8.cloned.1.call-start = ((), (), s32[]{:S(2)}) async-start(), calls=%async_computation.5 | async-start | bytes 3604480 | tf_op jit(solution)/shard_map/all_gather | solution.py:381
  44.5 773.5 %reduce-scatter.6.cloned.1.call-start = ((), (), s32[]{:S(2)}) async-start(), calls=%async_computation.7 | async-start | bytes 3604480 | tf_op jit(solution)/shard_map/reduce_scatter | solution.py:384
  45.4 141.1 %copy-start.31 = (f32[256]{0:T(256)}, f32[256]{0:T(256)S(1)}, u32[]{:S(2)}) copy-start(f32[256]{0:T(256)S(1)} %rsqrt_bitcast_fusion) | copy-start | bytes 3076
  186.5 6.3 copy-start.24
  186.8 6.0 copy-start.13
  280.8 17.6 %copy-start.9 = (bf16[2,128,4,8,64]{1,4,3,2,0:T(8,128)(2,1)}, bf16[2,128,4,8,64]{1,4,3,2,0:T(8,128)(2,1)S(1)}, u32[]{:S(2)}) copy-start(bf16[2,128,4,8,64]{1,4,3,2,0:T(8,128)(2,1)S(1)} %copy_dynamic-update-slice_fusion) | copy-start | bytes 3145732
  280.8 17.6 %copy-start.7 = (bf16[2,1024,2,4,64]{1,4,3,2,0:T(8,128)(2,1)S(1)}, bf16[2,1024,2,4,64]{1,4,3,2,0:T(8,128)(2,1)}, u32[]{:S(2)}) copy-start(bf16[2,1024,2,4,64]{1,4,3,2,0:T(8,128)(2,1)} %reshape.449) | copy-start | bytes 6291460
  298.4 12.9 %copy-start.26 = (f32[2,4,8,128]{3,2,1,0:T(8,128)}, f32[2,4,8,128]{3,2,1,0:T(8,128)S(1)}, u32[]{:S(2)}) copy-start(f32[2,4,8,128]{3,2,1,0:T(8,128)S(1)} %get-tuple-element.91) | copy-start | bytes 98308
  298.4 14.0 %copy-start.4 = (bf16[2,1,128,2048]{3,2,1,0:T(8,128)(2,1)S(1)}, bf16[2,1,128,2048]{3,2,1,0:T(8,128)(2,1)}, u32[]{:S(2)}) copy-start(bf16[2,1,128,2048]{3,2,1,0:T(8,128)(2,1)} %param.13) | copy-start | bytes 3145732
  425.4 394.0 %reduce-scatter.4.cloned.1.call-start = ((), (), s32[]{:S(2)}) async-start(), calls=%async_computation.6 | async-start | bytes 3604480 | tf_op jit(solution)/shard_map/reduce_scatter | solution.py:384
  434.9 43.4 %copy-start.35 = (bf16[2048,704]{1,0:T(8,128)(2,1)S(1)}, bf16[2048,704]{1,0:T(8,128)(2,1)}, u32[]{:S(2)}) copy-start(bf16[2048,704]{1,0:T(8,128)(2,1)} %all-gather.4.cloned.1.call-done) | copy-start | bytes 8650756
  434.9 43.4 %copy-start.40 = (bf16[2048,704]{0,1:T(8,128)(2,1)S(1)}, bf16[2048,704]{0,1:T(8,128)(2,1)}, u32[]{:S(2)}) copy-start(bf16[2048,704]{0,1:T(8,128)(2,1)} %get-tuple-element.68) | copy-start | bytes 8650756
  553.9 4.4 copy-start.27
  580.0 284.4 %reduce-scatter.8.cloned.1.call-start = ((), (), s32[]{:S(2)}) async-start(), calls=%async_computation.8 | async-start | bytes 3604480 | tf_op jit(solution)/shard_map/reduce_scatter | solution.py:384
  622.7 3.4 copy-start.10
  639.3 27.5 %copy-start.8 = (bf16[2,1024,2,4,64]{1,4,3,2,0:T(8,128)(2,1)S(1)}, bf16[2,1024,2,4,64]{1,4,3,2,0:T(8,128)(2,1)}, u32[]{:S(2)}) copy-start(bf16[2,1024,2,4,64]{1,4,3,2,0:T(8,128)(2,1)} %reshape.449) | copy-start | bytes 6291460
  666.8 9.0 %copy-start = (f32[256,512]{1,0:T(8,128)}, f32[256,512]{1,0:T(8,128)S(1)}, u32[]{:S(2)}) copy-start(f32[256,512]{1,0:T(8,128)S(1)} %shard_map.218) | copy-start | bytes 1572868
  695.1 8.3 copy-start.30
  695.1 9.6 %copy-start.12 = (bf16[2048,256]{1,0:T(8,128)(2,1)S(1)}, bf16[2048,256]{1,0:T(8,128)(2,1)}, u32[]{:S(2)}) copy-start(bf16[2048,256]{1,0:T(8,128)(2,1)} %copy.141) | copy-start | bytes 3145732
  707.9 4.3 copy-start.14
  719.7 96.7 %copy-start.6 = (bf16[2,1,128,2048]{3,2,1,0:T(8,128)(2,1)S(1)}, bf16[2,1,128,2048]{3,2,1,0:T(8,128)(2,1)}, u32[]{:S(2)}) copy-start(bf16[2,1,128,2048]{3,2,1,0:T(8,128)(2,1)} %param.13) | copy-start | bytes 3145732
  719.7 96.7 %copy-start.15 = (f32[256,2048]{1,0:T(8,128)S(1)}, f32[256,2048]{1,0:T(8,128)}, u32[]{:S(2)}) copy-start(f32[256,2048]{1,0:T(8,128)} %get-tuple-element.97) | copy-start | bytes 6291460
  (16 other events, 26.5 us)
Sparse Core Ops, SparseCore 0:
  43.2 108.9 all-gather.5
  153.8 62.4 all-gather.3
  217.8 72.7 all-gather.7
  425.5 53.7 reduce-scatter.5
  580.1 53.6 reduce-scatter.3
  694.0 54.8 reduce-scatter.7

commit v2 on v1

v2 whole, which is shorter than its diff:
```python
import functools

import jax
import jax.numpy as jnp
from jax import lax
from jax.experimental import pallas as pl
from jax.experimental.pallas import tpu as pltpu
from jax.sharding import PartitionSpec as P

D = 2048
HEADS = 32
KV_HEADS = 4
HEAD_DIM = 64
GROUP = 8
KVW = 256
QKV = D + 2 * KVW
PACK = QKV + 128

EPSILON = 1e-05
NEG_LARGE = -1e30
MESH = pl.DeviceIdType.MESH
MIB = 1 << 20
LONG = pl.CostEstimate(flops=50_000_000_000, bytes_accessed=150 * MIB, transcendentals=0)


def product(left, right):
    return jnp.dot(left, right, preferred_element_type=jnp.float32)


def product_nt(left, right):
    return lax.dot_general(left, right, (((1,), (1,)), ((), ())), preferred_element_type=jnp.float32)


def product_tn(left, right):
    return lax.dot_general(left, right, (((0,), (0,)), ((), ())), preferred_element_type=jnp.float32)


def rms_factor(values):
    return lax.rsqrt(jnp.mean(values * values, axis=-1, keepdims=True) + EPSILON)


def norm_back(d_scaled, normed, factor, gain):
    inner = d_scaled * gain
    mean = jnp.mean(inner * normed, axis=-1, keepdims=True)
    return factor * (inner - normed * mean), jnp.sum(d_scaled * normed, axis=0)


def slot_places(order, half_len, slot_ids):
    matches = (slot_ids // half_len)[:, None] == jnp.arange(order.shape[0], dtype=jnp.int32)[None, :]
    return jnp.sum(jnp.where(matches, order[None, :], 0), axis=1) * half_len + slot_ids % half_len


def place():
    s, r = lax.axis_index("seq"), lax.axis_index("rows")
    return lax.div(s, 2), lax.rem(s, 2), r


def send(src, dst, ssem, rsem, device):
    return pltpu.make_async_remote_copy(
        src_ref=src, dst_ref=dst, send_sem=ssem, recv_sem=rsem, device_id=device, device_id_type=MESH
    )


def greet(devices):
    barrier = pltpu.get_barrier_semaphore()
    for device in devices:
        pl.semaphore_signal(barrier, inc=1, device_id=device, device_id_type=MESH)
    pl.semaphore_wait(barrier, len(devices))


def corners(r):
    return r, r + 1 - 2 * lax.rem(r, 2), lax.rem(r + 2, 4), 3 - r


def exchange_others():
    return [(cc, j) for j in (3, 1, 2, 0) for cc in range(2) if (cc, j) != (0, 0)]


class Exchange:
    def __init__(self, own, out, ssem, rsem, l_sem):
        z, c, r = place()
        line = corners(r)
        self.own, self.out, self.ssem, self.rsem, self.here = own, out, ssem, rsem, (c, r)
        self.others = [(1 - c if cc else c, line[j]) for cc, j in exchange_others()]
        self.devices = [(z * 2 + core, row) for core, row in self.others]
        self.local = pltpu.make_async_copy(own.at[c, r], out.at[c, r], l_sem)

    def start(self):
        self.copies = []
        for i, other in enumerate(self.others):
            copy = send(self.own.at[other], self.out.at[self.here], self.ssem.at[i], self.rsem.at[i], self.devices[i])
            copy.start()
            self.copies.append(copy)
        self.local.start()

    def finish(self):
        for i, other in enumerate(self.others):
            dst = self.out.at[other]
            send(dst, dst, self.ssem.at[i], self.rsem.at[i], self.devices[i]).wait_recv()
        for copy in self.copies:
            copy.wait_send()
        self.local.wait()


class Line:
    def __init__(self, zs, way, lo, hi, src, dst, sems):
        z, c, r = place()
        lo, hi = (lo, min(hi, zs - 1)) if way == 1 else (max(lo, 1), hi)
        self.sends = (z >= lo) & (z < hi)
        self.gets = (z - way >= lo) & (z - way < hi)
        to = lax.rem(z + way + zs, zs)
        self.copy = send(src, dst, sems.at[0], sems.at[1], (to * 2 + c, r))

    def start(self):
        pl.when(self.sends)(self.copy.start)

    def finish(self):
        pl.when(self.sends)(self.copy.wait_send)
        pl.when(self.gets)(self.copy.wait_recv)


LINE_SEMS = pltpu.SemaphoreType.DMA((2,))
EXCHANGE_SEMS = [pltpu.SemaphoreType.DMA((7,)), pltpu.SemaphoreType.DMA((7,)), pltpu.SemaphoreType.DMA]


def neighbours(zs, planes, moved):
    z, c, r = place()
    line = corners(r)
    s = z * 2 + c
    devices = [(z * 2 + 1 - c, r)]
    if moved:
        devices = [(z * 2 + (1 - c if cc else c), line[j]) for cc, j in exchange_others()]
    elif planes:
        devices += [(s, line[1]), (s, line[2])]
    return devices + [(lax.rem(z + k, zs) * 2 + c, r) for k in range(1, zs)]


def gather_kernel(zs, flags, moves, lines, *refs):
    count = len(flags)
    carried = sum(not source for source, *_ in lines)
    taken = count + moves + carried
    own, line_own = refs[:count], refs[count + moves : taken]
    out, line_out = refs[taken : taken + count], refs[taken + count + moves : taken + count + moves + len(lines)]
    moved = [(refs[count + n], refs[taken + count + n]) for n in range(moves)]
    sems = refs[taken + count + moves + len(lines) :]
    z_ssem, z_rsem, f_ssem, f_rsem, h_ssem, h_rsem, c_ssem, c_rsem, l_sem = sems[:9]
    z, c, r = place()
    line = corners(r)
    s = z * 2 + c
    reach = zs if lines or any(flag[0] for flag in flags) else 1

    def at_z(other):
        return (other * 2 + c, r)

    twin = (z * 2 + 1 - c, r)
    greet(neighbours(reach, any(flag[1] for flag in flags), moves))
    exchanges = [Exchange(*pair, *sems[9 + 3 * n : 12 + 3 * n]) for n, pair in enumerate(moved)]
    waiting = list(line_own)
    going = [
        Line(zs, *way, moved[source - 1][1] if source else waiting.pop(0), dst, sems[9 + 3 * moves + n])
        for n, ((source, *way), dst) in enumerate(zip(lines, line_out))
    ]

    items = [(a, k) for k in range(zs) for a in range(count) if k == 0 or flags[a][0]]
    pending = []

    def slot(a, k, other, j):
        z_flag, planes = flags[a]
        if not z_flag:
            return out[a].at[other, j]
        core = 1 - c if other else c
        zz = lax.rem(z - k + zs, zs)
        return out[a].at[zz, core, line[j]] if planes else out[a].at[zz, core]

    def arrival(a, k, other, j):
        z_flag, planes = flags[a]
        if not z_flag:
            return out[a].at[other, j]
        zz = lax.rem(z - k + zs, zs)
        return out[a].at[zz, c, r] if planes else out[a].at[zz, c]

    for a in range(count):
        local = pltpu.make_async_copy(own[a], slot(a, 0, 0, 0), l_sem.at[a])
        local.start()
        pending.append(local.wait)
    for exchange_one in exchanges:
        exchange_one.start()
    for i, (a, k) in enumerate(items):
        if k:
            copy = send(own[a], arrival(a, 0, 0, 0), z_ssem.at[i], z_rsem.at[i], at_z(lax.rem(z + k, zs)))
            copy.start()
            pending.append(copy.wait_send)

    def to_twin(i, j, src):
        a, k = items[i]
        dst = slot(a, k, 0, j) if flags[a][0] else out[a].at[1, j]
        copy = send(src, dst, c_ssem.at[i, j], c_rsem.at[i, j], twin)
        copy.start()
        pending.append(copy.wait_send)

    def begin(i):
        a, k = items[i]
        src = own[a]
        if k:
            src = slot(a, k, 0, 0)
            send(src, src, z_ssem.at[i], z_rsem.at[i], at_z(lax.rem(z + k, zs))).wait_recv()
        if flags[a][1]:
            for j in (1, 2):
                copy = send(src, arrival(a, k, 0, j), f_ssem.at[i, j - 1], f_rsem.at[i, j - 1], (s, line[j]))
                copy.start()
                pending.append(copy.wait_send)
        to_twin(i, 0, src)

    def halves(a, ref, j):
        half = own[a].shape[0] // 2
        return ref.at[pl.ds(half if j == 1 else 0, half)]

    def forward(i):
        a, k = items[i]
        for j in (1, 2):
            src = slot(a, k, 0, j)
            send(src, src, f_ssem.at[i, j - 1], f_rsem.at[i, j - 1], (s, line[j])).wait_recv()
            there = slot(a, k, 0, j) if flags[a][0] else out[a].at[0, 3]
            copy = send(
                halves(a, src, j), halves(a, there, j), h_ssem.at[i, j - 1], h_rsem.at[i, j - 1], (s, line[3 - j])
            )
            copy.start()
            pending.append(copy.wait_send)
            to_twin(i, j, src)

    def finish(i):
        a, k = items[i]
        src = slot(a, k, 0, 3)
        for j in (1, 2):
            part = halves(a, src, j)
            send(part, part, h_ssem.at[i, j - 1], h_rsem.at[i, j - 1], (s, line[3 - j])).wait_recv()
        to_twin(i, 3, src)

    total = len(items)
    for i in range(total + 2):
        if i < total:
            begin(i)
        if i == total - 1:
            for exchange_one in exchanges:
                exchange_one.finish()
            for one in going:
                one.start()
        if 1 <= i <= total and flags[items[i - 1][0]][1]:
            forward(i - 1)
        if i >= 2 and flags[items[i - 2][0]][1]:
            finish(i - 2)
    for i, (a, k) in enumerate(items):
        for j in range(4 if flags[a][1] else 1):
            dst = slot(a, k, 1, j)
            send(dst, dst, c_ssem.at[i, j], c_rsem.at[i, j], twin).wait_recv()
    for one in going:
        one.finish()
    for wait in pending:
        wait()


def gather(arrays, flags, zs, collective_id, moved=(), lines=()):
    carried = [line[0] for line in lines if not isinstance(line[0], int)]
    plan = tuple((line[0] if isinstance(line[0], int) else 0,) + tuple(line[1:]) for line in lines)
    line_shapes = [moved[line[0] - 1] if isinstance(line[0], int) else line[0] for line in lines]
    n = sum(zs if z_flag else 1 for z_flag, _ in flags)
    sem = pltpu.SemaphoreType.DMA
    anywhere = pl.BlockSpec(memory_space=pl.ANY)
    shapes = [
        jax.ShapeDtypeStruct(((zs,) if z_flag else ()) + (2,) + ((4,) if planes else ()) + a.shape, a.dtype)
        for a, (z_flag, planes) in zip(arrays, flags)
    ] + [jax.ShapeDtypeStruct(m.shape, m.dtype) for m in (*moved, *line_shapes)]
    return pl.pallas_call(
        functools.partial(gather_kernel, zs, tuple(flags), len(moved), plan),
        out_shape=shapes,
        in_specs=[anywhere] * (len(arrays) + len(moved) + len(carried)),
        out_specs=[anywhere] * len(shapes),
        scratch_shapes=[
            sem((n,)), sem((n,)), sem((n, 2)), sem((n, 2)), sem((n, 2)), sem((n, 2)), sem((n, 4)), sem((n, 4)),
            sem((len(arrays),)),
        ] + EXCHANGE_SEMS * len(moved) + [LINE_SEMS] * len(lines),
        compiler_params=pltpu.CompilerParams(collective_id=collective_id, has_side_effects=True),
        cost_estimate=LONG,
    )(*arrays, *moved, *carried)


class Scatter:
    def __init__(self, zs, z_flag, planes, given, out, own, twin_in, half_in, full_in, z_in, l_sem, c_ssem, c_rsem, h_ssem, h_rsem,
                 f_ssem, f_rsem, z_ssem, z_rsem):
        self.__dict__.update(locals())
        self.z, self.c, self.r = place()
        self.line = corners(self.r)
        self.s = self.z * 2 + self.c
        self.twin = (self.z * 2 + 1 - self.c, self.r)
        self.rows = out.shape[0]
        self.step = 16
        self.spots = (3, 1, 2, 0) if planes else (0,)
        self.zs = zs if z_flag else 1
        self.order = list(range(1, self.zs)) + [0]
        self.pending = []

    def at_z(self, k):
        return (lax.rem(self.z + k, self.zs) * 2 + self.c, self.r)

    def block(self, k, other, j):
        if not self.z_flag:
            return self.given.at[other, j]
        zz, core = lax.rem(self.z + k, self.zs), 1 - self.c if other else self.c
        return self.given.at[zz, core, self.line[j]] if self.planes else self.given.at[zz, core]

    def start(self, copy):
        copy.start()
        self.pending.append(copy.wait_send)

    def local(self, k, j):
        return pltpu.make_async_copy(self.block(k, 0, j), self.own.at[k, j], self.l_sem.at[k, j])

    def begin(self):
        for k in self.order:
            for j in self.spots:
                block = self.block(k, 1, j)
                self.start(send(block, self.twin_in.at[k, j], self.c_ssem.at[k, j], self.c_rsem.at[k, j], self.twin))
                self.local(k, j).start()

    def settle(self, k, j):
        self.local(k, j).wait()
        send(self.own.at[k, j], self.twin_in.at[k, j], self.c_ssem.at[k, j], self.c_rsem.at[k, j], self.twin).wait_recv()

    def add(self, first, last, k, j, *more, final=False):
        step = self.step

        def body(n, carry):
            at = pl.ds(pl.multiple_of(first + n * step, step), step)
            value = self.own[k, j, at, :].astype(jnp.float32) + self.twin_in[k, j, at, :].astype(jnp.float32)
            for ref, offset in more:
                there = pl.ds(pl.multiple_of(first - offset + n * step, step), step)
                value = value + ref[there, :].astype(jnp.float32)
            if final:
                self.out[at, :] = value
            else:
                self.own[k, j, at, :] = value.astype(self.own.dtype)
            return carry

        lax.fori_loop(0, (last - first) // step, body, 0)

    def half_copy(self, k, n, src):
        dst = self.half_in.at[k, n]
        return send(dst if src is None else src, dst, self.h_ssem.at[k, n], self.h_rsem.at[k, n], (self.s, self.line[n + 1]))

    def full_copy(self, k, j, src):
        dst = self.full_in.at[k, j - 1]
        return send(dst if src is None else src, dst, self.f_ssem.at[k, j - 1], self.f_rsem.at[k, j - 1], (self.s, self.line[j]))

    def z_copy(self, k, src):
        dst = self.z_in.at[k]
        return send(dst if src is None else src, dst, self.z_ssem.at[k], self.z_rsem.at[k], self.at_z(k))

    def stage_a(self, k):
        half = self.rows // 2
        self.settle(k, 3)
        self.add(0, self.rows, k, 3)
        self.start(self.half_copy(k, 1, self.own.at[k, 3, pl.ds(half, half)]))
        self.start(self.half_copy(k, 0, self.own.at[k, 3, pl.ds(0, half)]))

    def stage_b(self, k):
        half = self.rows // 2
        for j in (1, 2):
            self.settle(k, j)
            n = 2 - j
            self.half_copy(k, n, None).wait_recv()
            more = (self.half_in.at[k, n], half if n else 0)
            self.add(0, half, k, j, *([] if n else [more]))
            self.add(half, self.rows, k, j, *([more] if n else []))
            self.start(self.full_copy(k, j, self.own.at[k, j]))

    def stage_c(self, k):
        self.settle(k, 0)
        more = []
        if self.planes:
            for j in (1, 2):
                self.full_copy(k, j, None).wait_recv()
                more.append((self.full_in.at[k, j - 1], 0))
        if k:
            self.add(0, self.rows, k, 0, *more)
            self.start(self.z_copy(k, self.own.at[k, 0]))
            return
        for k2 in range(1, self.zs):
            self.z_copy(k2, None).wait_recv()
            more.append((self.z_in.at[k2], 0))
        self.add(0, self.rows, 0, 0, *more, final=True)

    def end(self):
        for wait in self.pending:
            wait()


SCATTER_REFS = 14


def scatter_kernel(zs, flags, moves, lines, *refs):
    count, taken = len(flags), len(flags) + moves + len(lines)
    given, moved, line_own = refs[:count], refs[count : count + moves], refs[count + moves : taken]
    out, rest = refs[taken : taken + count], refs[taken + count :]
    moved_out, line_out, rest = rest[:moves], rest[moves : moves + len(lines)], rest[moves + len(lines) :]
    reach = zs if lines or any(flag[0] for flag in flags) else 1
    greet(neighbours(reach, any(flag[1] for flag in flags), moves))
    sums = [
        Scatter(zs, *flags[a], given[a], out[a], *rest[SCATTER_REFS * a : SCATTER_REFS * (a + 1)]) for a in range(count)
    ]
    rest = rest[SCATTER_REFS * count :]
    exchanges = [Exchange(moved[n], moved_out[n], *rest[3 * n : 3 * n + 3]) for n in range(moves)]
    rest = rest[3 * moves :]
    going = [Line(zs, *line, line_own[n], line_out[n], rest[n]) for n, line in enumerate(lines)]
    for one in sums:
        one.begin()
    for one in exchanges:
        one.start()
    for one in going:
        one.start()
    for one in sums:
        if not one.planes:
            for k in one.order[:-1]:
                one.stage_c(k)
    items = [(one, k) for k in list(range(1, zs)) + [0] for one in sums if one.planes and k < one.zs]
    total = len(items)
    for n in range(total + 2):
        for back, stage in enumerate((Scatter.stage_a, Scatter.stage_b, Scatter.stage_c)):
            if 0 <= n - back < total and (back < 2 or items[n - back][1]):
                stage(*items[n - back])
    for one in sums:
        one.stage_c(0)
    for one in exchanges + going:
        one.finish()
    for one in sums:
        one.end()


def scatter(arrays, flags, zs, collective_id, moved=(), lines=()):
    sem = pltpu.SemaphoreType.DMA
    anywhere = pl.BlockSpec(memory_space=pl.ANY)
    scratch, used, shapes = [], 0, []
    all_zs = zs
    for array, (z_flag, planes) in zip(arrays, flags):
        rows, columns = array.shape[-2:]
        zs = all_zs if z_flag else 1
        spots, low = 4 if planes else 1, array.dtype
        used += rows * columns * 2 * (zs * (2 * spots + (3 if planes else 0) + 1) + 4)
        shapes.append(jax.ShapeDtypeStruct((rows, columns), jnp.float32))
        scratch += [
            pltpu.VMEM((zs, spots, rows, columns), low),
            pltpu.VMEM((zs, spots, rows, columns), low),
            pltpu.VMEM((zs, 2, rows // 2, columns) if planes else (1, 2, 16, 128), low),
            pltpu.VMEM((zs, 2, rows, columns) if planes else (1, 2, 16, 128), low),
            pltpu.VMEM((zs, rows, columns) if zs > 1 else (1, 16, 128), low),
            sem((zs, 4)), sem((zs, 4)), sem((zs, 4)), sem((zs, 2)), sem((zs, 2)), sem((zs, 2)), sem((zs, 2)),
            sem((zs,)), sem((zs,)),
        ]
    count = len(arrays)
    return pl.pallas_call(
        functools.partial(scatter_kernel, all_zs, tuple(flags), len(moved), tuple(tuple(line[1:]) for line in lines)),
        out_shape=shapes + [jax.ShapeDtypeStruct(m.shape, m.dtype) for m in (*moved, *[line[0] for line in lines])],
        in_specs=[anywhere] * (count + len(moved) + len(lines)),
        out_specs=[pl.BlockSpec(memory_space=pltpu.VMEM)] * count + [anywhere] * (len(moved) + len(lines)),
        scratch_shapes=scratch + EXCHANGE_SEMS * len(moved) + [LINE_SEMS] * len(lines),
        compiler_params=pltpu.CompilerParams(
            collective_id=collective_id, has_side_effects=True, vmem_limit_bytes=used + 6 * MIB
        ),
        cost_estimate=LONG,
    )(*arrays, *moved, *[line[0] for line in lines])


def partner(tensor):
    lanes = tensor.shape[-1]
    half = HEAD_DIM // 2
    lane = lax.broadcasted_iota(jnp.int32, tensor.shape, tensor.ndim - 1)
    ahead = pltpu.roll(tensor, lanes - half, tensor.ndim - 1)
    behind = pltpu.roll(tensor, half, tensor.ndim - 1)
    return jnp.where(lax.rem(lane, HEAD_DIM) < half, ahead, behind)


def stack_heads(block, first):
    return jnp.concatenate(
        [block[:, (first + h) * HEAD_DIM : (first + h + 1) * HEAD_DIM] for h in range(GROUP)], axis=0
    )


def unstack_heads(stacked, span):
    return jnp.concatenate([stacked[h * span : (h + 1) * span] for h in range(GROUP)], axis=1)


def load_window(inverse_ref, kv_ref, window, first_block):
    half_len = kv_ref.shape[1] // 2
    for n in range(window.shape[0] // half_len):
        slot = inverse_ref[first_block + n]
        at = pl.ds(pl.multiple_of(lax.rem(slot, 2) * half_len, half_len), half_len)
        window[n * half_len : (n + 1) * half_len, :] = kv_ref[lax.div(slot, 2), at, :]


def window_of(order_ref, first_ref, count, half_len):
    m, half = pl.program_id(0), pl.program_id(1)
    my_block = order_ref[lax.axis_index("seq") * 2 + half]
    half_blocks = count // half_len // 2
    first_block = jnp.where(my_block >= half_blocks, half_blocks, 0)
    return first_block, my_block * half_len, first_ref[m]


def attend_kernel(order_ref, inverse_ref, first_ref, lin_ref, cos_ref, sin_ref, kv_ref, q_ref, out_ref, window, bias):
    span = lin_ref.shape[0]
    wide = window.shape[0]
    first_block, my_place, first = window_of(order_ref, first_ref, 2 * wide, span)
    load_window(inverse_ref, kv_ref, window, first_block)
    key_place = first_block * span + lax.broadcasted_iota(jnp.int32, (span, wide), 1)
    place_here = my_place + lax.broadcasted_iota(jnp.int32, (span, wide), 0)
    start = jnp.where(place_here >= first, first, 0)
    bias[...] = jnp.where((key_place <= place_here) & (key_place >= start), 0.0, NEG_LARGE)
    cosine, sine = cos_ref[...], sin_ref[...]
    width = GROUP * HEAD_DIM
    for g in range(KV_HEADS):
        at = slice(g * width, (g + 1) * width)
        lin = lin_ref[:, at]
        query = (lin * cosine + partner(lin) * sine).astype(jnp.bfloat16) * jnp.bfloat16(HEAD_DIM ** -0.5)
        q_ref[:, at] = query
        key = window[:, g * HEAD_DIM : (g + 1) * HEAD_DIM]
        value = window[:, KVW + g * HEAD_DIM : KVW + (g + 1) * HEAD_DIM]
        scores = product_nt(stack_heads(query, 0), key).reshape(GROUP, span, wide) + bias[...][None]
        exps = jnp.exp(scores - jnp.max(scores, axis=-1, keepdims=True))
        total = jnp.sum(exps, axis=-1, keepdims=True).reshape(GROUP * span, 1)
        mixed = product(exps.astype(jnp.bfloat16).reshape(GROUP * span, wide), value) / total
        out_ref[:, at] = unstack_heads(mixed, span).astype(jnp.bfloat16)


def attend_back_kernel(order_ref, inverse_ref, first_ref, q_ref, d_ref, cos_ref, sin_ref, kv_ref, dq_ref, dkv_ref, window, bias, sums):
    span = q_ref.shape[0]
    wide = window.shape[0]
    rows = GROUP * span
    half = pl.program_id(1)
    first_block, my_place, first = window_of(order_ref, first_ref, 2 * wide, span)
    load_window(inverse_ref, kv_ref, window, first_block)
    key_place = first_block * span + lax.broadcasted_iota(jnp.int32, (wide, rows), 0)
    place_here = my_place + lax.rem(lax.broadcasted_iota(jnp.int32, (wide, rows), 1), span)
    start = jnp.where(place_here >= first, first, 0)
    bias[...] = jnp.where((key_place <= place_here) & (key_place >= start), 0.0, NEG_LARGE)

    @pl.when(half == 0)
    def _():
        sums[...] = jnp.zeros_like(sums)

    cosine, sine = cos_ref[...], sin_ref[...]
    width = GROUP * HEAD_DIM
    d_keys, d_values = [], []
    for g in range(KV_HEADS):
        at = slice(g * width, (g + 1) * width)
        key = window[:, g * HEAD_DIM : (g + 1) * HEAD_DIM]
        value = window[:, KVW + g * HEAD_DIM : KVW + (g + 1) * HEAD_DIM]
        query = stack_heads(q_ref[:, at], 0)
        d_mixed = stack_heads(d_ref[:, at], 0)
        scores = product_nt(key, query) + bias[...]
        exps = jnp.exp(scores - jnp.max(scores, axis=0, keepdims=True))
        probs = exps * (1.0 / jnp.sum(exps, axis=0, keepdims=True))
        d_probs = product_nt(value, d_mixed)
        weighted = probs * d_probs
        delta = jnp.sum(weighted, axis=0, keepdims=True)
        d_scores = (weighted - probs * delta).astype(jnp.bfloat16)
        d_keys.append(product(d_scores, query))
        d_values.append(product(probs.astype(jnp.bfloat16), d_mixed))
        d_query = unstack_heads(product_tn(d_scores, key) * HEAD_DIM ** -0.5, span)
        dq_ref[:, at] = (d_query * cosine - partner(d_query) * sine).astype(jnp.bfloat16)
    d_window = jnp.concatenate(d_keys + d_values, axis=1)
    for n in range(wide // span):
        slot = inverse_ref[first_block + n]
        to = pl.ds(pl.multiple_of(lax.rem(slot, 2) * span, span), span)
        sums[lax.div(slot, 2), to, :] += d_window[n * span : (n + 1) * span]

    @pl.when(half == 1)
    def _():
        dkv_ref[...] = sums[...].astype(jnp.bfloat16)


def attention_specs(seq, micro, span):
    half_len = span // 2

    def rows(width):
        return pl.BlockSpec((half_len, width), lambda m, h, *_: (m * 2 + h, 0))

    whole = pl.BlockSpec((seq, span, 2 * KVW), lambda m, h, *_: (0, m, 0))
    return half_len, rows, whole


def attend(order, inverse, first, lin, cosine, sine, kv):
    seq, many, _ = kv.shape
    micro = first.shape[0]
    span = many // micro
    half_len, rows, whole = attention_specs(seq, micro, span)
    wide = seq * span // 2
    return pl.pallas_call(
        attend_kernel,
        grid_spec=pltpu.PrefetchScalarGridSpec(
            num_scalar_prefetch=3,
            grid=(micro, 2),
            in_specs=[rows(D), rows(GROUP * HEAD_DIM), rows(GROUP * HEAD_DIM), whole],
            out_specs=[rows(D), rows(D)],
            scratch_shapes=[pltpu.VMEM((wide, 2 * KVW), jnp.bfloat16), pltpu.VMEM((half_len, wide), jnp.float32)],
        ),
        out_shape=[jax.ShapeDtypeStruct((many, D), jnp.bfloat16)] * 2,
        compiler_params=pltpu.CompilerParams(vmem_limit_bytes=48 * MIB),
        cost_estimate=pl.CostEstimate(flops=8 * many * wide * D, bytes_accessed=16 * MIB, transcendentals=many * wide * HEADS),
    )(order, inverse, first, lin, cosine, sine, kv)


def attend_back(order, inverse, first, queries, d_heads, cosine, sine, kv):
    seq, many, _ = kv.shape
    micro = first.shape[0]
    span = many // micro
    half_len, rows, whole = attention_specs(seq, micro, span)
    wide = seq * span // 2
    return pl.pallas_call(
        attend_back_kernel,
        grid_spec=pltpu.PrefetchScalarGridSpec(
            num_scalar_prefetch=3,
            grid=(micro, 2),
            in_specs=[rows(D), rows(D), rows(GROUP * HEAD_DIM), rows(GROUP * HEAD_DIM), whole],
            out_specs=[rows(D), whole],
            scratch_shapes=[
                pltpu.VMEM((wide, 2 * KVW), jnp.bfloat16),
                pltpu.VMEM((wide, GROUP * half_len), jnp.float32),
                pltpu.VMEM((seq, span, 2 * KVW), jnp.float32),
            ],
        ),
        out_shape=[jax.ShapeDtypeStruct((many, D), jnp.bfloat16), jax.ShapeDtypeStruct(kv.shape, jnp.bfloat16)],
        compiler_params=pltpu.CompilerParams(vmem_limit_bytes=56 * MIB),
        cost_estimate=pl.CostEstimate(flops=20 * many * wide * D, bytes_accessed=24 * MIB, transcendentals=many * wide * HEADS),
    )(order, inverse, first, queries, d_heads, cosine, sine, kv)


def assemble(zs, pieces, whole, sem):
    if len(pieces) == 1:
        copy = pltpu.make_async_copy(pieces[0], whole, sem.at[0])
        copy.start()
        return [copy]
    z = lax.div(lax.axis_index("seq"), 2)
    size = whole.shape[0] // zs

    def rows(zz):
        return whole.at[pl.ds(pl.multiple_of(zz * size, size), size)]

    copies = [pltpu.make_async_copy(pieces[0], rows(z), sem.at[0])]
    copies[0].start()
    for k in range(1, zs):
        below = pltpu.make_async_copy(pieces[k], rows(lax.rem(z - k + zs, zs)), sem.at[k])
        above = pltpu.make_async_copy(pieces[2 * zs - 1 - k], rows(lax.rem(z - k + zs, zs)), sem.at[k])
        pl.when(z >= k)(below.start)
        pl.when(z < k)(above.start)
        copies.append(below)
    return copies


def ffn_kernel(zs, count, *refs):
    x_ref, dy_ref = refs[:2]
    both_pieces, down_pieces = refs[2 : 2 + count], refs[2 + count : 2 + 2 * count]
    out_ref, dx_ref, g_both_ref, g_down_ref, both_w, down_w, both_sum, down_sum, sem = refs[2 + 2 * count :]
    n = down_w.shape[0]
    step, last = pl.program_id(0), pl.num_programs(0) - 1

    @pl.when(step == 0)
    def _():
        copies = assemble(zs, both_pieces, both_w, sem.at[0]) + assemble(zs, down_pieces, down_w, sem.at[1])
        both_sum[...] = jnp.zeros_like(both_sum)
        down_sum[...] = jnp.zeros_like(down_sum)
        for copy in copies:
            copy.wait()

    x, dy = x_ref[...], dy_ref[...]
    lin = product(x, both_w[...])
    gate, upper = lin[:, :n], lin[:, n:]
    sig = 1.0 / (1.0 + jnp.exp(-gate))
    act = gate * sig
    hidden = (act * upper).astype(jnp.bfloat16)
    d_hidden = product_nt(dy, down_w[...])
    d_gate = d_hidden * upper * (sig * (1.0 + gate * (1.0 - sig)))
    d_both = jnp.concatenate([d_gate.astype(jnp.bfloat16), (d_hidden * act).astype(jnp.bfloat16)], axis=1)
    dx_ref[...] = product_nt(d_both, both_w[...]).astype(jnp.bfloat16)
    out_ref[...] = product(hidden, down_w[...]).astype(jnp.bfloat16)
    for at in range(0, D, 256):
        both_sum[at : at + 256, :] += product_tn(x[:, at : at + 256], d_both)
    part = n // 4
    for at in range(0, n, part):
        down_sum[at : at + part, :] += product_tn(hidden[:, at : at + part], dy)

    @pl.when(step == last)
    def _():
        both_w[...] = both_sum[...].astype(jnp.bfloat16)
        down_w[...] = down_sum[...].astype(jnp.bfloat16)
        copies = [
            pltpu.make_async_copy(both_w, g_both_ref, sem.at[0, 0]),
            pltpu.make_async_copy(down_w, g_down_ref, sem.at[1, 0]),
        ]
        for copy in copies:
            copy.start()
        for copy in copies:
            copy.wait()


def feed_forward(x, dy, both_pieces, down_pieces, zs):
    count = x.shape[0]
    spread_over = zs if len(both_pieces) > 1 else 1
    n = down_pieces[0].shape[0] * spread_over
    block = 256
    low = jnp.bfloat16
    tokens = pl.BlockSpec((block, D), lambda i: (i, 0))
    anywhere = pl.BlockSpec(memory_space=pl.ANY)
    return pl.pallas_call(
        functools.partial(ffn_kernel, zs, len(both_pieces)),
        grid=(count // block,),
        in_specs=[tokens, tokens] + [anywhere] * (2 * len(both_pieces)),
        out_specs=[tokens, tokens, anywhere, anywhere],
        out_shape=[jax.ShapeDtypeStruct(x.shape, low)] * 2
        + [jax.ShapeDtypeStruct((D, 2 * n), low), jax.ShapeDtypeStruct((n, D), low)],
        scratch_shapes=[
            pltpu.VMEM((D, 2 * n), low),
            pltpu.VMEM((n, D), low),
            pltpu.VMEM((D, 2 * n), jnp.float32),
            pltpu.VMEM((n, D), jnp.float32),
            pltpu.SemaphoreType.DMA((2, zs)),
        ],
        compiler_params=pltpu.CompilerParams(vmem_limit_bytes=60 * MIB),
        cost_estimate=pl.CostEstimate(flops=18 * count * D * n, bytes_accessed=60 * MIB, transcendentals=count * n),
    )(x, dy, *both_pieces, *down_pieces)


def spread_kernel(zs, rows, unit, gate_ref, up_ref, out):
    for c in range(2):
        for r in range(rows):
            for n, weight in enumerate((gate_ref, up_ref)):
                for z in range(zs):
                    at = ((z * 2 + c) * rows + r) * unit
                    to = (n * zs + z) * unit
                    out[c, r, :, to : to + unit] = weight[:, at : at + unit]


def spread(gate, up, zs, rows):
    wide, part = gate.shape
    unit = part // (zs * 2 * rows)
    return pl.pallas_call(
        functools.partial(spread_kernel, zs, rows, unit),
        out_shape=jax.ShapeDtypeStruct((2, rows, wide, 2 * zs * unit), gate.dtype),
    )(gate, up)


def collect_kernel(zs, rows, unit, given, *outs):
    for n, out in enumerate(outs):
        for c in range(2):
            for r in range(rows):
                for z in range(zs):
                    at = ((z * 2 + c) * rows + r) * unit
                    to = (n * zs + z) * unit
                    out[:, at : at + unit] = given[c, r, :, to : to + unit].astype(jnp.float32)


def collect(blocks, zs, rows, unit):
    shape = jax.ShapeDtypeStruct((blocks.shape[2], unit * zs * 2 * rows), jnp.float32)
    return pl.pallas_call(functools.partial(collect_kernel, zs, rows, unit), out_shape=[shape, shape])(blocks)


class Links:
    def __init__(self, seq, rows):
        self.zs, self.rows = seq // 2, rows
        self.kernels = rows == 4 and self.zs == 4
        self.z_groups = [[2 * z + c for z in range(self.zs)] for c in range(2)]
        self.core_groups = [[2 * z, 2 * z + 1] for z in range(self.zs)]

    def gather_z(self, block):
        return lax.all_gather(block, "seq", axis=0, tiled=True, axis_index_groups=self.z_groups)

    def scatter_z(self, blocks):
        return lax.psum_scatter(blocks, "seq", scatter_dimension=0, tiled=True, axis_index_groups=self.z_groups)

    def exchange_xla(self, blocks):
        moved = lax.all_to_all(blocks, "rows", split_axis=1, concat_axis=1, tiled=True)
        return lax.all_to_all(moved, "seq", split_axis=0, concat_axis=0, tiled=True, axis_index_groups=self.core_groups)

    def along(self, way, lo, hi):
        return [(2 * z + c, 2 * (z + way) + c) for z in range(lo, hi) for c in range(2) if 0 <= z + way < self.zs]

    def permute(self, lines):
        return [lax.ppermute(array, "seq", self.along(way, lo, hi)) for array, way, lo, hi in lines]

    def gather_lines(self, k, up, down):
        return [(up, 1, k - 1, self.zs), (down, -1, 0, self.zs - k + 1)]

    def part(self, blocks, to, held):
        z = lax.div(lax.axis_index("seq"), 2)
        found = lax.dynamic_index_in_dim(blocks, lax.rem(z + to + self.zs, self.zs), 0, keepdims=False)
        for other, there in held:
            found = found.astype(jnp.float32) + jnp.where(there, other.astype(jnp.float32), 0.0)
        return found

    def scatter_lines(self, k, blocks, held=None):
        up, down = self.held(held)
        low = blocks.dtype
        return [
            (self.part(blocks, -k, up).astype(low), 1, 0, k),
            (self.part(blocks, k, down).astype(low), -1, self.zs - k, self.zs),
        ]

    def scatter_end(self, blocks, held):
        up, down = self.held(held)
        return self.part(blocks, 0, up + down)

    def held(self, held):
        z = lax.div(lax.axis_index("seq"), 2)
        return ([(held[0], z > 0)], [(held[1], z < self.zs - 1)]) if held else ([], [])

    @staticmethod
    def tie(arrays, *others):
        if not others:
            return arrays
        return lax.optimization_barrier((*arrays, *others))[: len(arrays)]

    def gather(self, arrays, flags, collective_id, moved=(), lines=()):
        if self.kernels:
            return gather(arrays, flags, self.zs, collective_id, moved, lines)
        results = []
        for array, (z_flag, planes) in zip(arrays, flags):
            if planes:
                array = lax.all_gather(array, "rows", axis=0)
            array = lax.all_gather(array, "seq", axis=0, axis_index_groups=self.core_groups)
            results.append(self.gather_z(array[None]) if z_flag else array)
        return results + [self.exchange_xla(blocks) for blocks in moved] + [line[0] for line in lines]

    def scatter(self, arrays, flags, collective_id, moved=(), lines=()):
        if self.kernels:
            return scatter(arrays, flags, self.zs, collective_id, moved, lines)
        return (
            [
                self.scatter_one(self.scatter_z(blocks)[0] if z_flag else blocks, planes)
                for blocks, (z_flag, planes) in zip(arrays, flags)
            ]
            + [self.exchange_xla(blocks) for blocks in moved]
            + [line[0] for line in lines]
        )

    def scatter_one(self, blocks, planes):
        blocks = lax.psum_scatter(blocks, "seq", scatter_dimension=0, tiled=True, axis_index_groups=self.core_groups)[0]
        if planes:
            blocks = lax.psum_scatter(blocks, "rows", scatter_dimension=0, tiled=True)[0]
        return blocks.astype(jnp.float32)


def on_device(seq, rows, tokens, w_query, w_key, w_value, w_out, w_gate, w_up, w_down, gain_attn, gain_ffn, lengths, order, cotangent):
    links = Links(seq, rows)
    zs = links.zs
    micro, _, span, _ = tokens.shape
    half_len = span // 2
    many = micro * span
    low = jnp.bfloat16
    wide = w_gate.shape[0]
    unit = w_down.shape[0]

    chained = links.kernels
    both = spread(w_gate, w_up, zs, rows)
    gains = jnp.pad(jnp.stack([gain_attn, gain_ffn], axis=1), ((0, 0), (0, 126)))
    pack = jnp.concatenate([w_query, w_key, w_value, gains], axis=1)
    lines = [(1, 1, 0, zs), (1, -1, 0, zs)] if chained else []
    packed, both_own, *both_got = links.gather([pack], [(True, True)], 0, [both], lines)
    flat = (2 * rows * wide, 2 * zs * unit)
    both_own = both_own.reshape(flat)
    both_w, down_w = [both_own], [w_down]
    if chained:
        both_w += [None] * (2 * zs - 2)
        down_w += [None] * (2 * zs - 2)
        both_w[1], both_w[zs] = (b.reshape(flat) for b in both_got)
        down_w[1], down_w[zs] = links.permute(links.gather_lines(1, *links.tie([w_down, w_down], packed)))
    else:
        both_w, down_w = [links.gather_z(both_own)], [links.gather_z(w_down)]
    packed = packed.reshape(D, PACK)
    gain_one = packed[:, QKV].astype(jnp.float32)
    gain_two = packed[:, QKV + 1].astype(jnp.float32)
    dy_own = cotangent.reshape(many, D)

    mine = slot_places(order, half_len, lax.axis_index("seq") * span + jnp.arange(span, dtype=jnp.int32))
    first = lengths[:, 0, 0]
    start = jnp.where(mine[None, :] >= first[:, None], first[:, None], 0)
    inverse = 10000.0 ** (-jnp.arange(HEAD_DIM // 2, dtype=jnp.float32) / (HEAD_DIM // 2))
    angles = ((mine[None, :] - start).astype(jnp.float32)[..., None] * inverse).reshape(many, HEAD_DIM // 2)
    cosine, sine = jnp.cos(angles), jnp.sin(angles)
    cosine = jnp.tile(cosine, (1, 2 * GROUP))
    sine = jnp.tile(jnp.concatenate([-sine, sine], axis=1), (1, GROUP))
    slot_of = jnp.argmax(order[None, :] == jnp.arange(order.shape[0], dtype=jnp.int32)[:, None], axis=1).astype(jnp.int32)

    def turn(tensor, sign):
        swapped = jnp.flip(tensor.reshape(many, KV_HEADS, 2, HEAD_DIM // 2), axis=2).reshape(many, KVW)
        return tensor * cosine[:, :KVW] + sign * swapped * sine[:, :KVW]

    x = tokens.reshape(many, D).astype(jnp.float32)
    factor_one = rms_factor(x)
    attn_in = (x * factor_one * gain_one).astype(low)
    lin = product(attn_in, packed)
    kv_own = jnp.concatenate([turn(lin[:, D : D + KVW], 1.0), lin[:, D + KVW : QKV]], axis=1).astype(low)
    lines = []
    if chained:
        (kv_own,) = links.tie([kv_own], down_w[1], down_w[zs])
        lines = links.gather_lines(2, both_w[1], both_w[zs])
    kv, out_w, dy, *got = links.gather([kv_own, w_out, dy_own], [(True, False), (True, True), (False, True)], 1, (), lines)
    kv = kv.reshape(seq, many, 2 * KVW)
    out_w = out_w.reshape(D, D)
    dy = dy.reshape(2 * rows * many, D)
    if chained:
        both_w[2], both_w[zs + 1] = got
        down_w[2], down_w[zs + 1] = links.permute(links.gather_lines(2, *links.tie([down_w[1], down_w[zs]], kv)))
    queries, attended = attend(order, slot_of, first, lin, cosine, sine, kv)
    middle = x + product(attended, out_w)
    factor_two = rms_factor(middle)
    normed_two = middle * factor_two
    ffn_own = (normed_two * gain_two).astype(low)

    lines = []
    if chained:
        (ffn_own,) = links.tie([ffn_own], down_w[2], down_w[zs + 1])
        lines = links.gather_lines(3, both_w[2], both_w[zs + 1]) + links.gather_lines(3, down_w[2], down_w[zs + 1])
    ffn_in, *got = links.gather([ffn_own], [(False, True)], 2, (), lines)
    if chained:
        both_w[3], both_w[zs + 2], down_w[3], down_w[zs + 2] = got
    ffn_in = ffn_in.reshape(2 * rows * many, D)
    result_part, d_ffn_part, grad_both, grad_down = feed_forward(ffn_in, dy, both_w, down_w, zs)
    grad_both = grad_both.reshape(zs, *flat)
    grad_down = grad_down.reshape(zs, unit, D)
    lines = []
    if chained:
        lines = links.scatter_lines(1, grad_both) + links.scatter_lines(1, grad_down)
    d_ffn_in, *got = links.scatter([d_ffn_part.reshape(2, rows, many, D)], [(False, True)], 3, (), lines)
    if chained:
        lines = links.scatter_lines(2, grad_both, got[:2]) + links.scatter_lines(2, grad_down, got[2:])
        got = links.permute(lines)

    d_part, grad_gain_two = norm_back(d_ffn_in, normed_two, factor_two, gain_two)
    d_middle = dy_own.astype(jnp.float32) + d_part
    d_mid_low = d_middle.astype(low)
    grad_out = product_tn(attended, d_mid_low).astype(low)
    d_heads = product_nt(d_mid_low, out_w).astype(low)
    d_query, d_kv = attend_back(order, slot_of, first, queries, d_heads, cosine, sine, kv)
    shards = (zs, 2, rows, wide)
    lines = []
    if chained:
        d_query, d_kv, *got = lax.optimization_barrier((d_query, d_kv, *got))
        lines = links.scatter_lines(3, grad_both, got[:2])
        down_lines = links.scatter_lines(3, grad_down, got[2:])
    grad_query = product_tn(attn_in, d_query).astype(low)
    d_kv, grad_out, grad_query, result_sum, *got = links.scatter(
        [
            d_kv.reshape(zs, 2, many, 2 * KVW),
            grad_out.reshape(*shards, D),
            grad_query.reshape(*shards, D),
            result_part.reshape(2, rows, many, D),
        ],
        [(True, False), (True, True), (True, True), (False, True)],
        4,
        (),
        lines,
    )
    if chained:
        grad_both = links.scatter_end(grad_both, got).astype(low)
    else:
        grad_both, grad_down = links.scatter_z(grad_both)[0], links.scatter_z(grad_down)[0]
        down_lines = []
    result = (middle + result_sum).astype(low)
    d_key = turn(d_kv[:, :KVW], -1.0)
    d_kv = jnp.concatenate([d_key.astype(low), d_kv[:, KVW:].astype(low)], axis=1)
    d_attn_in = product_nt(d_query, packed[:, :D]) + product_nt(d_kv, packed[:, D:QKV])
    d_x, grad_gain_one = norm_back(d_attn_in, x * factor_one, factor_one, gain_one)
    x_grad = (d_middle + d_x).astype(low)
    gains_grad = jnp.pad(jnp.stack([grad_gain_one, grad_gain_two], axis=1), ((0, 0), (0, 126)))
    pack_grad = jnp.concatenate([product_tn(attn_in, d_kv), gains_grad], axis=1).astype(low)
    pack_grad, grad_both, *got = links.scatter(
        [pack_grad.reshape(*shards, 2 * KVW + 128)],
        [(True, True)],
        5,
        [grad_both.reshape(2, rows, wide, 2 * zs * unit)],
        down_lines,
    )
    if chained:
        grad_down = links.scatter_end(grad_down, got)
    grad_down = grad_down.astype(jnp.float32)
    grad_gate, grad_up = collect(grad_both, zs, rows, unit)

    return (
        result.reshape(tokens.shape),
        x_grad.reshape(tokens.shape),
        grad_query,
        pack_grad[:, :KVW],
        pack_grad[:, KVW : 2 * KVW],
        grad_out,
        grad_gate,
        grad_up,
        grad_down,
        pack_grad[:, 2 * KVW],
        pack_grad[:, 2 * KVW + 1],
    )


def solution(mesh):
    both = ("seq", "rows")
    row = P(None, "rows", "seq", None)
    weight, gain = P(both, None), P(both)
    return jax.shard_map(
        functools.partial(on_device, mesh.shape["seq"], mesh.shape["rows"]),
        mesh=mesh,
        in_specs=(row,) + (weight,) * 7 + (gain, gain, P(None, "rows", None), P(), row),
        out_specs=(row, row) + (weight,) * 7 + (gain, gain),
        check_vma=False,
    )
```

time: 884 us -> 690 us (0.78)
  matrix products: 222 us -> 40.9 us
  local copies, waits for them, and re-layouts: 79.2 us -> 27.1 us
  Pallas kernels: 500 us -> 537 us
  other arithmetic: 55.6 us -> 31.7 us
  starting transfers between devices: 0.24 us -> 22.1 us
  waiting for transfers between devices: 1.49 us -> 17.7 us
  between operations: 15.5 us -> 1.99 us
    dot_general x5 -> x0, matrix products: 68.8 us -> none  [the longest x1 21.7 us: on_device(): jnp.einsum('mtkgd,mskd->mkgts', d_heads, values, preferred_element_type=j...]
    dot_general x5 -> x3, matrix products: 52 us -> 14.1 us  [product_nt(): lax.dot_general(left, right, (((1,), (1,)), ((), ())), preferred_element_...]
    pallas_call x9 -> x11, Pallas kernels: 500 us -> 537 us  [the longest x3 213 us: gather(): pl.pallas_call(functools.partial(gather_kernel, zs, tuple(flags), len(mov...]
    dot_general x5 -> x2, matrix products: 43.7 us -> 14.7 us  [product(): return jnp.dot(left, right, preferred_element_type=jnp.float32)]
    dot_general x5 -> x3, matrix products: 39.5 us -> 12.1 us  [product_tn(): lax.dot_general(left, right, (((0,), (0,)), ((), ())), preferred_element_...]
    ppermute x0 -> x8, starting transfers between devices: none -> 22.1 us  [permute(): lax.ppermute(array, 'seq', self.along(way, lo, hi))]
    ppermute x0 -> x8, waiting for transfers between devices: none -> 17.7 us  [permute(): lax.ppermute(array, 'seq', self.along(way, lo, hi))]
    sub x1 -> x0, matrix products: 17.6 us -> none  [on_device(): exps = jnp.exp(scores - top)]
  transfers between devices with their start and end apart: 6 -> 8, of which waited for: 0 -> 4; matrix products, arithmetic and copies ran while one was open for 34% -> 6% of each run, Pallas kernels for 55% -> 3%
where the time goes in v2:
time: 690 us; the launch traced here: 679 us
  Pallas kernels  537 us (78%)
  matrix products  40.9 us (6%)
  other arithmetic  31.7 us (5%)
  local copies, waits for them, and re-layouts  27.1 us (4%)
  starting transfers between devices  22.1 us (3%)
  waiting for transfers between devices  17.7 us (3%)
    pallas_call x3, Pallas kernels, gather(): pl.pallas_call(functools.partial(gather_kernel, zs, tuple(flags), len(mov...  213 us
    pallas_call x3, Pallas kernels, scatter(): pl.pallas_call(functools.partial(scatter_kernel, all_zs, tuple(flags), le...  207 us
    pallas_call x1, Pallas kernels, feed_forward(): pl.pallas_call(functools.partial(ffn_kernel, zs, len(both_pieces)), grid=...  74.9 us
    pallas_call x1, Pallas kernels, attend_back(): pl.pallas_call(attend_back_kernel, grid_spec=pltpu.PrefetchScalarGridSpec...  22.4 us
    ppermute x8, starting transfers between devices, permute(): lax.ppermute(array, 'seq', self.along(way, lo, hi))  22.1 us
    ppermute x8, waiting for transfers between devices, permute(): lax.ppermute(array, 'seq', self.along(way, lo, hi))  17.7 us
    dot_general x2, matrix products, product(): return jnp.dot(left, right, preferred_element_type=jnp.float32)  14.7 us
    dot_general x3, matrix products, product_nt(): lax.dot_general(left, right, (((1,), (1,)), ((), ())), preferred_element_...  14.1 us
  transfers between devices with their start and end apart: 8, of which 4 were waited for; matrix products, arithmetic and copies ran while one was open for 6% of the time, Pallas kernels for 3%

profile of v2, /device:TPU:8, one launch (start us, length us, event | category | flops | bytes accessed | tf_op | source)
XLA Modules:
  0.0 678.6 jit_solution(4591021945906658745)
XLA Ops:
  1.5 3.1 shard_map.212.refs_1_
  5.4 72.2 %shard_map.213 = (bf16[4,2,4,64,2688]{4,3,2,1,0:T(8,128)(2,1)}, bf16[2,4,64,1408]{3,2,1,0:T(8,128)(2,1)}, bf16[2,4,64,1408]{3,2,1,0:T(8,128)(2,1)}, bf16[2,4,64,1408]{3,2,1,0:T(8,128)(2,1)}) custom-call(bf16[64,2688]{1,0:T(8,128)(2,1)} %fusion.21.refs_0_, bf16[2,4,64,1408]{3,2,1,0:T(8,128)(2,1)} %shard_map.212.refs_1_), custom_call_target="tpu_custom_call" | custom-call | flops 49999998976 | bytes 157286400 | tf_op jit(solution)/shard_map/pallas_call | solution.py:273
  77.6 4.1 collective-permute-start
  81.7 2.6 collective-permute-start.1
  84.5 2.5 slice_convert_fusion
  88.0 8.9 %fusion.31.lin_ref = f32[256,2688]{1,0:T(8,128)} fusion(bf16[256,2048]{1,0:T(8,128)(2,1)S(1)} %bitcast.135, bf16[2048,2688]{1,0:T(8,128)(2,1)} %bitcast.138), kind=kOutput, calls=%fused_computation.96 | convolution fusion | flops 2818572288 | bytes 14811136 | tf_op jit(solution)/shard_map/dot_general | solution.py:27
  110.6 92.5 %shard_map.214 = (bf16[4,2,256,512]{3,2,1,0:T(8,128)(2,1)}, bf16[4,2,4,64,2048]{4,3,2,1,0:T(8,128)(2,1)}, bf16[2,4,256,2048]{3,2,1,0:T(8,128)(2,1)}, bf16[512,1408]{1,0:T(8,128)(2,1)}, bf16[512,1408]{1,0:T(8,128)(2,1)}) custom-call(bf16[256,512]{1,0:T(8,128)(2,1)} %pad_maximum_fusion.1.refs_0_, bf16[64,2048]{1,0:T(8,128)(2,1)} %refs_1_.1, ...), custom_call_target="tpu_custom_call" | custom-call | flops 49999998976 | bytes 157286400 | tf_op jit(solution)/shard_map/pallas_call | solution.py:273
  204.8 13.5 %shard_map.215 = (bf16[256,2048]{1,0:T(8,128)(2,1)S(1)}, bf16[256,2048]{1,0:T(8,128)(2,1)S(1)}) custom-call(s32[16]{0:T(128)S(1)} %copy-done.8, s32[16]{0:T(128)S(1)} %get-tuple-element.63.inverse_ref, s32[2]{0:T(128)S(1)} %slice_reduce_fusion.2.first_ref, f32[256,2688]{1,0:T(8,128)} %fusion.31.lin_ref, f32[256,512]{1,0:T(8,128)S(1)} %copy.70.cos_ref, ...), custom_call_target="tpu_custom_call" | custom-call | flops 2147483648 | bytes 16777216 | tf_op jit(solution)/shard_map/pallas_call | solution.py:595
  218.3 3.5 collective-permute-start.2
  221.8 2.2 collective-permute-start.3
  224.0 5.9 multiply_reduce_fusion.4
  232.5 2.4 collective-permute-done.2.refs_3_.refs_11_
  234.9 4.0 collective-permute-done.3.refs_4_.refs_14_
  239.8 47.8 %shard_map.216 = (bf16[2,4,256,2048]{3,2,1,0:T(8,128)(2,1)}, bf16[512,1408]{1,0:T(8,128)(2,1)}, bf16[512,1408]{1,0:T(8,128)(2,1)}, bf16[176,2048]{1,0:T(8,128)(2,1)}, bf16[176,2048]{1,0:T(8,128)(2,1)}) custom-call(bf16[256,2048]{1,0:T(8,128)(2,1)} %multiply_convert_fusion.1.refs_0_, bf16[512,1408]{1,0:T(8,128)(2,1)} %get-tuple-element.77.refs_1_.refs_4_, ...), custom_call_target="tpu_custom_call" | custom-call | flops 49999998976 | bytes 157286400 | tf_op jit(solution)/shard_map/pallas_call | solution.py:273
  287.6 74.9 %shard_map.217 = (bf16[2048,2048]{1,0:T(8,128)(2,1)}, bf16[2048,2048]{1,0:T(8,128)(2,1)}, bf16[2048,1408]{1,0:T(8,128)(2,1)}, bf16[704,2048]{1,0:T(8,128)(2,1)}) custom-call(bf16[2048,2048]{1,0:T(8,128)(2,1)} %bitcast.157, bf16[2048,2048]{1,0:T(8,128)(2,1)} %bitcast.156, bf16[512,1408]{1,0:T(8,128)(2,1)} %bitcast.159, bf16[512,1408]{1,0:T(8,128)(2,1)} %bitcast.161, ...), custom_call_target="tpu_custom_call" | custom-call | flops 53150220288 | bytes 62914560 | tf_op jit(solution)/shard_map/pallas_call | solution.py:711
  364.7 2.3 dynamic-slice_bitcast_fusion.2
  367.2 54.6 %shard_map.218 = (f32[256,2048]{1,0:T(8,128)S(1)}, bf16[512,1408]{1,0:T(8,128)(2,1)S(1)}, bf16[512,1408]{1,0:T(8,128)(2,1)S(1)}, bf16[176,2048]{1,0:T(8,128)(2,1)S(1)}, bf16[176,2048]{1,0:T(8,128)(2,1)S(1)}) custom-call(bf16[2,4,256,2048]{3,2,1,0:T(8,128)(2,1)S(1)} %bitcast.108, bf16[512,1408]{1,0:T(8,128)(2,1)S(1)} %get-tuple-element.172.refs_1_, ...), custom_call_target="tpu_custom_call" | custom-call | flops 49999998976 | bytes 157286400 | tf_op jit(solution)/shard_map/pallas_call | solution.py:459
  425.8 2.6 collective-permute-start.4
  431.4 4.5 collective-permute-start.6
  437.2 3.4 convolution_convert_fusion.2.d_ref
  440.7 22.4 %shard_map.219 = (bf16[256,2048]{1,0:T(8,128)(2,1)}, bf16[8,256,512]{2,1,0:T(8,128)(2,1)}) custom-call(s32[16]{0:T(128)} %order_ref.3, s32[16]{0:T(128)} %copy-done.11, s32[2]{0:T(128)} %copy-done.7, bf16[256,2048]{1,0:T(8,128)(2,1)} %copy-done.12, bf16[256,2048]{1,0:T(8,128)(2,1)} %convolution_convert_fusion.2.d_ref, f32[256,512]{1,0:T(8,128)} %copy-done, ...), custom_call_target="tpu_custom_call" | custom-call | flops 5368709120 | bytes 25165824 | tf_op jit(solution)/shard_map/pallas_call | solution.py:616
  463.1 5.7 convolution_convert_fusion.1
  468.9 9.2 %collective-permute-done.6 = bf16[176,2048]{1,0:T(8,128)(2,1)S(1)} collective-permute-done((bf16[176,2048]{1,0:T(8,128)(2,1)}, bf16[176,2048]{1,0:T(8,128)(2,1)S(1)}, u32[]{:S(2)}, u32[]{:S(2)}) %collective-permute-start.6) | collective-permute-done | bytes 720928 | tf_op jit(solution)/shard_map/ppermute | solution.py:785
  480.2 5.7 convolution_convert_fusion
  485.9 4.2 fusion.4
  490.1 116.6 %shard_map.220 = (f32[256,512]{1,0:T(8,128)S(1)}, f32[64,2048]{1,0:T(8,128)S(1)}, f32[64,2048]{1,0:T(8,128)S(1)}, f32[256,2048]{1,0:T(8,128)}, bf16[512,1408]{1,0:T(8,128)(2,1)}, /*index=5*/bf16[512,1408]{1,0:T(8,128)(2,1)}) custom-call(bf16[4,2,256,512]{3,2,1,0:T(8,128)(2,1)} %bitcast.158, bf16[4,2,4,64,2048]{4,3,2,1,0:T(8,128)(2,1)} %bitcast.118, ...), custom_call_target="tpu_custom_call" | custom-call | flops 49999998976 | bytes 157286400 | tf_op jit(solution)/shard_map/pallas_call | solution.py:459
  608.1 2.5 fusion.11
  610.6 8.2 %multiply_reduce_fusion.1 = (bf16[2048]{0:T(1024)(128)(2,1)S(1)}, f32[256]{0:T(256)}, f32[256,2048]{1,0:T(8,128)}) fusion(bf16[2,1,128,2048]{3,2,1,0:T(8,128)(2,1)S(1)} %copy-done.18, f32[256]{0:T(256)S(1)} %copy-done.44, f32[2048]{0:T(1024)S(1)} %bitcast.143, f32[256,2048]{1,0:T(8,128)S(1)} %fusion.11, bf16[256,2048]{1,0:T(8,128)(2,1)S(1)} %copy-done.30, ...), kind=kOutput, calls=%fused_computation.23 | convolution fusion | flops 2151675648 | bytes 14694400 | tf_op jit(solution)/shard_map/dot_general | solution.py:31
  627.1 36.2 %shard_map.221 = (f32[64,640]{1,0:T(8,128)S(1)}, bf16[2,4,64,1408]{3,2,1,0:T(8,128)(2,1)S(1)}, bf16[176,2048]{1,0:T(8,128)(2,1)S(1)}, bf16[176,2048]{1,0:T(8,128)(2,1)S(1)}) custom-call(bf16[4,2,4,64,640]{4,3,2,1,0:T(8,128)(2,1)S(1)} %pad_maximum_fusion.refs_0_, bf16[2,4,64,1408]{3,2,1,0:T(8,128)(2,1)S(1)} %bitcast.107, ...), custom_call_target="tpu_custom_call" | custom-call | flops 49999998976 | bytes 157286400 | tf_op jit(solution)/shard_map/pallas_call | solution.py:459
  667.0 3.3 shard_map.222
  670.3 3.8 add_convert_fusion
  674.1 2.6 fusion.13
  (176 shorter events, 48.8 us)
Async XLA Ops:
  5.4 79.0 %copy-start.48 = (s32[2,1,2]{2,1,0:T(1,128)S(1)}, s32[2,1,2]{2,1,0:T(1,128)}, u32[]{:S(2)}) copy-start(s32[2,1,2]{2,1,0:T(1,128)} %param.23) | copy-start | bytes 52
  77.6 33.0 %collective-permute-start = (bf16[176,2048]{1,0:T(8,128)(2,1)}, bf16[176,2048]{1,0:T(8,128)(2,1)}, u32[]{:S(2)}, u32[]{:S(2)}) collective-permute-start(bf16[176,2048]{1,0:T(8,128)(2,1)} %refs_9_.1), channel_id=1, source_target_pairs={{0,8},{4,12},{8,16},{12,20},{16,24},{20,28},{1,9},{5,13},{9,17},{1... | collective-permute-start | bytes 2162696 | tf_op jit(solution)/shard_map/ppermute | solution.py:785
  81.7 29.0 %collective-permute-start.1 = (bf16[176,2048]{1,0:T(8,128)(2,1)}, bf16[176,2048]{1,0:T(8,128)(2,1)}, u32[]{:S(2)}, u32[]{:S(2)}) collective-permute-start(bf16[176,2048]{1,0:T(8,128)(2,1)} %refs_9_.1), channel_id=1, source_target_pairs={{8,0},{12,4},{16,8},{20,12},{24,16},{28,20},{9,1},{13,5},{17,9},{2... | collective-permute-start | bytes 2162696 | tf_op jit(solution)/shard_map/ppermute | solution.py:785
  84.5 118.7 %copy-start.7 = (s32[2]{0:T(128)}, s32[2]{0:T(128)S(1)}, u32[]{:S(2)}) copy-start(s32[2]{0:T(128)S(1)} %slice_reduce_fusion.2.first_ref) | copy-start | bytes 28
  87.3 9.7 %copy-start.35 = (f32[2048,1]{0,1:T(1,128)}, f32[2048,1]{0,1:T(1,128)S(1)}, u32[]{:S(2)}) copy-start(f32[2048,1]{0,1:T(1,128)S(1)} %copy.85) | copy-start | bytes 24580
  87.7 9.4 %copy-start.43 = (f32[256]{0:T(256)}, f32[256]{0:T(256)S(1)}, u32[]{:S(2)}) copy-start(f32[256]{0:T(256)S(1)} %get-tuple-element.184) | copy-start | bytes 3076
  97.3 9.6 %copy-start.19 = (bf16[256,2048]{1,0:T(8,128)(2,1)}, bf16[256,2048]{1,0:T(8,128)(2,1)S(1)}, u32[]{:S(2)}) copy-start(bf16[256,2048]{1,0:T(8,128)(2,1)S(1)} %multiply_convert_fusion) | copy-start | bytes 3145732
  99.7 103.5 %copy-start = (f32[256,512]{1,0:T(8,128)}, f32[256,512]{1,0:T(8,128)S(1)}, u32[]{:S(2)}) copy-start(f32[256,512]{1,0:T(8,128)S(1)} %copy.70.cos_ref) | copy-start | bytes 1572868
  102.6 100.6 %copy-start.2 = (f32[256,512]{1,0:T(8,128)}, f32[256,512]{1,0:T(8,128)S(1)}, u32[]{:S(2)}) copy-start(f32[256,512]{1,0:T(8,128)S(1)} %copy.71.sin_ref) | copy-start | bytes 1572868
  106.9 123.0 %copy-start.37 = (f32[2048,1]{0,1:T(1,128)}, f32[2048,1]{0,1:T(1,128)S(1)}, u32[]{:S(2)}) copy-start(f32[2048,1]{0,1:T(1,128)S(1)} %copy.86) | copy-start | bytes 24580
  110.6 92.6 %copy-start.11 = (s32[16]{0:T(128)}, s32[16]{0:T(128)S(1)}, u32[]{:S(2)}) copy-start(s32[16]{0:T(128)S(1)} %get-tuple-element.63.inverse_ref) | copy-start | bytes 196
  218.3 11.6 %copy-start.4 = (bf16[256,2048]{1,0:T(8,128)(2,1)}, bf16[256,2048]{1,0:T(8,128)(2,1)S(1)}, u32[]{:S(2)}) copy-start(bf16[256,2048]{1,0:T(8,128)(2,1)S(1)} %get-tuple-element.71) | copy-start | bytes 3145732
  218.3 11.6 %copy-start.12 = (bf16[256,2048]{1,0:T(8,128)(2,1)}, bf16[256,2048]{1,0:T(8,128)(2,1)S(1)}, u32[]{:S(2)}) copy-start(bf16[256,2048]{1,0:T(8,128)(2,1)S(1)} %get-tuple-element.73.q_ref) | copy-start | bytes 3145732
  218.3 16.5 %collective-permute-start.2 = (bf16[176,2048]{1,0:T(8,128)(2,1)}, bf16[176,2048]{1,0:T(8,128)(2,1)S(1)}, u32[]{:S(2)}, u32[]{:S(2)}) collective-permute-start(bf16[176,2048]{1,0:T(8,128)(2,1)} %collective-permute-done.refs_10_), channel_id=1, source_target_pairs={{8,16},{12,20},{16,24},{20,28},{9,17},{13,21},{17,25},{21,29},{10,... | collective-permute-start | bytes 2162696 | tf_op jit(solution)/shard_map/ppermute | solution.py:785
  221.8 17.1 %collective-permute-start.3 = (bf16[176,2048]{1,0:T(8,128)(2,1)}, bf16[176,2048]{1,0:T(8,128)(2,1)S(1)}, u32[]{:S(2)}, u32[]{:S(2)}) collective-permute-start(bf16[176,2048]{1,0:T(8,128)(2,1)} %collective-permute-done.1.refs_13_), channel_id=1, source_target_pairs={{8,0},{12,4},{16,8},{20,12},{9,1},{13,5},{17,9},{21,13},{10,2},{14... | collective-permute-start | bytes 2162696 | tf_op jit(solution)/shard_map/ppermute | solution.py:785
  364.7 59.1 %slice-start = ((s8[5767168]{0:T(1024)(128)(4,1)}), s8[4194304]{0:T(1024)(128)(4,1)S(1)}, s32[]{:S(2)}) async-start(s8[5767168]{0:T(1024)(128)(4,1)} %bitcast.114), calls=%async_computation | async-start | bytes 8388608
  367.2 54.6 %copy-start.14 = (f32[256,2048]{1,0:T(8,128)S(1)}, f32[256,2048]{1,0:T(8,128)}, u32[]{:S(2)}) copy-start(f32[256,2048]{1,0:T(8,128)} %copy-done.13) | copy-start | bytes 6291460
  367.2 54.6 %copy-start.38 = (f32[2048,1]{0,1:T(1,128)S(1)}, f32[2048,1]{0,1:T(1,128)}, u32[]{:S(2)}) copy-start(f32[2048,1]{0,1:T(1,128)} %copy-done.37) | copy-start | bytes 24580
  367.2 54.7 %copy-start.42 = (f32[256]{0:T(256)S(1)}, f32[256]{0:T(256)}, u32[]{:S(2)}) copy-start(f32[256]{0:T(256)} %copy-done.41) | copy-start | bytes 3076
  367.2 56.6 %slice-start.1 = ((s8[5767168]{0:T(1024)(128)(4,1)}), s8[1572864]{0:T(1024)(128)(4,1)S(1)}, s32[]{:S(2)}) async-start(s8[5767168]{0:T(1024)(128)(4,1)} %bitcast.114), calls=%async_computation.1 | async-start | bytes 3145728
  423.0 14.2 %slice-start.3 = ((s8[8388608]{0:T(1024)(128)(4,1)}), s8[4194304]{0:T(1024)(128)(4,1)S(1)}, s32[]{:S(2)}) async-start(s8[8388608]{0:T(1024)(128)(4,1)} %bitcast.153), calls=%async_computation.3 | async-start | bytes 8388608
  423.7 39.4 %copy-start.16 = (f32[256,2048]{1,0:T(8,128)}, f32[256,2048]{1,0:T(8,128)S(1)}, u32[]{:S(2)}) copy-start(f32[256,2048]{1,0:T(8,128)S(1)} %multiply_add_fusion) | copy-start | bytes 6291460
  423.8 13.5 %slice-start.4 = ((s8[8388608]{0:T(1024)(128)(4,1)}), s8[4194304]{0:T(1024)(128)(4,1)S(1)}, s32[]{:S(2)}) async-start(s8[8388608]{0:T(1024)(128)(4,1)} %bitcast.153), calls=%async_computation.4 | async-start | bytes 8388608
  425.8 54.4 %collective-permute-start.4 = (bf16[512,1408]{1,0:T(8,128)(2,1)}, bf16[512,1408]{1,0:T(8,128)(2,1)S(1)}, u32[]{:S(2)}, u32[]{:S(2)}) collective-permute-start(bf16[512,1408]{1,0:T(8,128)(2,1)} %get-tuple-element.170), channel_id=1, source_target_pairs={{0,8},{4,12},{8,16},{12,20},{1,9},{5,13},{9,17},{13,21},{2,10},{6,... | collective-permute-start | bytes 4325384 | tf_op jit(solution)/shard_map/ppermute | solution.py:785
  428.4 51.8 %collective-permute-start.5 = (bf16[512,1408]{1,0:T(8,128)(2,1)S(1)}, bf16[512,1408]{1,0:T(8,128)(2,1)S(1)}, u32[]{:S(2)}, u32[]{:S(2)}) collective-permute-start(bf16[512,1408]{1,0:T(8,128)(2,1)S(1)} %get-tuple-element.169), channel_id=1, source_target_pairs={{16,8},{20,12},{24,16},{28,20},{17,9},{21,13},{25,17},{29,21},{18,... | collective-permute-start | bytes 4325384 | tf_op jit(solution)/shard_map/ppermute | solution.py:785
  431.4 46.7 %collective-permute-start.6 = (bf16[176,2048]{1,0:T(8,128)(2,1)}, bf16[176,2048]{1,0:T(8,128)(2,1)S(1)}, u32[]{:S(2)}, u32[]{:S(2)}) collective-permute-start(bf16[176,2048]{1,0:T(8,128)(2,1)} %get-tuple-element.176), channel_id=1, source_target_pairs={{0,8},{4,12},{8,16},{12,20},{1,9},{5,13},{9,17},{13,21},{2,10},{6,... | collective-permute-start | bytes 2162696 | tf_op jit(solution)/shard_map/ppermute | solution.py:785
  435.9 44.3 %collective-permute-start.7 = (bf16[176,2048]{1,0:T(8,128)(2,1)}, bf16[176,2048]{1,0:T(8,128)(2,1)}, u32[]{:S(2)}, u32[]{:S(2)}) collective-permute-start(bf16[176,2048]{1,0:T(8,128)(2,1)} %get-tuple-element.175), channel_id=1, source_target_pairs={{16,8},{20,12},{24,16},{28,20},{17,9},{21,13},{25,17},{29,21},{18,... | collective-permute-start | bytes 2162696 | tf_op jit(solution)/shard_map/ppermute | solution.py:785
  440.7 22.4 %copy-start.5 = (bf16[256,2048]{1,0:T(8,128)(2,1)S(1)}, bf16[256,2048]{1,0:T(8,128)(2,1)}, u32[]{:S(2)}) copy-start(bf16[256,2048]{1,0:T(8,128)(2,1)} %copy-done.4) | copy-start | bytes 3145732
  463.1 17.1 %copy-start.20 = (bf16[256,2048]{1,0:T(8,128)(2,1)S(1)}, bf16[256,2048]{1,0:T(8,128)(2,1)}, u32[]{:S(2)}) copy-start(bf16[256,2048]{1,0:T(8,128)(2,1)} %copy-done.19) | copy-start | bytes 3145732
  463.1 17.1 %copy-start.29 = (bf16[256,2048]{1,0:T(8,128)(2,1)S(1)}, bf16[256,2048]{1,0:T(8,128)(2,1)}, u32[]{:S(2)}) copy-start(bf16[256,2048]{1,0:T(8,128)(2,1)} %get-tuple-element.97) | copy-start | bytes 3145732
  627.1 38.7 %copy-start.15 = (f32[256,2048]{1,0:T(8,128)S(1)}, f32[256,2048]{1,0:T(8,128)}, u32[]{:S(2)}) copy-start(f32[256,2048]{1,0:T(8,128)} %copy-done.13) | copy-start | bytes 6291460
  627.1 38.7 %copy-start.24 = (f32[256,2048]{1,0:T(8,128)S(1)}, f32[256,2048]{1,0:T(8,128)}, u32[]{:S(2)}) copy-start(f32[256,2048]{1,0:T(8,128)} %get-tuple-element.101) | copy-start | bytes 6291460
  (30 other events, 93.6 us)

commit v3 on v2

--- a/solution.py
+++ b/solution.py
@@ -45,6 +45,13 @@
     return factor * (inner - normed * mean), jnp.sum(d_scaled * normed, axis=0)
 
 
+def turn(tensor, cosine, sine):
+    rows, lanes = tensor.shape
+    half = HEAD_DIM // 2
+    swapped = jnp.flip(tensor.reshape(rows, lanes // HEAD_DIM, 2, half), axis=2).reshape(rows, lanes)
+    return tensor * jnp.tile(cosine, (1, lanes // 128)) + swapped * jnp.tile(sine, (1, lanes // 128))
+
+
 def slot_places(order, half_len, slot_ids):
     matches = (slot_ids // half_len)[:, None] == jnp.arange(order.shape[0], dtype=jnp.int32)[None, :]
     return jnp.sum(jnp.where(matches, order[None, :], 0), axis=1) * half_len + slot_ids % half_len
@@ -97,9 +104,11 @@
         for i, other in enumerate(self.others):
             dst = self.out.at[other]
             send(dst, dst, self.ssem.at[i], self.rsem.at[i], self.devices[i]).wait_recv()
+        self.local.wait()
+
+    def end(self):
         for copy in self.copies:
             copy.wait_send()
-        self.local.wait()
 
 
 class Line:
@@ -135,153 +144,117 @@
     return devices + [(lax.rem(z + k, zs) * 2 + c, r) for k in range(1, zs)]
 
 
-def gather_kernel(zs, flags, moves, lines, *refs):
-    count = len(flags)
-    carried = sum(not source for source, *_ in lines)
-    taken = count + moves + carried
-    own, line_own = refs[:count], refs[count + moves : taken]
-    out, line_out = refs[taken : taken + count], refs[taken + count + moves : taken + count + moves + len(lines)]
-    moved = [(refs[count + n], refs[taken + count + n]) for n in range(moves)]
-    sems = refs[taken + count + moves + len(lines) :]
-    z_ssem, z_rsem, f_ssem, f_rsem, h_ssem, h_rsem, c_ssem, c_rsem, l_sem = sems[:9]
-    z, c, r = place()
-    line = corners(r)
-    s = z * 2 + c
-    reach = zs if lines or any(flag[0] for flag in flags) else 1
-
-    def at_z(other):
-        return (other * 2 + c, r)
-
-    twin = (z * 2 + 1 - c, r)
-    greet(neighbours(reach, any(flag[1] for flag in flags), moves))
-    exchanges = [Exchange(*pair, *sems[9 + 3 * n : 12 + 3 * n]) for n, pair in enumerate(moved)]
-    waiting = list(line_own)
-    going = [
-        Line(zs, *way, moved[source - 1][1] if source else waiting.pop(0), dst, sems[9 + 3 * moves + n])
-        for n, ((source, *way), dst) in enumerate(zip(lines, line_out))
-    ]
-
-    items = [(a, k) for k in range(zs) for a in range(count) if k == 0 or flags[a][0]]
-    pending = []
-
-    def slot(a, k, other, j):
-        z_flag, planes = flags[a]
-        if not z_flag:
-            return out[a].at[other, j]
-        core = 1 - c if other else c
-        zz = lax.rem(z - k + zs, zs)
-        return out[a].at[zz, core, line[j]] if planes else out[a].at[zz, core]
-
-    def arrival(a, k, other, j):
-        z_flag, planes = flags[a]
-        if not z_flag:
-            return out[a].at[other, j]
-        zz = lax.rem(z - k + zs, zs)
-        return out[a].at[zz, c, r] if planes else out[a].at[zz, c]
-
-    for a in range(count):
-        local = pltpu.make_async_copy(own[a], slot(a, 0, 0, 0), l_sem.at[a])
-        local.start()
-        pending.append(local.wait)
-    for exchange_one in exchanges:
-        exchange_one.start()
-    for i, (a, k) in enumerate(items):
+class Gather:
+    def __init__(self, zs, z_flag, planes, own, out, z_ssem, z_rsem, f_ssem, f_rsem, h_ssem, h_rsem, c_ssem, c_rsem, l_sem):
+        self.__dict__.update(locals())
+        self.z, self.c, self.r = place()
+        self.line = corners(self.r)
+        self.s = self.z * 2 + self.c
+        self.twin = (self.z * 2 + 1 - self.c, self.r)
+        self.count = zs if z_flag else 1
+        self.half = own.shape[0] // 2
+        self.pending = []
+
+    def start(self, copy):
+        copy.start()
+        self.pending.append(copy.wait_send)
+
+    def slot(self, k, other, j):
+        if not self.z_flag:
+            return self.out.at[other, j]
+        core = 1 - self.c if other else self.c
+        zz = lax.rem(self.z - k + self.zs, self.zs)
+        return self.out.at[zz, core, self.line[j]] if self.planes else self.out.at[zz, core]
+
+    def z_copy(self, k, dst):
+        src = self.own if dst is None else dst
+        dst = self.slot(0, 0, 0) if dst is None else dst
+        to = (lax.rem(self.z + k, self.zs) * 2 + self.c, self.r)
+        return send(src, dst, self.z_ssem.at[k], self.z_rsem.at[k], to)
+
+    def near(self, k, j, src):
+        dst = self.slot(k, 0, j) if src is None or not self.z_flag else self.slot(k, 0, 0)
+        return send(dst if src is None else src, dst, self.f_ssem.at[k, j - 1], self.f_rsem.at[k, j - 1], (self.s, self.line[j]))
+
+    def part(self, ref, j):
+        return ref.at[pl.ds(self.half if j == 1 else 0, self.half)]
+
+    def far(self, k, j, src):
+        if src is None:
+            src = dst = self.part(self.slot(k, 0, 3), j)
+        else:
+            dst = self.part(src if self.z_flag else self.out.at[0, 3], j)
+            src = self.part(src, j)
+        return send(src, dst, self.h_ssem.at[k, j - 1], self.h_rsem.at[k, j - 1], (self.s, self.line[3 - j]))
+
+    def to_twin(self, k, j, src):
+        dst = self.slot(k, 0, j) if self.z_flag else self.out.at[1, j]
+        self.start(send(src, dst, self.c_ssem.at[k, j], self.c_rsem.at[k, j], self.twin))
+
+    def launch(self):
+        self.local = pltpu.make_async_copy(self.own, self.slot(0, 0, 0), self.l_sem)
+        self.local.start()
+        for k in range(1, self.count):
+            self.start(self.z_copy(k, None))
+
+    def begin(self, k):
+        src = self.own
         if k:
-            copy = send(own[a], arrival(a, 0, 0, 0), z_ssem.at[i], z_rsem.at[i], at_z(lax.rem(z + k, zs)))
-            copy.start()
-            pending.append(copy.wait_send)
-
-    def to_twin(i, j, src):
-        a, k = items[i]
-        dst = slot(a, k, 0, j) if flags[a][0] else out[a].at[1, j]
-        copy = send(src, dst, c_ssem.at[i, j], c_rsem.at[i, j], twin)
-        copy.start()
-        pending.append(copy.wait_send)
-
-    def begin(i):
-        a, k = items[i]
-        src = own[a]
-        if k:
-            src = slot(a, k, 0, 0)
-            send(src, src, z_ssem.at[i], z_rsem.at[i], at_z(lax.rem(z + k, zs))).wait_recv()
-        if flags[a][1]:
+            src = self.slot(k, 0, 0)
+            self.z_copy(k, src).wait_recv()
+        if self.planes:
             for j in (1, 2):
-                copy = send(src, arrival(a, k, 0, j), f_ssem.at[i, j - 1], f_rsem.at[i, j - 1], (s, line[j]))
-                copy.start()
-                pending.append(copy.wait_send)
-        to_twin(i, 0, src)
-
-    def halves(a, ref, j):
-        half = own[a].shape[0] // 2
-        return ref.at[pl.ds(half if j == 1 else 0, half)]
-
-    def forward(i):
-        a, k = items[i]
+                self.start(self.near(k, j, src))
+        self.to_twin(k, 0, src)
+
+    def forward(self, k):
         for j in (1, 2):
-            src = slot(a, k, 0, j)
-            send(src, src, f_ssem.at[i, j - 1], f_rsem.at[i, j - 1], (s, line[j])).wait_recv()
-            there = slot(a, k, 0, j) if flags[a][0] else out[a].at[0, 3]
-            copy = send(
-                halves(a, src, j), halves(a, there, j), h_ssem.at[i, j - 1], h_rsem.at[i, j - 1], (s, line[3 - j])
-            )
-            copy.start()
-            pending.append(copy.wait_send)
-            to_twin(i, j, src)
-
-    def finish(i):
-        a, k = items[i]
-        src = slot(a, k, 0, 3)
+            self.near(k, j, None).wait_recv()
+            src = self.slot(k, 0, j)
+            self.start(self.far(k, j, src))
+            self.to_twin(k, j, src)
+
+    def finish(self, k):
         for j in (1, 2):
-            part = halves(a, src, j)
-            send(part, part, h_ssem.at[i, j - 1], h_rsem.at[i, j - 1], (s, line[3 - j])).wait_recv()
-        to_twin(i, 3, src)
-
-    total = len(items)
-    for i in range(total + 2):
-        if i < total:
-            begin(i)
-        if i == total - 1:
-            for exchange_one in exchanges:
-                exchange_one.finish()
-            for one in going:
-                one.start()
-        if 1 <= i <= total and flags[items[i - 1][0]][1]:
-            forward(i - 1)
-        if i >= 2 and flags[items[i - 2][0]][1]:
-            finish(i - 2)
-    for i, (a, k) in enumerate(items):
-        for j in range(4 if flags[a][1] else 1):
-            dst = slot(a, k, 1, j)
-            send(dst, dst, c_ssem.at[i, j], c_rsem.at[i, j], twin).wait_recv()
-    for one in going:
-        one.finish()
-    for wait in pending:
-        wait()
-
-
-def gather(arrays, flags, zs, collective_id, moved=(), lines=()):
-    carried = [line[0] for line in lines if not isinstance(line[0], int)]
-    plan = tuple((line[0] if isinstance(line[0], int) else 0,) + tuple(line[1:]) for line in lines)
-    line_shapes = [moved[line[0] - 1] if isinstance(line[0], int) else line[0] for line in lines]
-    n = sum(zs if z_flag else 1 for z_flag, _ in flags)
+            self.far(k, j, None).wait_recv()
+        self.to_twin(k, 3, self.slot(k, 0, 3))
+
+    def complete(self, k):
+        if k == 0:
+            self.local.wait()
+        for j in range(4 if self.planes else 1):
+            dst = self.slot(k, 1, j)
+            send(dst, dst, self.c_ssem.at[k, j], self.c_rsem.at[k, j], self.twin).wait_recv()
+
+    def end(self):
+        for wait in self.pending:
+            wait()
+
+
+def gather_sems(zs, z_flag):
     sem = pltpu.SemaphoreType.DMA
-    anywhere = pl.BlockSpec(memory_space=pl.ANY)
-    shapes = [
-        jax.ShapeDtypeStruct(((zs,) if z_flag else ()) + (2,) + ((4,) if planes else ()) + a.shape, a.dtype)
-        for a, (z_flag, planes) in zip(arrays, flags)
-    ] + [jax.ShapeDtypeStruct(m.shape, m.dtype) for m in (*moved, *line_shapes)]
-    return pl.pallas_call(
-        functools.partial(gather_kernel, zs, tuple(flags), len(moved), plan),
-        out_shape=shapes,
-        in_specs=[anywhere] * (len(arrays) + len(moved) + len(carried)),
-        out_specs=[anywhere] * len(shapes),
-        scratch_shapes=[
-            sem((n,)), sem((n,)), sem((n, 2)), sem((n, 2)), sem((n, 2)), sem((n, 2)), sem((n, 4)), sem((n, 4)),
-            sem((len(arrays),)),
-        ] + EXCHANGE_SEMS * len(moved) + [LINE_SEMS] * len(lines),
-        compiler_params=pltpu.CompilerParams(collective_id=collective_id, has_side_effects=True),
-        cost_estimate=LONG,
-    )(*arrays, *moved, *carried)
+    n = zs if z_flag else 1
+    return [sem((n,)), sem((n,)), sem((n, 2)), sem((n, 2)), sem((n, 2)), sem((n, 2)), sem((n, 4)), sem((n, 4)), sem]
+
+
+class Chain:
+    def __init__(self, zs, own, got, sems):
+        self.zs, self.own, self.got, self.sems = zs, own, got, sems
+        self.lines = []
+
+    def start(self, k):
+        zs = self.zs
+        up, down = (self.own, self.own) if k == 1 else (self.got[k - 2], self.got[zs + k - 3])
+        self.lines = [
+            Line(zs, 1, k - 1, zs, up, self.got[k - 1], self.sems.at[k - 1]),
+            Line(zs, -1, 0, zs - k + 1, down, self.got[zs + k - 2], self.sems.at[zs + k - 2]),
+        ]
+        for line in self.lines:
+            line.start()
+
+    def finish(self):
+        for line in self.lines:
+            line.finish()
 
 
 class Scatter:
@@ -431,7 +404,7 @@
         one.stage_c(0)
     for one in exchanges + going:
         one.finish()
-    for one in sums:
+    for one in exchanges + sums:
         one.end()
 
 
@@ -513,8 +486,9 @@
     place_here = my_place + lax.broadcasted_iota(jnp.int32, (span, wide), 0)
     start = jnp.where(place_here >= first, first, 0)
     bias[...] = jnp.where((key_place <= place_here) & (key_place >= start), 0.0, NEG_LARGE)
-    cosine, sine = cos_ref[...], sin_ref[...]
     width = GROUP * HEAD_DIM
+    cosine = jnp.concatenate([cos_ref[...]] * (width // 128), axis=1)
+    sine = jnp.concatenate([sin_ref[...]] * (width // 128), axis=1)
     for g in range(KV_HEADS):
         at = slice(g * width, (g + 1) * width)
         lin = lin_ref[:, at]
@@ -545,8 +519,9 @@
     def _():
         sums[...] = jnp.zeros_like(sums)
 
-    cosine, sine = cos_ref[...], sin_ref[...]
     width = GROUP * HEAD_DIM
+    cosine = jnp.concatenate([cos_ref[...]] * (width // 128), axis=1)
+    sine = jnp.concatenate([sin_ref[...]] * (width // 128), axis=1)
     d_keys, d_values = [], []
     for g in range(KV_HEADS):
         at = slice(g * width, (g + 1) * width)
@@ -597,7 +572,7 @@
         grid_spec=pltpu.PrefetchScalarGridSpec(
             num_scalar_prefetch=3,
             grid=(micro, 2),
-            in_specs=[rows(D), rows(GROUP * HEAD_DIM), rows(GROUP * HEAD_DIM), whole],
+            in_specs=[rows(D), rows(128), rows(128), whole],
             out_specs=[rows(D), rows(D)],
             scratch_shapes=[pltpu.VMEM((wide, 2 * KVW), jnp.bfloat16), pltpu.VMEM((half_len, wide), jnp.float32)],
         ),
@@ -618,7 +593,7 @@
         grid_spec=pltpu.PrefetchScalarGridSpec(
             num_scalar_prefetch=3,
             grid=(micro, 2),
-            in_specs=[rows(D), rows(D), rows(GROUP * HEAD_DIM), rows(GROUP * HEAD_DIM), whole],
+            in_specs=[rows(D), rows(D), rows(128), rows(128), whole],
             out_specs=[rows(D), whole],
             scratch_shapes=[
                 pltpu.VMEM((wide, 2 * KVW), jnp.bfloat16),
@@ -761,6 +736,229 @@
     return pl.pallas_call(functools.partial(collect_kernel, zs, rows, unit), out_shape=[shape, shape])(blocks)
 
 
+def forward_kernel(zs, micro, *refs):
+    order_ref, places_ref, first_ref, freq_ref, x_ref, pack_ref, both_ref, down_ref, out_ref, dy_ref = refs[:10]
+    packed, both_own, kv_all, out_all, dy_all, ffn_all = refs[10:16]
+    steps = 2 * zs - 2
+    both_got, down_got = refs[16 : 16 + steps], refs[16 + steps : 16 + 2 * steps]
+    q_ref, attn_ref, attended_ref, middle_ref, gains_ref, cos_ref, sin_ref = refs[16 + 2 * steps : 23 + 2 * steps]
+    (staged, lin, kv_own, kv_here, window, bias, out_w, ffn_own, sems, *more) = refs[23 + 2 * steps :]
+    low = jnp.bfloat16
+    z, c, r = place()
+    many = x_ref.shape[0]
+    span = many // micro
+    half_len = span // 2
+    rows = D // zs
+    greet(neighbours(zs, True, True))
+
+    exchange = Exchange(both_ref, both_own, *more[:3])
+    both_chain, down_chain = Chain(zs, both_own, both_got, more[3]), Chain(zs, down_ref, down_got, more[4])
+    more = more[5:]
+    weights = Gather(zs, True, True, pack_ref, packed, *more[:9])
+    outs = Gather(zs, True, True, out_ref, out_all, *more[9:18])
+    pairs = Gather(zs, True, False, kv_own, kv_all, *more[18:27])
+    dys = Gather(zs, False, True, dy_ref, dy_all, *more[27:36])
+    ffns = Gather(zs, False, True, ffn_own, ffn_all, *more[36:45])
+
+    weights.launch()
+    exchange.start()
+    weights.begin(0)
+    outs.launch()
+
+    lane = lax.broadcasted_iota(jnp.int32, (half_len, 128), 1)
+    for i in range(2 * micro):
+        place_here = order_ref[(z * 2 + c) * 2 + i % 2] * half_len + lax.broadcasted_iota(jnp.int32, (half_len, 128), 0)
+        start = jnp.where(place_here >= first_ref[i // 2], first_ref[i // 2], 0)
+        angle = (place_here - start).astype(jnp.float32) * freq_ref[...]
+        cos_ref[i * half_len : (i + 1) * half_len, :] = jnp.cos(angle)
+        sine = jnp.sin(angle)
+        sin_ref[i * half_len : (i + 1) * half_len, :] = jnp.where(lax.rem(lane, HEAD_DIM) < HEAD_DIM // 2, -sine, sine)
+    x = x_ref[...].astype(jnp.float32)
+    factor = rms_factor(x)
+
+    loads = {}
+
+    def load(k):
+        weights.complete(k)
+        zz = lax.rem(z - k + zs, zs)
+        loads[k] = pltpu.make_async_copy(packed.at[zz], staged.at[k % 2], sems.at[k % 2])
+        loads[k].start()
+
+    def project(k):
+        loads[k].wait()
+        zz = lax.rem(z - k + zs, zs)
+        at = pl.ds(pl.multiple_of(zz * rows, rows), rows)
+        block = staged[k % 2].reshape(rows, PACK)
+        gains = block[:, QKV:].astype(jnp.float32).T[:8]
+        gains_ref[:, at] = gains
+        attn_in = (x_ref[:, at].astype(jnp.float32) * factor * gains[0:1]).astype(low)
+        attn_ref[:, at] = attn_in
+        value = product(attn_in, block[:, :QKV])
+        lin[...] = value if k == 0 else lin[...] + value
+
+    weights.begin(1)
+    weights.forward(0)
+    weights.begin(2)
+    weights.forward(1)
+    weights.finish(0)
+    weights.begin(3)
+    down_chain.start(1)
+    exchange.finish()
+    both_chain.start(1)
+    weights.forward(2)
+    weights.finish(1)
+    load(0)
+    weights.forward(3)
+    weights.finish(2)
+    outs.begin(0)
+    load(1)
+    project(0)
+    outs.begin(1)
+    project(1)
+    weights.finish(3)
+    dys.launch()
+    dys.begin(0)
+    load(2)
+    load(3)
+    project(2)
+    project(3)
+
+    width = GROUP * HEAD_DIM
+    cosine = jnp.concatenate([cos_ref[...]] * (width // 128), axis=1)
+    sine = jnp.concatenate([sin_ref[...]] * (width // 128), axis=1)
+
+    def turned(block, w):
+        return block * cosine[:, :w] + partner(block) * sine[:, :w]
+
+    kv_own[:, :KVW] = turned(lin[:, D : D + KVW], KVW).astype(low)
+    kv_own[:, KVW:] = lin[:, D + KVW :].astype(low)
+    pairs.launch()
+    pairs.begin(0)
+    for g in range(KV_HEADS):
+        at = slice(g * width, (g + 1) * width)
+        q_ref[:, at] = turned(lin[:, at], width).astype(low) * low(HEAD_DIM ** -0.5)
+    outs.forward(0)
+    outs.begin(2)
+    for k in range(1, zs):
+        pairs.begin(k)
+    outs.forward(1)
+    outs.finish(0)
+    outs.begin(3)
+    for k in range(zs):
+        pairs.complete(k)
+    both_chain.finish()
+    down_chain.finish()
+    both_chain.start(2)
+    down_chain.start(2)
+    kv_load = pltpu.make_async_copy(kv_all, kv_here, sems.at[2])
+    kv_load.start()
+    outs.forward(2)
+    outs.finish(1)
+    kv_load.wait()
+
+    wide = window.shape[0]
+    half_blocks = wide // half_len
+
+    def attend_some(i, carry):
+        m, half = lax.div(i, 2), lax.rem(i, 2)
+        my_block = order_ref[(z * 2 + c) * 2 + half]
+        first_block = jnp.where(my_block >= half_blocks, half_blocks, 0)
+        wanted = first_block * half_len + lax.broadcasted_iota(jnp.int32, (wide, 2 * wide), 0)
+        chosen = jnp.where(places_ref[...] == wanted, 1.0, 0.0).astype(low)
+        at = pl.ds(pl.multiple_of(m * span, span), span)
+        window[...] = product(chosen, kv_here[:, :, at, :].reshape(2 * wide, 2 * KVW)).astype(low)
+        key_place = first_block * half_len + lax.broadcasted_iota(jnp.int32, (half_len, wide), 1)
+        place_here = my_block * half_len + lax.broadcasted_iota(jnp.int32, (half_len, wide), 0)
+        first = first_ref[m]
+        start = jnp.where(place_here >= first, first, 0)
+        bias[...] = jnp.where((key_place <= place_here) & (key_place >= start), 0.0, NEG_LARGE)
+        here = pl.ds(pl.multiple_of(i * half_len, half_len), half_len)
+        for g in range(KV_HEADS):
+            at = slice(g * width, (g + 1) * width)
+            key = window[:, g * HEAD_DIM : (g + 1) * HEAD_DIM]
+            value = window[:, KVW + g * HEAD_DIM : KVW + (g + 1) * HEAD_DIM]
+            scores = product_nt(stack_heads(q_ref[here, at], 0), key).reshape(GROUP, half_len, wide) + bias[...][None]
+            exps = jnp.exp(scores - jnp.max(scores, axis=-1, keepdims=True))
+            total = jnp.sum(exps, axis=-1, keepdims=True).reshape(GROUP * half_len, 1)
+            mixed = product(exps.astype(low).reshape(GROUP * half_len, wide), value) / total
+            attended_ref[here, at] = unstack_heads(mixed, half_len).astype(low)
+        return carry
+
+    lax.fori_loop(0, 2 * micro, attend_some, 0)
+    outs.forward(3)
+    outs.finish(2)
+    outs.finish(3)
+    dys.forward(0)
+    for k in range(zs):
+        outs.complete(k)
+    out_load = pltpu.make_async_copy(out_all, out_w, sems.at[3])
+    out_load.start()
+    dys.finish(0)
+    out_load.wait()
+    middle = x_ref[...].astype(jnp.float32) + product(attended_ref[...], out_w[...].reshape(D, D))
+    middle_ref[...] = middle
+    ffn_own[...] = (middle * rms_factor(middle) * gains_ref[1:2, :]).astype(low)
+    ffns.launch()
+    ffns.begin(0)
+    dys.complete(0)
+    ffns.forward(0)
+    both_chain.finish()
+    down_chain.finish()
+    both_chain.start(3)
+    down_chain.start(3)
+    ffns.finish(0)
+    ffns.complete(0)
+    both_chain.finish()
+    down_chain.finish()
+    exchange.end()
+    for one in (weights, outs, pairs, dys, ffns):
+        one.end()
+
+
+def forward(order, first, tokens, pack, both, down, w_out, dy, zs, collective_id):
+    many = tokens.shape[0]
+    micro = first.shape[0]
+    seq = 2 * zs
+    wide = seq * (many // micro) // 2
+    low, full = jnp.bfloat16, jnp.float32
+    places = (order[:, None] * (many // micro // 2) + jnp.arange(many // micro // 2, dtype=jnp.int32)).reshape(1, 2 * wide)
+    freq = 10000.0 ** (-(jnp.arange(128, dtype=jnp.int32) % (HEAD_DIM // 2)).astype(full) / (HEAD_DIM // 2))
+    anywhere, here, smem = (pl.BlockSpec(memory_space=m) for m in (pl.ANY, pltpu.VMEM, pltpu.SMEM))
+    shape = jax.ShapeDtypeStruct
+    out_any = [
+        shape((zs, 2, 4) + pack.shape, low),
+        shape(both.shape, low),
+        shape((zs, 2, many, 2 * KVW), low),
+        shape((zs, 2, 4) + w_out.shape, low),
+        shape((2, 4) + dy.shape, low),
+        shape((2, 4, many, D), low),
+    ] + [shape(both.shape, low)] * (2 * zs - 2) + [shape(down.shape, low)] * (2 * zs - 2)
+    out_here = [shape((many, D), t) for t in (low, low, low, full)] + [shape((8, D), full)] + [shape((many, 128), full)] * 2
+    sem = pltpu.SemaphoreType.DMA
+    found = pl.pallas_call(
+        functools.partial(forward_kernel, zs, micro),
+        out_shape=out_any + out_here,
+        in_specs=[smem, here, smem] + [here] * 2 + [anywhere] * 5,
+        out_specs=[anywhere] * len(out_any) + [here] * len(out_here),
+        scratch_shapes=[
+            pltpu.VMEM((2, 2, 4) + pack.shape, low),
+            pltpu.VMEM((many, QKV), full),
+            pltpu.VMEM((many, 2 * KVW), low),
+            pltpu.VMEM((zs, 2, many, 2 * KVW), low),
+            pltpu.VMEM((wide, 2 * KVW), low),
+            pltpu.VMEM((many // micro // 2, wide), full),
+            pltpu.VMEM((zs, 2, 4) + w_out.shape, low),
+            pltpu.VMEM((many, D), low),
+            sem((4,)),
+        ] + EXCHANGE_SEMS + [sem((2 * zs - 2, 2))] * 2 + gather_sems(zs, True) * 3 + gather_sems(zs, False) * 2,
+        compiler_params=pltpu.CompilerParams(
+            collective_id=collective_id, has_side_effects=True, vmem_limit_bytes=56 * MIB
+        ),
+        cost_estimate=LONG,
+    )(order, places, first, freq.reshape(1, 128), tokens, pack, both, down, w_out, dy)
+    return found
+
+
 class Links:
     def __init__(self, seq, rows):
         self.zs, self.rows = seq // 2, rows
@@ -783,9 +981,6 @@
 
     def permute(self, lines):
         return [lax.ppermute(array, "seq", self.along(way, lo, hi)) for array, way, lo, hi in lines]
-
-    def gather_lines(self, k, up, down):
-        return [(up, 1, k - 1, self.zs), (down, -1, 0, self.zs - k + 1)]
 
     def part(self, blocks, to, held):
         z = lax.div(lax.axis_index("seq"), 2)
@@ -816,16 +1011,11 @@
             return arrays
         return lax.optimization_barrier((*arrays, *others))[: len(arrays)]
 
-    def gather(self, arrays, flags, collective_id, moved=(), lines=()):
-        if self.kernels:
-            return gather(arrays, flags, self.zs, collective_id, moved, lines)
-        results = []
-        for array, (z_flag, planes) in zip(arrays, flags):
-            if planes:
-                array = lax.all_gather(array, "rows", axis=0)
-            array = lax.all_gather(array, "seq", axis=0, axis_index_groups=self.core_groups)
-            results.append(self.gather_z(array[None]) if z_flag else array)
-        return results + [self.exchange_xla(blocks) for blocks in moved] + [line[0] for line in lines]
+    def gather(self, array, z_flag, planes):
+        if planes:
+            array = lax.all_gather(array, "rows", axis=0)
+        array = lax.all_gather(array, "seq", axis=0, axis_index_groups=self.core_groups)
+        return self.gather_z(array[None]) if z_flag else array
 
     def scatter(self, arrays, flags, collective_id, moved=(), lines=()):
         if self.kernels:
@@ -856,70 +1046,49 @@
     wide = w_gate.shape[0]
     unit = w_down.shape[0]
 
-    chained = links.kernels
     both = spread(w_gate, w_up, zs, rows)
+    flat = (2 * rows * wide, 2 * zs * unit)
     gains = jnp.pad(jnp.stack([gain_attn, gain_ffn], axis=1), ((0, 0), (0, 126)))
     pack = jnp.concatenate([w_query, w_key, w_value, gains], axis=1)
-    lines = [(1, 1, 0, zs), (1, -1, 0, zs)] if chained else []
-    packed, both_own, *both_got = links.gather([pack], [(True, True)], 0, [both], lines)
-    flat = (2 * rows * wide, 2 * zs * unit)
-    both_own = both_own.reshape(flat)
-    both_w, down_w = [both_own], [w_down]
+    dy_own = cotangent.reshape(many, D)
+    own_tokens = tokens.reshape(many, D)
+    x = own_tokens.astype(jnp.float32)
+    factor_one = rms_factor(x)
+    first = lengths[:, 0, 0]
+    slot_of = jnp.argmax(order[None, :] == jnp.arange(order.shape[0], dtype=jnp.int32)[:, None], axis=1).astype(jnp.int32)
+    chained = links.kernels
     if chained:
-        both_w += [None] * (2 * zs - 2)
-        down_w += [None] * (2 * zs - 2)
-        both_w[1], both_w[zs] = (b.reshape(flat) for b in both_got)
-        down_w[1], down_w[zs] = links.permute(links.gather_lines(1, *links.tie([w_down, w_down], packed)))
+        found = forward(order, first, own_tokens, pack, both, w_down, w_out, dy_own, zs, 0)
+        packed, both_own, kv, out_w, dy, ffn_in = found[:6]
+        both_w = [b.reshape(flat) for b in (both_own, *found[6 : 4 + 2 * zs])]
+        down_w = [w_down, *found[4 + 2 * zs : 2 + 4 * zs]]
+        queries, attn_in, attended, middle, gains, cosine, sine = found[2 + 4 * zs :]
+        packed = packed.reshape(D, PACK)
+        gain_one, gain_two = gains[0], gains[1]
     else:
-        both_w, down_w = [links.gather_z(both_own)], [links.gather_z(w_down)]
-    packed = packed.reshape(D, PACK)
-    gain_one = packed[:, QKV].astype(jnp.float32)
-    gain_two = packed[:, QKV + 1].astype(jnp.float32)
-    dy_own = cotangent.reshape(many, D)
-
-    mine = slot_places(order, half_len, lax.axis_index("seq") * span + jnp.arange(span, dtype=jnp.int32))
-    first = lengths[:, 0, 0]
-    start = jnp.where(mine[None, :] >= first[:, None], first[:, None], 0)
-    inverse = 10000.0 ** (-jnp.arange(HEAD_DIM // 2, dtype=jnp.float32) / (HEAD_DIM // 2))
-    angles = ((mine[None, :] - start).astype(jnp.float32)[..., None] * inverse).reshape(many, HEAD_DIM // 2)
-    cosine, sine = jnp.cos(angles), jnp.sin(angles)
-    cosine = jnp.tile(cosine, (1, 2 * GROUP))
-    sine = jnp.tile(jnp.concatenate([-sine, sine], axis=1), (1, GROUP))
-    slot_of = jnp.argmax(order[None, :] == jnp.arange(order.shape[0], dtype=jnp.int32)[:, None], axis=1).astype(jnp.int32)
-
-    def turn(tensor, sign):
-        swapped = jnp.flip(tensor.reshape(many, KV_HEADS, 2, HEAD_DIM // 2), axis=2).reshape(many, KVW)
-        return tensor * cosine[:, :KVW] + sign * swapped * sine[:, :KVW]
-
-    x = tokens.reshape(many, D).astype(jnp.float32)
-    factor_one = rms_factor(x)
-    attn_in = (x * factor_one * gain_one).astype(low)
-    lin = product(attn_in, packed)
-    kv_own = jnp.concatenate([turn(lin[:, D : D + KVW], 1.0), lin[:, D + KVW : QKV]], axis=1).astype(low)
-    lines = []
-    if chained:
-        (kv_own,) = links.tie([kv_own], down_w[1], down_w[zs])
-        lines = links.gather_lines(2, both_w[1], both_w[zs])
-    kv, out_w, dy, *got = links.gather([kv_own, w_out, dy_own], [(True, False), (True, True), (False, True)], 1, (), lines)
+        both_w = [links.gather_z(links.exchange_xla(both).reshape(flat))]
+        down_w = [links.gather_z(w_down)]
+        packed, dy = links.gather(pack, True, True).reshape(D, PACK), links.gather(dy_own, False, True)
+        gain_one, gain_two = packed[:, QKV].astype(jnp.float32), packed[:, QKV + 1].astype(jnp.float32)
+        mine = slot_places(order, half_len, lax.axis_index("seq") * span + jnp.arange(span, dtype=jnp.int32))
+        start = jnp.where(mine[None, :] >= first[:, None], first[:, None], 0)
+        inverse = 10000.0 ** (-jnp.arange(HEAD_DIM // 2, dtype=jnp.float32) / (HEAD_DIM // 2))
+        angles = ((mine[None, :] - start).astype(jnp.float32)[..., None] * inverse).reshape(many, HEAD_DIM // 2)
+        cosine, sine = jnp.cos(angles), jnp.sin(angles)
+        cosine, sine = jnp.tile(cosine, (1, 4)), jnp.tile(jnp.concatenate([-sine, sine], axis=1), (1, 2))
+        attn_in = (x * factor_one * gain_one).astype(low)
+        lin = product(attn_in, packed)
+        kv_own = jnp.concatenate([turn(lin[:, D : D + KVW], cosine, sine), lin[:, D + KVW : QKV]], axis=1).astype(low)
+        kv, out_w = links.gather(kv_own, True, False), links.gather(w_out, True, True)
+        queries, attended = attend(order, slot_of, first, lin, cosine, sine, kv.reshape(seq, many, 2 * KVW))
+        middle = x + product(attended, out_w.reshape(D, D))
+        ffn_in = links.gather((middle * rms_factor(middle) * gain_two).astype(low), False, True)
     kv = kv.reshape(seq, many, 2 * KVW)
     out_w = out_w.reshape(D, D)
     dy = dy.reshape(2 * rows * many, D)
-    if chained:
-        both_w[2], both_w[zs + 1] = got
-        down_w[2], down_w[zs + 1] = links.permute(links.gather_lines(2, *links.tie([down_w[1], down_w[zs]], kv)))
-    queries, attended = attend(order, slot_of, first, lin, cosine, sine, kv)
-    middle = x + product(attended, out_w)
     factor_two = rms_factor(middle)
     normed_two = middle * factor_two
-    ffn_own = (normed_two * gain_two).astype(low)
-
-    lines = []
-    if chained:
-        (ffn_own,) = links.tie([ffn_own], down_w[2], down_w[zs + 1])
-        lines = links.gather_lines(3, both_w[2], both_w[zs + 1]) + links.gather_lines(3, down_w[2], down_w[zs + 1])
-    ffn_in, *got = links.gather([ffn_own], [(False, True)], 2, (), lines)
-    if chained:
-        both_w[3], both_w[zs + 2], down_w[3], down_w[zs + 2] = got
+
     ffn_in = ffn_in.reshape(2 * rows * many, D)
     result_part, d_ffn_part, grad_both, grad_down = feed_forward(ffn_in, dy, both_w, down_w, zs)
     grad_both = grad_both.reshape(zs, *flat)
@@ -963,7 +1132,7 @@
         grad_both, grad_down = links.scatter_z(grad_both)[0], links.scatter_z(grad_down)[0]
         down_lines = []
     result = (middle + result_sum).astype(low)
-    d_key = turn(d_kv[:, :KVW], -1.0)
+    d_key = turn(d_kv[:, :KVW], cosine, -sine)
     d_kv = jnp.concatenate([d_key.astype(low), d_kv[:, KVW:].astype(low)], axis=1)
     d_attn_in = product_nt(d_query, packed[:, :D]) + product_nt(d_kv, packed[:, D:QKV])
     d_x, grad_gain_one = norm_back(d_attn_in, x * factor_one, factor_one, gain_one)

time: 690 us -> 645 us (0.935)
  waiting for transfers between devices: 17.7 us -> 0.56 us
  matrix products: 40.9 us -> 26.9 us
  Pallas kernels: 537 us -> 551 us
  starting transfers between devices: 22.1 us -> 9.72 us
    ppermute x8 -> x4, waiting for transfers between devices: 17.7 us -> 0.56 us  [permute(): lax.ppermute(array, 'seq', self.along(way, lo, hi))]
    dot_general x2 -> x0, matrix products: 14.7 us -> none  [product(): return jnp.dot(left, right, preferred_element_type=jnp.float32)]
    ppermute x8 -> x4, starting transfers between devices: 22.1 us -> 9.72 us  [permute(): lax.ppermute(array, 'seq', self.along(way, lo, hi))]
    pallas_call x1, Pallas kernels: 74.9 us -> 86.1 us  [feed_forward(): pl.pallas_call(functools.partial(ffn_kernel, zs, len(both_pieces)), grid=...]
    pallas_call x4 -> x1, Pallas kernels: 226 us -> 230 us  [forward(): pl.pallas_call(functools.partial(forward_kernel, zs, micro), out_shape=ou...]
  transfers between devices with their start and end apart: 8 -> 4, of which waited for: 4 -> 1; matrix products, arithmetic and copies ran while one was open for 6% -> 3% of each run, Pallas kernels for 3% -> 3%
where the time goes in v3:
time: 645 us; the launch traced here: 639 us
  Pallas kernels  551 us (85%)
  other arithmetic  28.8 us (4%)
  matrix products  26.9 us (4%)
  local copies, waits for them, and re-layouts  21.4 us (3%)
  starting transfers between devices  9.72 us (2%)
    pallas_call x1, Pallas kernels, forward(): pl.pallas_call(functools.partial(forward_kernel, zs, micro), out_shape=ou...  230 us
    pallas_call x3, Pallas kernels, scatter(): pl.pallas_call(functools.partial(scatter_kernel, all_zs, tuple(flags), le...  205 us
    pallas_call x1, Pallas kernels, feed_forward(): pl.pallas_call(functools.partial(ffn_kernel, zs, len(both_pieces)), grid=...  86.1 us
    pallas_call x1, Pallas kernels, attend_back(): pl.pallas_call(attend_back_kernel, grid_spec=pltpu.PrefetchScalarGridSpec...  22.3 us
    dot_general x3, matrix products, product_tn(): lax.dot_general(left, right, (((0,), (0,)), ((), ())), preferred_element_...  13.4 us
    dot_general x3, matrix products, product_nt(): lax.dot_general(left, right, (((1,), (1,)), ((), ())), preferred_element_...  13.4 us
    unnamed x65, local copies, waits for them, and re-layouts  13 us
  transfers between devices with their start and end apart: 4, of which 1 were waited for; matrix products, arithmetic and copies ran while one was open for 3% of the time, Pallas kernels for 3%

profile of v3, /device:TPU:8, one launch (start us, length us, event | category | flops | bytes accessed | tf_op | source)
XLA Modules:
  0.0 639.3 jit_solution(1118086495933782555)
XLA Ops:
  1.2 1.3 slice_reduce_fusion.2.refs_2_.first_ref
  4.7 3.1 shard_map.212.refs_6_
  8.6 230.4 %shard_map.213 = (bf16[4,2,4,64,2688]{4,3,2,1,0:T(8,128)(2,1)}, bf16[2,4,64,1408]{3,2,1,0:T(8,128)(2,1)}, bf16[4,2,256,512]{3,2,1,0:T(8,128)(2,1)}, bf16[4,2,4,6...) custom-call(s32[16]{0:T(128)} %order_ref.1, ...), custom_call_target="tpu_custom_call" | custom-call | flops 49999998976 | bytes 157286400 | tf_op jit(solution)/shard_map/pallas_call | solution.py:938
  238.9 86.1 %shard_map.214 = (bf16[2048,2048]{1,0:T(8,128)(2,1)}, bf16[2048,2048]{1,0:T(8,128)(2,1)}, bf16[2048,1408]{1,0:T(8,128)(2,1)}, bf16[704,2048]{1,0:T(8,128)(2,1)}) custom-call(bf16[2048,2048]{1,0:T(8,128)(2,1)} %bitcast.135, bf16[2048,2048]{1,0:T(8,128)(2,1)} %bitcast.134, bf16[512,1408]{1,0:T(8,128)(2,1)} %bitcast.138, bf16[512,1408]{1,0:T(8,128)(2,1)} %bitcast.139, ...), custom_call_target="tpu_custom_call" | custom-call | flops 53150220288 | bytes 62914560 | tf_op jit(solution)/shard_map/pallas_call | solution.py:686
  325.0 2.2 dynamic-slice_bitcast_fusion
  327.7 1.3 dynamic-slice_bitcast_fusion.2
  329.0 1.1 copy-done.1
  330.1 1.1 copy-done.2
  331.2 3.4 copy-done.3
  334.6 51.0 %shard_map.215 = (f32[256,2048]{1,0:T(8,128)S(1)}, bf16[512,1408]{1,0:T(8,128)(2,1)S(1)}, bf16[512,1408]{1,0:T(8,128)(2,1)S(1)}, bf16[176,2048]{1,0:T(8,128)(2,1)S(1)}, bf16[176,2048]{1,0:T(8,128)(2,1)S(1)}) custom-call(bf16[2,4,256,2048]{3,2,1,0:T(8,128)(2,1)S(1)} %bitcast.99, bf16[512,1408]{1,0:T(8,128)(2,1)S(1)} %get-tuple-element.176.refs_1_, ...), custom_call_target="tpu_custom_call" | custom-call | flops 49999998976 | bytes 157286400 | tf_op jit(solution)/shard_map/pallas_call | solution.py:432
  385.6 1.6 fusion.16
  387.3 2.6 collective-permute-start.2
  389.9 1.3 collective-permute-start.3
  391.2 4.4 fusion.6
  395.6 4.5 collective-permute-start
  400.2 1.3 collective-permute-start.1
  405.1 3.3 convolution_convert_fusion.3.d_ref
  409.9 22.3 %shard_map.216 = (bf16[256,2048]{1,0:T(8,128)(2,1)}, bf16[8,256,512]{2,1,0:T(8,128)(2,1)}) custom-call(s32[16]{0:T(128)} %order_ref.1, s32[16]{0:T(128)} %get-tuple-element.67.inverse_ref, s32[2]{0:T(128)} %slice_reduce_fusion.2.refs_2_.first_ref, bf16[256,2048]{1,0:T(8,128)(2,1)} %get-tuple-element.68.q_ref, ...), custom_call_target="tpu_custom_call" | custom-call | flops 5368709120 | bytes 25165824 | tf_op jit(solution)/shard_map/pallas_call | solution.py:591
  432.3 5.8 convolution_convert_fusion.1
  438.6 5.7 convolution_convert_fusion
  444.3 4.2 fusion.4
  448.5 118.4 %shard_map.217 = (f32[256,512]{1,0:T(8,128)S(1)}, f32[64,2048]{1,0:T(8,128)S(1)}, f32[64,2048]{1,0:T(8,128)S(1)}, f32[256,2048]{1,0:T(8,128)}, bf16[512,1408]{1,0:T(8,128)(2,1)}, /*index=5*/bf16[512,1408]{1,0:T(8,128)(2,1)}) custom-call(bf16[4,2,256,512]{3,2,1,0:T(8,128)(2,1)} %bitcast.137, bf16[4,2,4,64,2048]{4,3,2,1,0:T(8,128)(2,1)} %bitcast.106, ...), custom_call_target="tpu_custom_call" | custom-call | flops 49999998976 | bytes 157286400 | tf_op jit(solution)/shard_map/pallas_call | solution.py:432
  568.0 2.0 convolution_convert_fusion.2
  570.0 2.5 fusion.11
  572.5 7.6 %multiply_reduce_fusion.1 = (bf16[2048]{0:T(1024)(128)(2,1)S(1)}, f32[256]{0:T(256)S(1)}, f32[256,2048]{1,0:T(8,128)}) fusion(f32[256]{0:T(256)S(1)} %rsqrt_bitcast_fusion, bf16[2,1,128,2048]{3,2,1,0:T(8,128)(2,1)S(1)} %copy-done.11, f32[2048]{0:T(1024)S(1)} %bitcast.126, f32[256,2048]{1,0:T(8,128)S(1)} %fusion.11, bf16[256,2048]{1,0:T(8,128)(2,1)S(1)} %copy-done.20, ...), kind=kOutput, calls=%fused_computation.22 | convolution fusion | flops 2151675648 | bytes 14694400 | tf_op jit(solution)/shard_map/dot_general | solution.py:31
  581.3 2.5 fusion.14
  585.6 2.1 fusion.3
  587.7 36.0 %shard_map.218 = (f32[64,640]{1,0:T(8,128)S(1)}, bf16[2,4,64,1408]{3,2,1,0:T(8,128)(2,1)S(1)}, bf16[176,2048]{1,0:T(8,128)(2,1)S(1)}, bf16[176,2048]{1,0:T(8,128)(2,1)S(1)}) custom-call(bf16[4,2,4,64,640]{4,3,2,1,0:T(8,128)(2,1)S(1)} %pad_maximum_fusion.refs_0_, bf16[2,4,64,1408]{3,2,1,0:T(8,128)(2,1)S(1)} %bitcast.98, ...), custom_call_target="tpu_custom_call" | custom-call | flops 49999998976 | bytes 157286400 | tf_op jit(solution)/shard_map/pallas_call | solution.py:432
  626.2 3.3 shard_map.219
  629.5 3.6 add_convert_fusion.1
  633.1 2.7 fusion.13
  635.9 1.6 add_convert_fusion
  (101 shorter events, 17.6 us)
Async XLA Ops:
  0.6 7.2 %copy-start.21 = (bf16[64,2048]{1,0:T(8,128)(2,1)S(1)}, bf16[64,2048]{1,0:T(8,128)(2,1)}, u32[]{:S(2)}) copy-start(bf16[64,2048]{1,0:T(8,128)(2,1)} %param.14) | copy-start | bytes 786436
  0.7 7.2 %copy-start.25 = (bf16[64,256]{1,0:T(8,128)(2,1)S(1)}, bf16[64,256]{1,0:T(8,128)(2,1)}, u32[]{:S(2)}) copy-start(bf16[64,256]{1,0:T(8,128)(2,1)} %param.15) | copy-start | bytes 98308
  0.7 7.1 %copy-start.24 = (bf16[64,256]{1,0:T(8,128)(2,1)S(1)}, bf16[64,256]{1,0:T(8,128)(2,1)}, u32[]{:S(2)}) copy-start(bf16[64,256]{1,0:T(8,128)(2,1)} %param.16) | copy-start | bytes 98308
  325.0 2.7 copy-start.7
  329.0 1.1 copy-start.1
  331.2 3.4 copy-start.3
  334.6 51.0 %copy-start.8 = (bf16[704,2048]{1,0:T(8,128)(2,1)S(1)}, bf16[704,2048]{1,0:T(8,128)(2,1)}, u32[]{:S(2)}) copy-start(bf16[704,2048]{1,0:T(8,128)(2,1)} %get-tuple-element.86) | copy-start | bytes 8650756
  387.3 50.8 %collective-permute-start.2 = (bf16[176,2048]{1,0:T(8,128)(2,1)}, bf16[176,2048]{1,0:T(8,128)(2,1)}, u32[]{:S(2)}, u32[]{:S(2)}) collective-permute-start(bf16[176,2048]{1,0:T(8,128)(2,1)} %get-tuple-element.180), channel_id=1, source_target_pairs={{0,8},{4,12},{8,16},{12,20},{1,9},{5,13},{9,17},{13,21},{2,10},{6,... | collective-permute-start | bytes 2162696 | tf_op jit(solution)/shard_map/ppermute | solution.py:983
  389.9 48.2 %collective-permute-start.3 = (bf16[176,2048]{1,0:T(8,128)(2,1)}, bf16[176,2048]{1,0:T(8,128)(2,1)}, u32[]{:S(2)}, u32[]{:S(2)}) collective-permute-start(bf16[176,2048]{1,0:T(8,128)(2,1)} %get-tuple-element.179), channel_id=1, source_target_pairs={{16,8},{20,12},{24,16},{28,20},{17,9},{21,13},{25,17},{29,21},{18,... | collective-permute-start | bytes 2162696 | tf_op jit(solution)/shard_map/ppermute | solution.py:983
  391.2 10.3 %copy-start.4 = (f32[256,2048]{1,0:T(8,128)S(1)}, f32[256,2048]{1,0:T(8,128)}, u32[]{:S(2)}) copy-start(f32[256,2048]{1,0:T(8,128)} %get-tuple-element.66) | copy-start | bytes 6291460
  391.2 13.4 %slice-start.2 = ((s8[8388608]{0:T(1024)(128)(4,1)}), s8[4194304]{0:T(1024)(128)(4,1)S(1)}, s32[]{:S(2)}) async-start(s8[8388608]{0:T(1024)(128)(4,1)} %bitcast.131), calls=%async_computation.2 | async-start | bytes 8388608
  395.6 42.4 %collective-permute-start = (bf16[512,1408]{1,0:T(8,128)(2,1)}, bf16[512,1408]{1,0:T(8,128)(2,1)}, u32[]{:S(2)}, u32[]{:S(2)}) collective-permute-start(bf16[512,1408]{1,0:T(8,128)(2,1)} %get-tuple-element.174), channel_id=1, source_target_pairs={{0,8},{4,12},{8,16},{12,20},{1,9},{5,13},{9,17},{13,21},{2,10},{6,... | collective-permute-start | bytes 4325384 | tf_op jit(solution)/shard_map/ppermute | solution.py:983
  400.2 38.5 %collective-permute-start.1 = (bf16[512,1408]{1,0:T(8,128)(2,1)}, bf16[512,1408]{1,0:T(8,128)(2,1)}, u32[]{:S(2)}, u32[]{:S(2)}) collective-permute-start(bf16[512,1408]{1,0:T(8,128)(2,1)} %get-tuple-element.173), channel_id=1, source_target_pairs={{16,8},{20,12},{24,16},{28,20},{17,9},{21,13},{25,17},{29,21},{18,... | collective-permute-start | bytes 4325384 | tf_op jit(solution)/shard_map/ppermute | solution.py:983
  402.6 1.2 copy-start.18
  402.6 2.5 slice-start.3
  404.5 27.7 %copy-start.5 = (f32[256,2048]{1,0:T(8,128)}, f32[256,2048]{1,0:T(8,128)S(1)}, u32[]{:S(2)}) copy-start(f32[256,2048]{1,0:T(8,128)S(1)} %multiply_add_fusion) | copy-start | bytes 6291460
  405.1 3.4 copy-start.26
  405.1 4.4 copy-start.23
  405.1 4.4 copy-start.10
  409.9 22.4 %copy-start.15 = (bf16[256,2048]{1,0:T(8,128)(2,1)S(1)}, bf16[256,2048]{1,0:T(8,128)(2,1)}, u32[]{:S(2)}) copy-start(bf16[256,2048]{1,0:T(8,128)(2,1)} %get-tuple-element.100) | copy-start | bytes 3145732
  409.9 34.4 %slice-start = ((s8[5767168]{0:T(1024)(128)(4,1)}), s8[1572864]{0:T(1024)(128)(4,1)S(1)}, s32[]{:S(2)}) async-start(s8[5767168]{0:T(1024)(128)(4,1)} %bitcast.103), calls=%async_computation | async-start | bytes 3145728
  432.2 6.4 copy-start.9
  432.2 6.4 copy-start.19
  432.2 12.1 %slice-start.1 = ((s8[5767168]{0:T(1024)(128)(4,1)}), s8[4194304]{0:T(1024)(128)(4,1)S(1)}, s32[]{:S(2)}) async-start(s8[5767168]{0:T(1024)(128)(4,1)} %bitcast.103), calls=%async_computation.1 | async-start | bytes 8388608
  570.0 2.5 copy-start.11
  570.0 2.5 copy-start.20
  581.3 2.5 copy-start.14
  583.8 1.4 copy-start.16
  583.9 1.8 copy-start.17
  629.5 6.3 copy-start.13
  633.1 2.7 copy-start.6
  633.1 2.7 copy-start.12
  (3 other events, 3.1 us)

commit v4 on v3

--- a/solution.py
+++ b/solution.py
@@ -258,19 +258,21 @@
 
 
 class Scatter:
-    def __init__(self, zs, z_flag, planes, given, out, own, twin_in, half_in, full_in, z_in, l_sem, c_ssem, c_rsem, h_ssem, h_rsem,
-                 f_ssem, f_rsem, z_ssem, z_rsem):
+    def __init__(self, zs, z_flag, planes, given, final, stage, twin_in, half_in, full_in, z_in, l_sem, c_ssem, c_rsem, h_ssem,
+                 h_rsem, f_ssem, f_rsem, z_ssem, z_rsem):
         self.__dict__.update(locals())
         self.z, self.c, self.r = place()
         self.line = corners(self.r)
         self.s = self.z * 2 + self.c
         self.twin = (self.z * 2 + 1 - self.c, self.r)
-        self.rows = out.shape[0]
+        self.rows = twin_in.shape[2]
         self.step = 16
         self.spots = (3, 1, 2, 0) if planes else (0,)
         self.zs = zs if z_flag else 1
         self.order = list(range(1, self.zs)) + [0]
         self.pending = []
+        self.loads = []
+        self.settled = 0
 
     def at_z(self, k):
         return (lax.rem(self.z + k, self.zs) * 2 + self.c, self.r)
@@ -285,36 +287,48 @@
         copy.start()
         self.pending.append(copy.wait_send)
 
-    def local(self, k, j):
-        return pltpu.make_async_copy(self.block(k, 0, j), self.own.at[k, j], self.l_sem.at[k, j])
-
-    def begin(self):
+    def begin(self, schedule):
         for k in self.order:
             for j in self.spots:
-                block = self.block(k, 1, j)
-                self.start(send(block, self.twin_in.at[k, j], self.c_ssem.at[k, j], self.c_rsem.at[k, j], self.twin))
-                self.local(k, j).start()
-
-    def settle(self, k, j):
-        self.local(k, j).wait()
-        send(self.own.at[k, j], self.twin_in.at[k, j], self.c_ssem.at[k, j], self.c_rsem.at[k, j], self.twin).wait_recv()
-
-    def add(self, first, last, k, j, *more, final=False):
+                self.start(self.twin_copy(k, j, self.block(k, 1, j)))
+        if self.stage is not None:
+            self.loads = [
+                pltpu.make_async_copy(self.block(k, 0, j), self.stage.at[n % 2], self.l_sem.at[n % 2])
+                for n, (k, j) in enumerate(schedule)
+            ]
+            for load in self.loads[:2]:
+                load.start()
+
+    def twin_copy(self, k, j, src):
+        dst = self.twin_in.at[k, j]
+        return send(dst if src is None else src, dst, self.c_ssem.at[k, j], self.c_rsem.at[k, j], self.twin)
+
+    def settle(self, k, j, parts):
+        own = self.block(k, 0, j)
+        n = self.settled
+        if self.stage is not None:
+            self.loads[n].wait()
+            own = self.stage.at[n % 2]
+        self.twin_copy(k, j, None).wait_recv()
         step = self.step
-
-        def body(n, carry):
-            at = pl.ds(pl.multiple_of(first + n * step, step), step)
-            value = self.own[k, j, at, :].astype(jnp.float32) + self.twin_in[k, j, at, :].astype(jnp.float32)
-            for ref, offset in more:
-                there = pl.ds(pl.multiple_of(first - offset + n * step, step), step)
-                value = value + ref[there, :].astype(jnp.float32)
-            if final:
-                self.out[at, :] = value
-            else:
-                self.own[k, j, at, :] = value.astype(self.own.dtype)
-            return carry
-
-        lax.fori_loop(0, (last - first) // step, body, 0)
+        for first, last, more in parts:
+
+            def body(i, carry, first=first, more=more):
+                at = pl.ds(pl.multiple_of(first + i * step, step), step)
+                value = own[at, :].astype(jnp.float32) + self.twin_in[k, j, at, :].astype(jnp.float32)
+                for ref, offset in more:
+                    there = pl.ds(pl.multiple_of(first - offset + i * step, step), step)
+                    value = value + ref[there, :].astype(jnp.float32)
+                if k == 0 and j == 0:
+                    self.final(at, value)
+                else:
+                    self.twin_in[k, j, at, :] = value.astype(self.twin_in.dtype)
+                return carry
+
+            lax.fori_loop(0, (last - first) // step, body, 0)
+        if n + 2 < len(self.loads):
+            self.loads[n + 2].start()
+        self.settled = n + 1
 
     def half_copy(self, k, n, src):
         dst = self.half_in.at[k, n]
@@ -330,116 +344,132 @@
 
     def stage_a(self, k):
         half = self.rows // 2
-        self.settle(k, 3)
-        self.add(0, self.rows, k, 3)
-        self.start(self.half_copy(k, 1, self.own.at[k, 3, pl.ds(half, half)]))
-        self.start(self.half_copy(k, 0, self.own.at[k, 3, pl.ds(0, half)]))
+        self.settle(k, 3, [(0, self.rows, [])])
+        self.start(self.half_copy(k, 1, self.twin_in.at[k, 3, pl.ds(half, half)]))
+        self.start(self.half_copy(k, 0, self.twin_in.at[k, 3, pl.ds(0, half)]))
 
     def stage_b(self, k):
         half = self.rows // 2
         for j in (1, 2):
-            self.settle(k, j)
             n = 2 - j
             self.half_copy(k, n, None).wait_recv()
-            more = (self.half_in.at[k, n], half if n else 0)
-            self.add(0, half, k, j, *([] if n else [more]))
-            self.add(half, self.rows, k, j, *([more] if n else []))
-            self.start(self.full_copy(k, j, self.own.at[k, j]))
+            more = [(self.half_in.at[k, n], half if n else 0)]
+            self.settle(k, j, [(0, half, [] if n else more), (half, self.rows, more if n else [])])
+            self.start(self.full_copy(k, j, self.twin_in.at[k, j]))
 
     def stage_c(self, k):
-        self.settle(k, 0)
         more = []
         if self.planes:
             for j in (1, 2):
                 self.full_copy(k, j, None).wait_recv()
                 more.append((self.full_in.at[k, j - 1], 0))
+        if not k:
+            for other in range(1, self.zs):
+                self.z_copy(other, None).wait_recv()
+                more.append((self.z_in.at[other], 0))
+        self.settle(k, 0, [(0, self.rows, more)])
         if k:
-            self.add(0, self.rows, k, 0, *more)
-            self.start(self.z_copy(k, self.own.at[k, 0]))
-            return
-        for k2 in range(1, self.zs):
-            self.z_copy(k2, None).wait_recv()
-            more.append((self.z_in.at[k2], 0))
-        self.add(0, self.rows, 0, 0, *more, final=True)
+            self.start(self.z_copy(k, self.twin_in.at[k, 0]))
 
     def end(self):
         for wait in self.pending:
             wait()
 
 
+def scatter_scratch(zs, planes, rows, columns, staged):
+    sem = pltpu.SemaphoreType.DMA
+    low, least = jnp.bfloat16, (1, 2, 16, 128)
+    spots = 4 if planes else 1
+    return [
+        pltpu.VMEM((2, rows, columns) if staged else (16, 128), low),
+        pltpu.VMEM((zs, spots, rows, columns), low),
+        pltpu.VMEM((zs, 2, rows // 2, columns) if planes else least, low),
+        pltpu.VMEM((zs, 2, rows, columns) if planes else least, low),
+        pltpu.VMEM((zs, rows, columns) if zs > 1 else least[1:], low),
+        sem((2,)), sem((zs, 4)), sem((zs, 4)), sem((zs, 2)), sem((zs, 2)), sem((zs, 2)), sem((zs, 2)), sem((zs,)), sem((zs,)),
+    ]
+
+
 SCATTER_REFS = 14
 
 
-def scatter_kernel(zs, flags, moves, lines, *refs):
-    count, taken = len(flags), len(flags) + moves + len(lines)
-    given, moved, line_own = refs[:count], refs[count : count + moves], refs[count + moves : taken]
-    out, rest = refs[taken : taken + count], refs[taken + count :]
-    moved_out, line_out, rest = rest[:moves], rest[moves : moves + len(lines)], rest[moves + len(lines) :]
-    reach = zs if lines or any(flag[0] for flag in flags) else 1
-    greet(neighbours(reach, any(flag[1] for flag in flags), moves))
-    sums = [
-        Scatter(zs, *flags[a], given[a], out[a], *rest[SCATTER_REFS * a : SCATTER_REFS * (a + 1)]) for a in range(count)
-    ]
-    rest = rest[SCATTER_REFS * count :]
-    exchanges = [Exchange(moved[n], moved_out[n], *rest[3 * n : 3 * n + 3]) for n in range(moves)]
-    rest = rest[3 * moves :]
-    going = [Line(zs, *line, line_own[n], line_out[n], rest[n]) for n, line in enumerate(lines)]
-    for one in sums:
-        one.begin()
-    for one in exchanges:
-        one.start()
-    for one in going:
-        one.start()
-    for one in sums:
-        if not one.planes:
-            for k in one.order[:-1]:
-                one.stage_c(k)
-    items = [(one, k) for k in list(range(1, zs)) + [0] for one in sums if one.planes and k < one.zs]
-    total = len(items)
-    for n in range(total + 2):
-        for back, stage in enumerate((Scatter.stage_a, Scatter.stage_b, Scatter.stage_c)):
-            if 0 <= n - back < total and (back < 2 or items[n - back][1]):
-                stage(*items[n - back])
-    for one in sums:
-        one.stage_c(0)
-    for one in exchanges + going:
-        one.finish()
-    for one in exchanges + sums:
-        one.end()
-
-
-def scatter(arrays, flags, zs, collective_id, moved=(), lines=()):
-    sem = pltpu.SemaphoreType.DMA
-    anywhere = pl.BlockSpec(memory_space=pl.ANY)
-    scratch, used, shapes = [], 0, []
-    all_zs = zs
-    for array, (z_flag, planes) in zip(arrays, flags):
-        rows, columns = array.shape[-2:]
-        zs = all_zs if z_flag else 1
-        spots, low = 4 if planes else 1, array.dtype
-        used += rows * columns * 2 * (zs * (2 * spots + (3 if planes else 0) + 1) + 4)
-        shapes.append(jax.ShapeDtypeStruct((rows, columns), jnp.float32))
-        scratch += [
-            pltpu.VMEM((zs, spots, rows, columns), low),
-            pltpu.VMEM((zs, spots, rows, columns), low),
-            pltpu.VMEM((zs, 2, rows // 2, columns) if planes else (1, 2, 16, 128), low),
-            pltpu.VMEM((zs, 2, rows, columns) if planes else (1, 2, 16, 128), low),
-            pltpu.VMEM((zs, rows, columns) if zs > 1 else (1, 16, 128), low),
-            sem((zs, 4)), sem((zs, 4)), sem((zs, 4)), sem((zs, 2)), sem((zs, 2)), sem((zs, 2)), sem((zs, 2)),
-            sem((zs,)), sem((zs,)),
+def scatter_plan(items):
+    rounds = []
+    for n in range(len(items) + 2):
+        rounds.append([])
+        for back, stage in enumerate(("a", "b", "c")):
+            if 0 <= n - back < len(items):
+                name, k = items[n - back]
+                if stage != "c" or k:
+                    rounds[-1].append((name, stage, k))
+    rounds.append([(name, "c", 0) for name, k in items if not k])
+    places = {"a": (3,), "b": (1, 2), "c": (0,)}
+    schedules = {}
+    for name, stage, k in sum(rounds, []):
+        schedules.setdefault(name, []).extend((k, j) for j in places[stage])
+    return rounds, schedules
+
+
+def run_stage(scatters, name, stage, k):
+    {"a": Scatter.stage_a, "b": Scatter.stage_b, "c": Scatter.stage_c}[stage](scatters[name], k)
+
+
+class SumChain:
+    def __init__(self, zs, parts, got, held, sems, l_sem):
+        self.__dict__.update(locals())
+        self.z = place()[0]
+
+    def own(self, to):
+        return self.parts.at[lax.rem(self.z + to + self.zs, self.zs)]
+
+    def fetch(self, k):
+        self.loads = [
+            pltpu.make_async_copy(self.own(-k), self.held.at[0], self.l_sem.at[0]),
+            pltpu.make_async_copy(self.own(k), self.held.at[1], self.l_sem.at[1]),
         ]
-    count = len(arrays)
-    return pl.pallas_call(
-        functools.partial(scatter_kernel, all_zs, tuple(flags), len(moved), tuple(tuple(line[1:]) for line in lines)),
-        out_shape=shapes + [jax.ShapeDtypeStruct(m.shape, m.dtype) for m in (*moved, *[line[0] for line in lines])],
-        in_specs=[anywhere] * (count + len(moved) + len(lines)),
-        out_specs=[pl.BlockSpec(memory_space=pltpu.VMEM)] * count + [anywhere] * (len(moved) + len(lines)),
-        scratch_shapes=scratch + EXCHANGE_SEMS * len(moved) + [LINE_SEMS] * len(lines),
-        compiler_params=pltpu.CompilerParams(
-            collective_id=collective_id, has_side_effects=True, vmem_limit_bytes=used + 6 * MIB
-        ),
-        cost_estimate=LONG,
-    )(*arrays, *moved, *[line[0] for line in lines])
+        for load in self.loads:
+            load.start()
+
+    def add(self, into, more):
+        self.got[into] = (self.got[into].astype(jnp.float32) + self.held[more].astype(jnp.float32)).astype(self.got.dtype)
+
+    def start(self, k):
+        zs, z, got = self.zs, self.z, self.got
+        up, down = k - 1, zs - 2 + k
+        self.lines = [
+            Line(zs, 1, 0, 1, self.own(-k), got.at[up], self.sems.at[up]),
+            Line(zs, -1, zs - 1, zs, self.own(k), got.at[down], self.sems.at[down]),
+        ]
+        if k > 1:
+            for load in self.loads:
+                load.wait()
+            pl.when((z >= 1) & (z < k))(functools.partial(self.add, up - 1, 0))
+            pl.when((z >= zs - k) & (z < zs - 1))(functools.partial(self.add, down - 1, 1))
+            self.lines += [
+                Line(zs, 1, 1, k, got.at[up - 1], got.at[up], self.sems.at[up]),
+                Line(zs, -1, zs - k, zs - 1, got.at[down - 1], got.at[down], self.sems.at[down]),
+            ]
+        for line in self.lines:
+            line.start()
+        if k < zs - 1:
+            self.fetch(k + 1)
+        else:
+            self.loads = [pltpu.make_async_copy(self.own(0), self.held.at[0], self.l_sem.at[0])]
+            self.loads[0].start()
+
+    def finish(self):
+        for line in self.lines:
+            line.finish()
+
+    def total(self):
+        zs, z = self.zs, self.z
+        self.loads[0].wait()
+
+        def add(come):
+            self.held[0] = (self.held[0].astype(jnp.float32) + self.got[come].astype(jnp.float32)).astype(self.held.dtype)
+
+        pl.when(z > 0)(functools.partial(add, zs - 2))
+        pl.when(z < zs - 1)(functools.partial(add, 2 * zs - 3))
 
 
 def partner(tensor):
@@ -503,6 +533,18 @@
         out_ref[:, at] = unstack_heads(mixed, span).astype(jnp.bfloat16)
 
 
+def attend_back_heads(queries, d_heads, key, value, bias, span):
+    query, d_mixed = stack_heads(queries, 0), stack_heads(d_heads, 0)
+    scores = product_nt(key, query) + bias[...]
+    exps = jnp.exp(scores - jnp.max(scores, axis=0, keepdims=True))
+    probs = exps * (1.0 / jnp.sum(exps, axis=0, keepdims=True))
+    weighted = probs * product_nt(value, d_mixed)
+    delta = jnp.sum(weighted, axis=0, keepdims=True)
+    d_scores = (weighted - probs * delta).astype(jnp.bfloat16)
+    d_query = unstack_heads(product_tn(d_scores, key) * HEAD_DIM ** -0.5, span)
+    return product(d_scores, query), product(probs.astype(jnp.bfloat16), d_mixed), d_query
+
+
 def attend_back_kernel(order_ref, inverse_ref, first_ref, q_ref, d_ref, cos_ref, sin_ref, kv_ref, dq_ref, dkv_ref, window, bias, sums):
     span = q_ref.shape[0]
     wide = window.shape[0]
@@ -527,18 +569,9 @@
         at = slice(g * width, (g + 1) * width)
         key = window[:, g * HEAD_DIM : (g + 1) * HEAD_DIM]
         value = window[:, KVW + g * HEAD_DIM : KVW + (g + 1) * HEAD_DIM]
-        query = stack_heads(q_ref[:, at], 0)
-        d_mixed = stack_heads(d_ref[:, at], 0)
-        scores = product_nt(key, query) + bias[...]
-        exps = jnp.exp(scores - jnp.max(scores, axis=0, keepdims=True))
-        probs = exps * (1.0 / jnp.sum(exps, axis=0, keepdims=True))
-        d_probs = product_nt(value, d_mixed)
-        weighted = probs * d_probs
-        delta = jnp.sum(weighted, axis=0, keepdims=True)
-        d_scores = (weighted - probs * delta).astype(jnp.bfloat16)
-        d_keys.append(product(d_scores, query))
-        d_values.append(product(probs.astype(jnp.bfloat16), d_mixed))
-        d_query = unstack_heads(product_tn(d_scores, key) * HEAD_DIM ** -0.5, span)
+        d_key, d_value, d_query = attend_back_heads(q_ref[:, at], d_ref[:, at], key, value, bias, span)
+        d_keys.append(d_key)
+        d_values.append(d_value)
         dq_ref[:, at] = (d_query * cosine - partner(d_query) * sine).astype(jnp.bfloat16)
     d_window = jnp.concatenate(d_keys + d_values, axis=1)
     for n in range(wide // span):
@@ -839,6 +872,10 @@
         q_ref[:, at] = turned(lin[:, at], width).astype(low) * low(HEAD_DIM ** -0.5)
     outs.forward(0)
     outs.begin(2)
+    both_chain.finish()
+    down_chain.finish()
+    both_chain.start(2)
+    down_chain.start(2)
     for k in range(1, zs):
         pairs.begin(k)
     outs.forward(1)
@@ -846,10 +883,6 @@
     outs.begin(3)
     for k in range(zs):
         pairs.complete(k)
-    both_chain.finish()
-    down_chain.finish()
-    both_chain.start(2)
-    down_chain.start(2)
     kv_load = pltpu.make_async_copy(kv_all, kv_here, sems.at[2])
     kv_load.start()
     outs.forward(2)
@@ -900,12 +933,12 @@
     ffn_own[...] = (middle * rms_factor(middle) * gains_ref[1:2, :]).astype(low)
     ffns.launch()
     ffns.begin(0)
-    dys.complete(0)
-    ffns.forward(0)
     both_chain.finish()
     down_chain.finish()
     both_chain.start(3)
     down_chain.start(3)
+    dys.complete(0)
+    ffns.forward(0)
     ffns.finish(0)
     ffns.complete(0)
     both_chain.finish()
@@ -915,13 +948,16 @@
         one.end()
 
 
+def places_of(order, span):
+    return (order[:, None] * (span // 2) + jnp.arange(span // 2, dtype=jnp.int32)).reshape(1, -1)
+
+
 def forward(order, first, tokens, pack, both, down, w_out, dy, zs, collective_id):
     many = tokens.shape[0]
     micro = first.shape[0]
     seq = 2 * zs
     wide = seq * (many // micro) // 2
     low, full = jnp.bfloat16, jnp.float32
-    places = (order[:, None] * (many // micro // 2) + jnp.arange(many // micro // 2, dtype=jnp.int32)).reshape(1, 2 * wide)
     freq = 10000.0 ** (-(jnp.arange(128, dtype=jnp.int32) % (HEAD_DIM // 2)).astype(full) / (HEAD_DIM // 2))
     anywhere, here, smem = (pl.BlockSpec(memory_space=m) for m in (pl.ANY, pltpu.VMEM, pltpu.SMEM))
     shape = jax.ShapeDtypeStruct
@@ -955,8 +991,292 @@
             collective_id=collective_id, has_side_effects=True, vmem_limit_bytes=56 * MIB
         ),
         cost_estimate=LONG,
-    )(order, places, first, freq.reshape(1, 128), tokens, pack, both, down, w_out, dy)
+    )(order, places_of(order, many // micro), first, freq.reshape(1, 128), tokens, pack, both, down, w_out, dy)
     return found
+
+
+def back_kernel(zs, micro, *refs):
+    (order_ref, places_ref, first_ref, dy_ref, middle_ref, gains_ref, q_ref, cos_ref, sin_ref) = refs[:9]
+    dx_part, out_part, both_part, down_part, out_all, kv_all = refs[9:15]
+    result_ref, d_middle_ref, dq_ref, dkv_ref, gain_ref, down_ref, both_up, both_down = refs[15:23]
+    out_w, kv_here, d_heads, chosen, window, bias, d_places, sems, got, held, d_sems, dl_sem, b_sems, *more = refs[23:]
+    low, full = jnp.bfloat16, jnp.float32
+    z, c, r = place()
+    many = dy_ref.shape[0]
+    span = many // micro
+    half_len = span // 2
+    greet(neighbours(zs, True, False))
+
+    def take_d_ffn(at, value):
+        d_middle_ref[at, :] = value
+
+    def take_result(at, value):
+        result_ref[at, :] = (middle_ref[at, :] + value).astype(low)
+
+    scatters = {
+        "dx": Scatter(1, False, True, dx_part, take_d_ffn, *more[:SCATTER_REFS]),
+        "out": Scatter(1, False, True, out_part, take_result, *more[SCATTER_REFS : 2 * SCATTER_REFS]),
+    }
+    down = SumChain(zs, down_part, got, held, d_sems, dl_sem)
+    lines = [
+        Line(zs, 1, 0, 1, both_part.at[lax.rem(z + zs - 1, zs)], both_up, b_sems.at[0]),
+        Line(zs, -1, zs - 1, zs, both_part.at[lax.rem(z + 1, zs)], both_down, b_sems.at[1]),
+    ]
+    schedule = [(0, 3), (0, 1), (0, 2), (0, 0)]
+    scatters["dx"].begin(schedule)
+    down.start(1)
+    for line in lines:
+        line.start()
+    loads = [pltpu.make_async_copy(out_all, out_w, sems.at[0]), pltpu.make_async_copy(kv_all, kv_here, sems.at[1])]
+    for load in loads:
+        load.start()
+    scatters["dx"].stage_a(0)
+    scatters["out"].begin(schedule)
+    scatters["dx"].stage_b(0)
+    scatters["out"].stage_a(0)
+    scatters["dx"].stage_c(0)
+    scatters["out"].stage_b(0)
+    down.finish()
+    down.start(2)
+
+    gain_ref[0:1, :] = jnp.zeros((1, D), full)
+
+    def norm_some(i, carry):
+        at = pl.ds(pl.multiple_of(i * half_len, half_len), half_len)
+        middle, d_ffn = middle_ref[at, :], d_middle_ref[at, :]
+        factor = rms_factor(middle)
+        normed = middle * factor
+        inner = d_ffn * gains_ref[1:2, :]
+        d_norm = factor * (inner - normed * jnp.mean(inner * normed, axis=-1, keepdims=True))
+        d_middle_ref[at, :] = dy_ref[at, :].astype(full) + d_norm
+        gain_ref[0:1, :] += jnp.sum(d_ffn * normed, axis=0, keepdims=True)
+        return carry
+
+    lax.fori_loop(0, many // half_len, norm_some, 0)
+    for load in loads:
+        load.wait()
+    d_heads[...] = product_nt(d_middle_ref[...].astype(low), out_w[...].reshape(D, D)).astype(low)
+
+    wide = window.shape[0]
+    half_blocks = wide // half_len
+    width = GROUP * HEAD_DIM
+
+    def attend_some(i, carry):
+        m, half = lax.div(i, 2), lax.rem(i, 2)
+        my_block = order_ref[(z * 2 + c) * 2 + half]
+        first_block = jnp.where(my_block >= half_blocks, half_blocks, 0)
+        wanted = first_block * half_len + lax.broadcasted_iota(jnp.int32, (wide, 2 * wide), 0)
+        chosen[...] = jnp.where(places_ref[...] == wanted, 1.0, 0.0).astype(low)
+        rows = pl.ds(pl.multiple_of(m * span, span), span)
+        window[...] = product(chosen[...], kv_here[:, :, rows, :].reshape(2 * wide, 2 * KVW)).astype(low)
+        key_place = first_block * half_len + lax.broadcasted_iota(jnp.int32, bias.shape, 0)
+        place_here = my_block * half_len + lax.rem(lax.broadcasted_iota(jnp.int32, bias.shape, 1), half_len)
+        first = first_ref[m]
+        start = jnp.where(place_here >= first, first, 0)
+        bias[...] = jnp.where((key_place <= place_here) & (key_place >= start), 0.0, NEG_LARGE)
+        here = pl.ds(pl.multiple_of(i * half_len, half_len), half_len)
+        cosine = jnp.concatenate([cos_ref[here, :]] * (width // 128), axis=1)
+        sine = jnp.concatenate([sin_ref[here, :]] * (width // 128), axis=1)
+        d_keys, d_values = [], []
+        for g in range(KV_HEADS):
+            at = slice(g * width, (g + 1) * width)
+            key = window[:, g * HEAD_DIM : (g + 1) * HEAD_DIM]
+            value = window[:, KVW + g * HEAD_DIM : KVW + (g + 1) * HEAD_DIM]
+            d_key, d_value, d_query = attend_back_heads(q_ref[here, at], d_heads[here, at], key, value, bias, half_len)
+            d_keys.append(d_key)
+            d_values.append(d_value)
+            dq_ref[here, at] = (d_query * cosine - partner(d_query) * sine).astype(low)
+        d_window = jnp.concatenate(d_keys + d_values, axis=1).astype(low)
+        spread_back = product_tn(chosen[...], d_window)
+
+        @pl.when(half == 0)
+        def _():
+            d_places[...] = spread_back
+
+        @pl.when(half == 1)
+        def _():
+            both = (d_places[...] + spread_back).astype(low)
+            dkv_ref[:, :, rows, :] = both.reshape(zs, 2, span, 2 * KVW)
+
+        return carry
+
+    lax.fori_loop(0, micro, attend_some, 0)
+    down.finish()
+    down.start(3)
+    lax.fori_loop(micro, 2 * micro, attend_some, 0)
+    scatters["out"].stage_c(0)
+    down.finish()
+    down.total()
+    down_ref[...] = held[0].astype(full)
+    for line in lines:
+        line.finish()
+    for one in scatters.values():
+        one.end()
+
+
+def back(order, first, dy, middle, gains, queries, cosine, sine, dx_part, out_part, both_part, down_part, out_all, kv_all,
+         zs, collective_id):
+    many = dy.shape[0]
+    micro = first.shape[0]
+    span = many // micro
+    wide = zs * span
+    low, full = jnp.bfloat16, jnp.float32
+    anywhere, here, smem = (pl.BlockSpec(memory_space=m) for m in (pl.ANY, pltpu.VMEM, pltpu.SMEM))
+    shape, sem = jax.ShapeDtypeStruct, pltpu.SemaphoreType.DMA
+    unit = down_part.shape[1]
+    piece = shape(both_part.shape[1:], low)
+    return pl.pallas_call(
+        functools.partial(back_kernel, zs, micro),
+        out_shape=[
+            shape((many, D), low), shape((many, D), full), shape((many, D), low), shape(kv_all.shape, low),
+            shape((8, D), full), shape((unit, D), full), piece, piece,
+        ],
+        in_specs=[smem, here, smem] + [here] * 6 + [anywhere] * 6,
+        out_specs=[here] * 6 + [anywhere] * 2,
+        scratch_shapes=[
+            pltpu.VMEM(out_all.shape, low),
+            pltpu.VMEM(kv_all.shape, low),
+            pltpu.VMEM((many, D), low),
+            pltpu.VMEM((wide, 2 * wide), low),
+            pltpu.VMEM((wide, 2 * KVW), low),
+            pltpu.VMEM((wide, GROUP * span // 2), full),
+            pltpu.VMEM((2 * wide, 2 * KVW), full),
+            sem((2,)),
+            pltpu.VMEM((2 * zs - 2, unit, D), low),
+            pltpu.VMEM((2, unit, D), low),
+            sem((2 * zs - 2, 2)), sem((2,)), sem((2, 2)),
+        ] + scatter_scratch(1, True, many, D, True) * 2,
+        compiler_params=pltpu.CompilerParams(
+            collective_id=collective_id, has_side_effects=True, vmem_limit_bytes=62 * MIB
+        ),
+        cost_estimate=LONG,
+    )(order, places_of(order, span), first, dy, middle, gains, queries, cosine, sine, dx_part, out_part, both_part, down_part,
+      out_all, kv_all)
+
+
+def weights_kernel(zs, *refs):
+    x_ref, attn_ref, d_middle_ref, d_attn_ref, gains_ref, gain_two_ref, cos_ref, sin_ref, dkv_ref = refs[:9]
+    packed, both_part, both_up, both_down, g_out, g_query = refs[9:15]
+    x_grad_ref, out_ref, query_ref, pack_ref, moved_ref = refs[15:20]
+    kv_w, d_kv, pack_g, sems, got, held, b_sems, bl_sem, *more = refs[20:]
+    exchange_sems, more = more[:3], more[3:]
+    low, full = jnp.bfloat16, jnp.float32
+    greet(neighbours(zs, True, True))
+
+    def into(ref):
+        def take(at, value):
+            ref[at, :] = value
+
+        return take
+
+    def next_refs(staged):
+        nonlocal more
+        mine, more = more[:SCATTER_REFS], more[SCATTER_REFS:]
+        return mine if staged else [None, *mine[1:]]
+
+    pairs = Scatter(zs, True, False, dkv_ref, into(d_kv), *next_refs(False))
+    scatters = {
+        "out": Scatter(zs, True, True, g_out, into(out_ref), *next_refs(True)),
+        "query": Scatter(zs, True, True, g_query, into(query_ref), *next_refs(True)),
+        "pack": Scatter(zs, True, True, pack_g, into(pack_ref), *next_refs(False)),
+    }
+    items = [(name, k) for k in range(1, zs) for name in ("out", "query")]
+    items[4:4] = [("pack", 1)]
+    items += [("pack", k) for k in range(2, zs)] + [("out", 0), ("query", 0), ("pack", 0)]
+    rounds, schedules = scatter_plan(items)
+
+    chain = SumChain(zs, both_part, got, held, b_sems, bl_sem)
+    loads = [
+        pltpu.make_async_copy(both_up, got.at[0], sems.at[0]),
+        pltpu.make_async_copy(both_down, got.at[zs - 1], sems.at[1]),
+        pltpu.make_async_copy(packed.at[:, :, :, :, pl.ds(D, 2 * KVW)], kv_w, sems.at[2]),
+    ]
+    for load in loads:
+        load.start()
+    chain.fetch(2)
+    pairs.begin([])
+    scatters["out"].begin(schedules["out"])
+    scatters["query"].begin(schedules["query"])
+    for k in range(1, zs):
+        pairs.stage_c(k)
+    for load in loads:
+        load.wait()
+    chain.start(2)
+
+    def keys_and_norm():
+        pairs.stage_c(0)
+        lanes = KVW // 128
+        cosine = jnp.concatenate([cos_ref[...]] * lanes, axis=1)
+        sine = jnp.concatenate([sin_ref[...]] * lanes, axis=1)
+        d_key = d_kv[:, :KVW]
+        d_lin = jnp.concatenate([d_key * cosine - partner(d_key) * sine, d_kv[:, KVW:]], axis=1).astype(low)
+        d_attn = d_attn_ref[...] + product_nt(d_lin, kv_w[...].reshape(D, 2 * KVW))
+        x = x_ref[...].astype(full)
+        factor = rms_factor(x)
+        normed = x * factor
+        inner = d_attn * gains_ref[0:1, :]
+        d_x = factor * (inner - normed * jnp.mean(inner * normed, axis=-1, keepdims=True))
+        x_grad_ref[...] = (d_middle_ref[...] + d_x).astype(low)
+        gain_one = jnp.sum(d_attn * normed, axis=0, keepdims=True)
+        rows = lax.broadcasted_iota(jnp.int32, (128, D), 0)
+        both = jnp.where(rows == 0, gain_one, jnp.where(rows == 1, gain_two_ref[0:1, :], 0.0))
+        pack = jnp.concatenate([product_tn(attn_ref[...], d_lin), both.T], axis=1).astype(low)
+        pack_g[...] = pack.reshape(pack_g.shape)
+        scatters["pack"].begin([])
+
+    for n, stages in enumerate(rounds):
+        if n == 3:
+            keys_and_norm()
+        if n == 6:
+            chain.finish()
+            chain.start(3)
+        if n == len(rounds) - 1:
+            chain.finish()
+            chain.total()
+            exchange = Exchange(held.at[0], moved_ref, *exchange_sems)
+            exchange.start()
+        for stage in stages:
+            run_stage(scatters, *stage)
+    exchange.finish()
+    exchange.end()
+    for one in (pairs, *scatters.values()):
+        one.end()
+
+
+def weight_sums(x, attn_in, d_middle, d_attn, gains, gain_two, cosine, sine, d_kv, packed, both_part, both_up, both_down, g_out,
+                g_query, zs, collective_id):
+    many = x.shape[0]
+    low, full = jnp.bfloat16, jnp.float32
+    anywhere, here = (pl.BlockSpec(memory_space=m) for m in (pl.ANY, pltpu.VMEM))
+    shape, sem = jax.ShapeDtypeStruct, pltpu.SemaphoreType.DMA
+    wide = packed.shape[3]
+    narrow = 2 * KVW + 128
+    block = both_part.shape[1:]
+    return pl.pallas_call(
+        functools.partial(weights_kernel, zs),
+        out_shape=[
+            shape((many, D), low), shape((wide, D), full), shape((wide, D), full), shape((wide, narrow), full), shape(block, low),
+        ],
+        in_specs=[here] * 9 + [anywhere] * 6,
+        out_specs=[here] * 4 + [anywhere],
+        scratch_shapes=[
+            pltpu.VMEM(packed.shape[:4] + (2 * KVW,), low),
+            pltpu.VMEM((many, 2 * KVW), full),
+            pltpu.VMEM((zs, 2, 4, wide, narrow), low),
+            sem((3,)),
+            pltpu.VMEM((2 * zs - 2,) + block, low),
+            pltpu.VMEM((2,) + block, low),
+            sem((2 * zs - 2, 2)), sem((2,)),
+        ] + EXCHANGE_SEMS
+        + scatter_scratch(zs, False, many, 2 * KVW, False)
+        + scatter_scratch(zs, True, wide, D, True) * 2
+        + scatter_scratch(zs, True, wide, narrow, False),
+        compiler_params=pltpu.CompilerParams(
+            collective_id=collective_id, has_side_effects=True, vmem_limit_bytes=62 * MIB
+        ),
+        cost_estimate=LONG,
+    )(x, attn_in, d_middle, d_attn, gains, gain_two, cosine, sine, d_kv, packed, both_part, both_up, both_down, g_out,
+      g_query)
 
 
 class Links:
@@ -976,60 +1296,14 @@
         moved = lax.all_to_all(blocks, "rows", split_axis=1, concat_axis=1, tiled=True)
         return lax.all_to_all(moved, "seq", split_axis=0, concat_axis=0, tiled=True, axis_index_groups=self.core_groups)
 
-    def along(self, way, lo, hi):
-        return [(2 * z + c, 2 * (z + way) + c) for z in range(lo, hi) for c in range(2) if 0 <= z + way < self.zs]
-
-    def permute(self, lines):
-        return [lax.ppermute(array, "seq", self.along(way, lo, hi)) for array, way, lo, hi in lines]
-
-    def part(self, blocks, to, held):
-        z = lax.div(lax.axis_index("seq"), 2)
-        found = lax.dynamic_index_in_dim(blocks, lax.rem(z + to + self.zs, self.zs), 0, keepdims=False)
-        for other, there in held:
-            found = found.astype(jnp.float32) + jnp.where(there, other.astype(jnp.float32), 0.0)
-        return found
-
-    def scatter_lines(self, k, blocks, held=None):
-        up, down = self.held(held)
-        low = blocks.dtype
-        return [
-            (self.part(blocks, -k, up).astype(low), 1, 0, k),
-            (self.part(blocks, k, down).astype(low), -1, self.zs - k, self.zs),
-        ]
-
-    def scatter_end(self, blocks, held):
-        up, down = self.held(held)
-        return self.part(blocks, 0, up + down)
-
-    def held(self, held):
-        z = lax.div(lax.axis_index("seq"), 2)
-        return ([(held[0], z > 0)], [(held[1], z < self.zs - 1)]) if held else ([], [])
-
-    @staticmethod
-    def tie(arrays, *others):
-        if not others:
-            return arrays
-        return lax.optimization_barrier((*arrays, *others))[: len(arrays)]
-
     def gather(self, array, z_flag, planes):
         if planes:
             array = lax.all_gather(array, "rows", axis=0)
         array = lax.all_gather(array, "seq", axis=0, axis_index_groups=self.core_groups)
         return self.gather_z(array[None]) if z_flag else array
 
-    def scatter(self, arrays, flags, collective_id, moved=(), lines=()):
-        if self.kernels:
-            return scatter(arrays, flags, self.zs, collective_id, moved, lines)
-        return (
-            [
-                self.scatter_one(self.scatter_z(blocks)[0] if z_flag else blocks, planes)
-                for blocks, (z_flag, planes) in zip(arrays, flags)
-            ]
-            + [self.exchange_xla(blocks) for blocks in moved]
-            + [line[0] for line in lines]
-        )
-
-    def scatter_one(self, blocks, planes):
+    def scatter(self, blocks, z_flag, planes):
+        blocks = self.scatter_z(blocks)[0] if z_flag else blocks
         blocks = lax.psum_scatter(blocks, "seq", scatter_dimension=0, tiled=True, axis_index_groups=self.core_groups)[0]
         if planes:
             blocks = lax.psum_scatter(blocks, "rows", scatter_dimension=0, tiled=True)[0]
@@ -1053,7 +1327,6 @@
     dy_own = cotangent.reshape(many, D)
     own_tokens = tokens.reshape(many, D)
     x = own_tokens.astype(jnp.float32)
-    factor_one = rms_factor(x)
     first = lengths[:, 0, 0]
     slot_of = jnp.argmax(order[None, :] == jnp.arange(order.shape[0], dtype=jnp.int32)[:, None], axis=1).astype(jnp.int32)
     chained = links.kernels
@@ -1064,7 +1337,6 @@
         down_w = [w_down, *found[4 + 2 * zs : 2 + 4 * zs]]
         queries, attn_in, attended, middle, gains, cosine, sine = found[2 + 4 * zs :]
         packed = packed.reshape(D, PACK)
-        gain_one, gain_two = gains[0], gains[1]
     else:
         both_w = [links.gather_z(links.exchange_xla(both).reshape(flat))]
         down_w = [links.gather_z(w_down)]
@@ -1076,7 +1348,7 @@
         angles = ((mine[None, :] - start).astype(jnp.float32)[..., None] * inverse).reshape(many, HEAD_DIM // 2)
         cosine, sine = jnp.cos(angles), jnp.sin(angles)
         cosine, sine = jnp.tile(cosine, (1, 4)), jnp.tile(jnp.concatenate([-sine, sine], axis=1), (1, 2))
-        attn_in = (x * factor_one * gain_one).astype(low)
+        attn_in = (x * rms_factor(x) * gain_one).astype(low)
         lin = product(attn_in, packed)
         kv_own = jnp.concatenate([turn(lin[:, D : D + KVW], cosine, sine), lin[:, D + KVW : QKV]], axis=1).astype(low)
         kv, out_w = links.gather(kv_own, True, False), links.gather(w_out, True, True)
@@ -1086,69 +1358,49 @@
     kv = kv.reshape(seq, many, 2 * KVW)
     out_w = out_w.reshape(D, D)
     dy = dy.reshape(2 * rows * many, D)
-    factor_two = rms_factor(middle)
-    normed_two = middle * factor_two
 
     ffn_in = ffn_in.reshape(2 * rows * many, D)
     result_part, d_ffn_part, grad_both, grad_down = feed_forward(ffn_in, dy, both_w, down_w, zs)
-    grad_both = grad_both.reshape(zs, *flat)
+    shards = (zs, 2, rows, wide)
+    grad_both = grad_both.reshape(*shards, 2 * zs * unit)
     grad_down = grad_down.reshape(zs, unit, D)
-    lines = []
+    d_ffn_part, result_part = (part.reshape(2, rows, many, D) for part in (d_ffn_part, result_part))
     if chained:
-        lines = links.scatter_lines(1, grad_both) + links.scatter_lines(1, grad_down)
-    d_ffn_in, *got = links.scatter([d_ffn_part.reshape(2, rows, many, D)], [(False, True)], 3, (), lines)
-    if chained:
-        lines = links.scatter_lines(2, grad_both, got[:2]) + links.scatter_lines(2, grad_down, got[2:])
-        got = links.permute(lines)
-
-    d_part, grad_gain_two = norm_back(d_ffn_in, normed_two, factor_two, gain_two)
-    d_middle = dy_own.astype(jnp.float32) + d_part
-    d_mid_low = d_middle.astype(low)
-    grad_out = product_tn(attended, d_mid_low).astype(low)
-    d_heads = product_nt(d_mid_low, out_w).astype(low)
-    d_query, d_kv = attend_back(order, slot_of, first, queries, d_heads, cosine, sine, kv)
-    shards = (zs, 2, rows, wide)
-    lines = []
-    if chained:
-        d_query, d_kv, *got = lax.optimization_barrier((d_query, d_kv, *got))
-        lines = links.scatter_lines(3, grad_both, got[:2])
-        down_lines = links.scatter_lines(3, grad_down, got[2:])
-    grad_query = product_tn(attn_in, d_query).astype(low)
-    d_kv, grad_out, grad_query, result_sum, *got = links.scatter(
-        [
-            d_kv.reshape(zs, 2, many, 2 * KVW),
-            grad_out.reshape(*shards, D),
-            grad_query.reshape(*shards, D),
-            result_part.reshape(2, rows, many, D),
-        ],
-        [(True, False), (True, True), (True, True), (False, True)],
-        4,
-        (),
-        lines,
-    )
-    if chained:
-        grad_both = links.scatter_end(grad_both, got).astype(low)
+        out_all, kv_all = out_w.reshape(*shards, D), kv.reshape(zs, 2, many, 2 * KVW)
+        result, d_middle, d_query, d_kv, gain_two_grad, grad_down, both_up, both_down = back(
+            order, first, dy_own, middle, gains, queries, cosine, sine, d_ffn_part, result_part, grad_both, grad_down,
+            out_all, kv_all, zs, 1,
+        )
+        grad_out = product_tn(attended, d_middle.astype(low)).astype(low).reshape(*shards, D)
+        grad_query = product_tn(attn_in, d_query).astype(low).reshape(*shards, D)
+        d_attn = product_nt(d_query, packed[:, :D])
+        x_grad, grad_out, grad_query, pack_grad, grad_both = weight_sums(
+            own_tokens, attn_in, d_middle, d_attn, gains, gain_two_grad, cosine, sine, d_kv, packed.reshape(*shards, PACK),
+            grad_both, both_up, both_down, grad_out, grad_query, zs, 2,
+        )
     else:
-        grad_both, grad_down = links.scatter_z(grad_both)[0], links.scatter_z(grad_down)[0]
-        down_lines = []
-    result = (middle + result_sum).astype(low)
-    d_key = turn(d_kv[:, :KVW], cosine, -sine)
-    d_kv = jnp.concatenate([d_key.astype(low), d_kv[:, KVW:].astype(low)], axis=1)
-    d_attn_in = product_nt(d_query, packed[:, :D]) + product_nt(d_kv, packed[:, D:QKV])
-    d_x, grad_gain_one = norm_back(d_attn_in, x * factor_one, factor_one, gain_one)
-    x_grad = (d_middle + d_x).astype(low)
-    gains_grad = jnp.pad(jnp.stack([grad_gain_one, grad_gain_two], axis=1), ((0, 0), (0, 126)))
-    pack_grad = jnp.concatenate([product_tn(attn_in, d_kv), gains_grad], axis=1).astype(low)
-    pack_grad, grad_both, *got = links.scatter(
-        [pack_grad.reshape(*shards, 2 * KVW + 128)],
-        [(True, True)],
-        5,
-        [grad_both.reshape(2, rows, wide, 2 * zs * unit)],
-        down_lines,
-    )
-    if chained:
-        grad_down = links.scatter_end(grad_down, got)
-    grad_down = grad_down.astype(jnp.float32)
+        d_ffn_in = links.scatter(d_ffn_part, False, True)
+        result = (middle + links.scatter(result_part, False, True)).astype(low)
+        grad_both = links.exchange_xla(links.scatter_z(grad_both)[0])
+        grad_down = links.scatter_z(grad_down)[0].astype(jnp.float32)
+        factor_two = rms_factor(middle)
+        d_part, grad_gain_two = norm_back(d_ffn_in, middle * factor_two, factor_two, gain_two)
+        d_middle = dy_own.astype(jnp.float32) + d_part
+        d_mid_low = d_middle.astype(low)
+        grad_out = links.scatter(product_tn(attended, d_mid_low).astype(low).reshape(*shards, D), True, True)
+        d_heads = product_nt(d_mid_low, out_w).astype(low)
+        d_query, d_kv = attend_back(order, slot_of, first, queries, d_heads, cosine, sine, kv)
+        grad_query = links.scatter(product_tn(attn_in, d_query).astype(low).reshape(*shards, D), True, True)
+        d_kv = links.scatter(d_kv.reshape(zs, 2, many, 2 * KVW), True, False)
+        d_key = turn(d_kv[:, :KVW], cosine, -sine)
+        d_kv = jnp.concatenate([d_key.astype(low), d_kv[:, KVW:].astype(low)], axis=1)
+        d_attn_in = product_nt(d_query, packed[:, :D]) + product_nt(d_kv, packed[:, D:QKV])
+        factor_one = rms_factor(x)
+        d_x, grad_gain_one = norm_back(d_attn_in, x * factor_one, factor_one, gain_one)
+        x_grad = (d_middle + d_x).astype(low)
+        gains_grad = jnp.pad(jnp.stack([grad_gain_one, grad_gain_two], axis=1), ((0, 0), (0, 126)))
+        pack_grad = jnp.concatenate([product_tn(attn_in, d_kv), gains_grad], axis=1).astype(low)
+        pack_grad = links.scatter(pack_grad.reshape(*shards, 2 * KVW + 128), True, True)
     grad_gate, grad_up = collect(grad_both, zs, rows, unit)
 
     return (

time: 645 us -> 619 us (0.960)
  other arithmetic: 28.8 us -> 3.68 us
  Pallas kernels: 551 us -> 575 us
  local copies, waits for them, and re-layouts: 21.4 us -> 9.92 us
  starting transfers between devices: 9.72 us -> 0 us
  matrix products: 26.9 us -> 19 us
    pallas_call x4 -> x2, Pallas kernels: 228 us -> 267 us  [the longest x1 162 us: weight_sums(): pl.pallas_call(functools.partial(weights_kernel, zs), out_shape=[shape((m...]
    convert_element_type x8 -> x0, other arithmetic: 20.1 us -> none  [the longest x4 12.7 us: scatter_lines(): self.part(blocks, k, down).astype(low)]
    pallas_call x1, Pallas kernels: 86.1 us -> 75.2 us  [feed_forward(): pl.pallas_call(functools.partial(ffn_kernel, zs, len(both_pieces)), grid=...]
    ppermute x4 -> x0, starting transfers between devices: 9.72 us -> none  [permute(): lax.ppermute(array, 'seq', self.along(way, lo, hi))]
    unnamed x65 -> x23, local copies, waits for them, and re-layouts: 13 us -> 4.66 us
    dot_general x3 -> x1, matrix products: 13.4 us -> 7.58 us  [product_nt(): lax.dot_general(left, right, (((1,), (1,)), ((), ())), preferred_element_...]
    dot_general x3 -> x2, matrix products: 13.4 us -> 11.5 us  [product_tn(): lax.dot_general(left, right, (((0,), (0,)), ((), ())), preferred_element_...]
  transfers between devices with their start and end apart: 4 -> 0, of which waited for: 1 -> 0; matrix products, arithmetic and copies ran while one was open for 3% -> 0% of each run, Pallas kernels for 3% -> 0%
where the time goes in v4:
time: 619 us; the launch traced here: 609 us
  Pallas kernels  575 us (93%)
  matrix products  19 us (3%)
  local copies, waits for them, and re-layouts  9.92 us (2%)
    pallas_call x1, Pallas kernels, forward(): pl.pallas_call(functools.partial(forward_kernel, zs, micro), out_shape=ou...  226 us
    pallas_call x1, Pallas kernels, weight_sums(): pl.pallas_call(functools.partial(weights_kernel, zs), out_shape=[shape((m...  162 us
    pallas_call x1, Pallas kernels, back(): pl.pallas_call(functools.partial(back_kernel, zs, micro), out_shape=[shap...  106 us
    pallas_call x1, Pallas kernels, feed_forward(): pl.pallas_call(functools.partial(ffn_kernel, zs, len(both_pieces)), grid=...  75.2 us

profile of v4, /device:TPU:8, one launch (start us, length us, event | category | flops | bytes accessed | tf_op | source)
XLA Modules:
  0.0 608.6 jit_solution(3749584827058967190)
XLA Ops:
  0.6 1.3 slice_reduce_fusion.2.refs_2_
  2.0 0.7 pad_maximum_fusion
  2.6 0.7 broadcast_multiply_fusion
  3.3 0.5 fusion.8.refs_3_
  3.8 0.1 iota_add_fusion
  3.9 0.7 add.48.refs_1_
  4.6 0.1 copy.32
  4.7 1.7 fusion.4.refs_5_
  6.4 3.1 shard_map.212.refs_6_
  9.5 225.9 %shard_map.213 = (bf16[4,2,4,64,2688]{4,3,2,1,0:T(8,128)(2,1)}, bf16[2,4,64,1408]{3,2,1,0:T(8,128)(2,1)}, bf16[4,2,256,512]{3,2,1,0:T(8,128)(2,1)}, bf16[4,2,4,6...) custom-call(s32[16]{0:T(128)} %refs_0_.3, ...), custom_call_target="tpu_custom_call" | custom-call | flops 49999998976 | bytes 157286400 | tf_op jit(solution)/shard_map/pallas_call | solution.py:974
  235.4 75.2 %shard_map.214 = (bf16[2048,2048]{1,0:T(8,128)(2,1)}, bf16[2048,2048]{1,0:T(8,128)(2,1)}, bf16[2048,1408]{1,0:T(8,128)(2,1)}, bf16[704,2048]{1,0:T(8,128)(2,1)}) custom-call(bf16[2048,2048]{1,0:T(8,128)(2,1)} %bitcast.44, bf16[2048,2048]{1,0:T(8,128)(2,1)} %bitcast.43, bf16[512,1408]{1,0:T(8,128)(2,1)} %bitcast.48, bf16[512,1408]{1,0:T(8,128)(2,1)} %bitcast.49, ...), custom_call_target="tpu_custom_call" | custom-call | flops 53150220288 | bytes 62914560 | tf_op jit(solution)/shard_map/pallas_call | solution.py:719
  310.7 105.8 %shard_map.215 = (bf16[256,2048]{1,0:T(8,128)(2,1)}, f32[256,2048]{1,0:T(8,128)}, bf16[256,2048]{1,0:T(8,128)(2,1)}, bf16[4,2,256,512]{3,2,1,0:T(8,128)(2,1)}, f...) custom-call(s32[16]{0:T(128)} %refs_0_.3, ...), custom_call_target="tpu_custom_call" | custom-call | flops 49999998976 | bytes 157286400 | tf_op jit(solution)/shard_map/pallas_call | solution.py:1128
  416.4 0.0 copy-start.2
  416.4 0.0 copy-start.4
  416.5 7.6 %fusion.refs_3_ = f32[256,2048]{1,0:T(8,128)} fusion(bf16[256,2048]{1,0:T(8,128)(2,1)} %get-tuple-element.84, bf16[2048,2688]{1,0:T(8,128)(2,1)} %bitcast.40), kind=kOutput, calls=%fused_computation | convolution fusion | flops 2147483648 | bytes 11534336 | tf_op jit(solution)/shard_map/dot_general | solution.py:31
  424.0 0.0 copy-done.2
  424.0 0.0 copy-done.4
  424.1 5.7 convolution_convert_fusion
  429.7 5.8 convolution_convert_fusion.1
  435.5 161.5 %shard_map.216 = (bf16[256,2048]{1,0:T(8,128)(2,1)}, f32[64,2048]{1,0:T(8,128)}, f32[64,2048]{1,0:T(8,128)}, f32[64,640]{1,0:T(8,128)}, bf16[2,4,64,1408]{3,2,1,0:T(8,128)(2,1)}) custom-call(bf16[256,2048]{1,0:T(8,128)(2,1)} %bitcast.37, bf16[256,2048]{1,0:T(8,128)(2,1)} %get-tuple-element.82.refs_1_, f32[256,2048]{1,0:T(8,128)} %get-tuple-element.83.refs_2_, ...), custom_call_target="tpu_custom_call" | custom-call | flops 49999998976 | bytes 157286400 | tf_op jit(solution)/shard_map/pallas_call | solution.py:1255
  597.1 0.0 copy-start.5
  597.1 0.0 copy-start.6
  597.1 1.6 slice_reduce_fusion
  598.7 1.5 fusion.9
  600.2 3.3 shard_map.217
  603.5 1.0 copy.40
  604.5 0.0 copy-done.6
  604.5 1.0 copy.41
  605.5 0.8 copy.42
  606.3 0.8 copy.43
  607.1 0.0 copy-done.3
  607.1 1.1 copy.44
  (10 shorter events, 0.0 us)
Async XLA Ops:
  416.4 7.6 %copy-start.2 = (bf16[256,2048]{1,0:T(8,128)(2,1)S(1)}, bf16[256,2048]{1,0:T(8,128)(2,1)}, u32[]{:S(2)}) copy-start(bf16[256,2048]{1,0:T(8,128)(2,1)} %get-tuple-element.82.refs_1_) | copy-start | bytes 3145732
  416.4 7.6 %copy-start.4 = (bf16[256,2048]{1,0:T(8,128)(2,1)S(1)}, bf16[256,2048]{1,0:T(8,128)(2,1)}, u32[]{:S(2)}) copy-start(bf16[256,2048]{1,0:T(8,128)(2,1)} %get-tuple-element.84) | copy-start | bytes 3145732
  424.0 5.7 copy-start
  424.0 5.7 copy-start.1
  597.1 6.4 %copy-start.5 = (bf16[256,2048]{1,0:T(8,128)(2,1)S(1)}, bf16[256,2048]{1,0:T(8,128)(2,1)}, u32[]{:S(2)}) copy-start(bf16[256,2048]{1,0:T(8,128)(2,1)} %get-tuple-element.81) | copy-start | bytes 3145732
  597.1 7.4 %copy-start.6 = (bf16[256,2048]{1,0:T(8,128)(2,1)S(1)}, bf16[256,2048]{1,0:T(8,128)(2,1)}, u32[]{:S(2)}) copy-start(bf16[256,2048]{1,0:T(8,128)(2,1)} %get-tuple-element.91) | copy-start | bytes 3145732
  603.5 2.0 copy-start.8
  604.5 1.8 copy-start.7
  604.5 2.6 copy-start.3

commit v5 on v4

--- a/solution.py
+++ b/solution.py
@@ -154,6 +154,9 @@
         self.count = zs if z_flag else 1
         self.half = own.shape[0] // 2
         self.pending = []
+        self.sent = []
+        z = self.z
+        self.kth = [0, jnp.where(z == 0, 3, 1), jnp.where((z == 0) | (z == 3), 2, 3), jnp.where(z == 0, 1, jnp.where(z == 3, 3, 2))]
 
     def start(self, copy):
         copy.start()
@@ -166,11 +169,17 @@
         zz = lax.rem(self.z - k + self.zs, self.zs)
         return self.out.at[zz, core, self.line[j]] if self.planes else self.out.at[zz, core]
 
-    def z_copy(self, k, dst):
-        src = self.own if dst is None else dst
-        dst = self.slot(0, 0, 0) if dst is None else dst
-        to = (lax.rem(self.z + k, self.zs) * 2 + self.c, self.r)
-        return send(src, dst, self.z_ssem.at[k], self.z_rsem.at[k], to)
+    def z_copy(self, n, way, k, src, dst):
+        to = (lax.rem(self.z + way + self.zs, self.zs) * 2 + self.c, self.r)
+        return send(src, dst, self.z_ssem.at[n, 0 if way == 1 else 1], self.z_rsem.at[k], to)
+
+    def hand_on(self, n, src, dst):
+        z, k, zs = self.z, self.kth[n], self.zs
+        up, down = (z < zs - 1, z > 0) if n == 0 else ((z >= k) & (z < zs - 1), (z < k) & (z > 0))
+        for way, goes, step in ((1, up, 1), (-1, down, zs - 1)):
+            copy = self.z_copy(n, way, lax.rem(k + step, zs), src, dst)
+            pl.when(goes)(copy.start)
+            self.sent.append((goes, copy))
 
     def near(self, k, j, src):
         dst = self.slot(k, 0, j) if src is None or not self.z_flag else self.slot(k, 0, 0)
@@ -194,39 +203,52 @@
     def launch(self):
         self.local = pltpu.make_async_copy(self.own, self.slot(0, 0, 0), self.l_sem)
         self.local.start()
-        for k in range(1, self.count):
-            self.start(self.z_copy(k, None))
-
-    def begin(self, k):
-        src = self.own
-        if k:
-            src = self.slot(k, 0, 0)
-            self.z_copy(k, src).wait_recv()
+        if self.count > 1 and self.planes:
+            self.hand_on(0, self.own, self.slot(0, 0, 0))
+        elif self.count > 1:
+            for k in range(1, self.count):
+                self.start(self.z_copy(k, k, k, self.own, self.slot(0, 0, 0)))
+
+    def arrive(self, n):
+        k = self.kth[n]
+        src = self.slot(k, 0, 0)
+        self.z_copy(n, 1, k, src, src).wait_recv()
+        if self.planes:
+            self.hand_on(n, src, src)
+
+    def begin(self, n):
+        k = self.kth[n]
+        src = self.slot(k, 0, 0) if n else self.own
         if self.planes:
             for j in (1, 2):
                 self.start(self.near(k, j, src))
         self.to_twin(k, 0, src)
 
-    def forward(self, k):
+    def forward(self, n):
+        k = self.kth[n]
         for j in (1, 2):
             self.near(k, j, None).wait_recv()
             src = self.slot(k, 0, j)
             self.start(self.far(k, j, src))
             self.to_twin(k, j, src)
 
-    def finish(self, k):
+    def finish(self, n):
+        k = self.kth[n]
         for j in (1, 2):
             self.far(k, j, None).wait_recv()
         self.to_twin(k, 3, self.slot(k, 0, 3))
 
-    def complete(self, k):
-        if k == 0:
+    def complete(self, n):
+        k = self.kth[n]
+        if n == 0:
             self.local.wait()
         for j in range(4 if self.planes else 1):
             dst = self.slot(k, 1, j)
             send(dst, dst, self.c_ssem.at[k, j], self.c_rsem.at[k, j], self.twin).wait_recv()
 
     def end(self):
+        for goes, copy in self.sent:
+            pl.when(goes)(copy.wait_send)
         for wait in self.pending:
             wait()
 
@@ -234,7 +256,7 @@
 def gather_sems(zs, z_flag):
     sem = pltpu.SemaphoreType.DMA
     n = zs if z_flag else 1
-    return [sem((n,)), sem((n,)), sem((n, 2)), sem((n, 2)), sem((n, 2)), sem((n, 2)), sem((n, 4)), sem((n, 4)), sem]
+    return [sem((n, 2)), sem((n,)), sem((n, 2)), sem((n, 2)), sem((n, 2)), sem((n, 2)), sem((n, 4)), sem((n, 4)), sem]
 
 
 class Chain:
@@ -431,14 +453,15 @@
             load.start()
 
     def add(self, into, more):
-        self.got[into] = (self.got[into].astype(jnp.float32) + self.held[more].astype(jnp.float32)).astype(self.got.dtype)
+        ref = self.got[into]
+        ref[...] = (ref[...].astype(jnp.float32) + self.held[more].astype(jnp.float32)).astype(ref.dtype)
 
     def start(self, k):
         zs, z, got = self.zs, self.z, self.got
         up, down = k - 1, zs - 2 + k
         self.lines = [
-            Line(zs, 1, 0, 1, self.own(-k), got.at[up], self.sems.at[up]),
-            Line(zs, -1, zs - 1, zs, self.own(k), got.at[down], self.sems.at[down]),
+            Line(zs, 1, 0, 1, self.own(-k), got[up], self.sems.at[up]),
+            Line(zs, -1, zs - 1, zs, self.own(k), got[down], self.sems.at[down]),
         ]
         if k > 1:
             for load in self.loads:
@@ -446,14 +469,14 @@
             pl.when((z >= 1) & (z < k))(functools.partial(self.add, up - 1, 0))
             pl.when((z >= zs - k) & (z < zs - 1))(functools.partial(self.add, down - 1, 1))
             self.lines += [
-                Line(zs, 1, 1, k, got.at[up - 1], got.at[up], self.sems.at[up]),
-                Line(zs, -1, zs - k, zs - 1, got.at[down - 1], got.at[down], self.sems.at[down]),
+                Line(zs, 1, 1, k, got[up - 1], got[up], self.sems.at[up]),
+                Line(zs, -1, zs - k, zs - 1, got[down - 1], got[down], self.sems.at[down]),
             ]
         for line in self.lines:
             line.start()
-        if k < zs - 1:
+        if k < zs - 1 and self.got[up + 1] is not None:
             self.fetch(k + 1)
-        else:
+        elif k == zs - 1:
             self.loads = [pltpu.make_async_copy(self.own(0), self.held.at[0], self.l_sem.at[0])]
             self.loads[0].start()
 
@@ -466,7 +489,7 @@
         self.loads[0].wait()
 
         def add(come):
-            self.held[0] = (self.held[0].astype(jnp.float32) + self.got[come].astype(jnp.float32)).astype(self.held.dtype)
+            self.held[0] = (self.held[0].astype(jnp.float32) + self.got[come][...].astype(jnp.float32)).astype(self.held.dtype)
 
         pl.when(z > 0)(functools.partial(add, zs - 2))
         pl.when(z < zs - 1)(functools.partial(add, 2 * zs - 3))
@@ -651,22 +674,72 @@
     def rows(zz):
         return whole.at[pl.ds(pl.multiple_of(zz * size, size), size)]
 
+    if len(pieces) == 2:
+        pieces = [pieces[0], *(pieces[1].at[k] for k in range(zs - 1))]
     copies = [pltpu.make_async_copy(pieces[0], rows(z), sem.at[0])]
     copies[0].start()
     for k in range(1, zs):
-        below = pltpu.make_async_copy(pieces[k], rows(lax.rem(z - k + zs, zs)), sem.at[k])
-        above = pltpu.make_async_copy(pieces[2 * zs - 1 - k], rows(lax.rem(z - k + zs, zs)), sem.at[k])
-        pl.when(z >= k)(below.start)
-        pl.when(z < k)(above.start)
+        to = rows(lax.rem(z - k + zs, zs))
+        below = pltpu.make_async_copy(pieces[k], to, sem.at[k])
+        if len(pieces) == zs:
+            below.start()
+        else:
+            above = pltpu.make_async_copy(pieces[2 * zs - 1 - k], to, sem.at[k])
+            pl.when(z >= k)(below.start)
+            pl.when(z < k)(above.start)
         copies.append(below)
     return copies
 
 
-def ffn_kernel(zs, count, *refs):
+class Around:
+    def __init__(self, zs, block, got, sems):
+        z, c, r = place()
+        self.copies = [
+            send(block(k), got.at[k - 1], sems.at[k - 1, 0], sems.at[k - 1, 1], (lax.rem(z + k, zs) * 2 + c, r))
+            for k in range(1, zs)
+        ]
+
+    def start(self):
+        for copy in self.copies:
+            copy.start()
+
+    def finish(self):
+        for copy in self.copies:
+            copy.wait()
+
+
+def swiglu(lin, d_hidden):
+    n = d_hidden.shape[1]
+    gate, upper = lin[:, :n], lin[:, n:]
+    sig = 1.0 / (1.0 + jnp.exp(-gate))
+    act = gate * sig
+    d_gate = d_hidden * upper * (sig * (1.0 + gate * (1.0 - sig)))
+    d_both = jnp.concatenate([d_gate.astype(jnp.bfloat16), (d_hidden * act).astype(jnp.bfloat16)], axis=1)
+    return (act * upper).astype(jnp.bfloat16), d_both
+
+
+def add_gradients(x, dy, hidden, d_both, both_sum, down_sum):
+    for at in range(0, D, 256):
+        both_sum[at : at + 256, :] += product_tn(x[:, at : at + 256], d_both)
+    part = hidden.shape[1] // 4
+    for at in range(0, hidden.shape[1], part):
+        down_sum[at : at + part, :] += product_tn(hidden[:, at : at + part], dy)
+
+
+def put_gradients(sums, staged, out, sem):
+    copies = []
+    for n in range(2):
+        staged[n][...] = sums[n][...].astype(jnp.bfloat16)
+        copies.append(pltpu.make_async_copy(staged[n], out[n], sem.at[n, 0]))
+        copies[-1].start()
+    for copy in copies:
+        copy.wait()
+
+
+def ffn_first_kernel(zs, count, *refs):
     x_ref, dy_ref = refs[:2]
     both_pieces, down_pieces = refs[2 : 2 + count], refs[2 + count : 2 + 2 * count]
-    out_ref, dx_ref, g_both_ref, g_down_ref, both_w, down_w, both_sum, down_sum, sem = refs[2 + 2 * count :]
-    n = down_w.shape[0]
+    hidden_ref, d_both_ref, g_both_ref, g_down_ref, both_w, down_w, both_sum, down_sum, sem = refs[2 + 2 * count :]
     step, last = pl.program_id(0), pl.num_programs(0) - 1
 
     @pl.when(step == 0)
@@ -678,71 +751,157 @@
             copy.wait()
 
     x, dy = x_ref[...], dy_ref[...]
-    lin = product(x, both_w[...])
-    gate, upper = lin[:, :n], lin[:, n:]
-    sig = 1.0 / (1.0 + jnp.exp(-gate))
-    act = gate * sig
-    hidden = (act * upper).astype(jnp.bfloat16)
-    d_hidden = product_nt(dy, down_w[...])
-    d_gate = d_hidden * upper * (sig * (1.0 + gate * (1.0 - sig)))
-    d_both = jnp.concatenate([d_gate.astype(jnp.bfloat16), (d_hidden * act).astype(jnp.bfloat16)], axis=1)
-    dx_ref[...] = product_nt(d_both, both_w[...]).astype(jnp.bfloat16)
-    out_ref[...] = product(hidden, down_w[...]).astype(jnp.bfloat16)
-    for at in range(0, D, 256):
-        both_sum[at : at + 256, :] += product_tn(x[:, at : at + 256], d_both)
-    part = n // 4
-    for at in range(0, n, part):
-        down_sum[at : at + part, :] += product_tn(hidden[:, at : at + part], dy)
+    hidden, d_both = swiglu(product(x, both_w[...]), product_nt(dy, down_w[...]))
+    hidden_ref[...] = hidden
+    d_both_ref[...] = d_both
+    add_gradients(x, dy, hidden, d_both, both_sum, down_sum)
 
     @pl.when(step == last)
     def _():
-        both_w[...] = both_sum[...].astype(jnp.bfloat16)
+        put_gradients((both_sum, down_sum), (both_w, down_w), (g_both_ref, g_down_ref), sem)
+
+
+def ffn_second_kernel(zs, counts, linked, *refs):
+    x_ref, dy_ref, hidden_ref, d_both_ref = refs[:4]
+    refs = refs[4:]
+    pieces = []
+    for count in counts:
+        pieces += [refs[:count], refs[count : 2 * count]]
+        refs = refs[2 * count :]
+    if linked:
+        g_both_one, g_down_one, *refs = refs
+    out_ref, dx_ref, g_both_ref, g_down_ref, *refs = refs
+    if linked:
+        *got, both_one, down_one, both_w, down_w, both_sum, down_sum, stage, sem, z_sem = refs
+    else:
+        got, (both_one, down_one, both_w, down_w, both_sum, down_sum, stage, sem) = [], refs
+    n, wide = stage.shape[1] // 2, down_w.shape[0]
+    down_rows = down_w.at[pl.ds(0, n)]
+    step, last = pl.program_id(0), pl.num_programs(0) - 1
+    lines = []
+    if linked:
+        z = lax.div(lax.axis_index("seq"), 2)
+        for at, parts in ((0, g_both_one), (2, g_down_one)):
+            lines += [
+                Line(zs, 1, 0, 1, parts.at[lax.rem(z + zs - 1, zs)], got[at], z_sem.at[at]),
+                Line(zs, -1, zs - 1, zs, parts.at[lax.rem(z + 1, zs)], got[at + 1], z_sem.at[at + 1]),
+            ]
+
+    @pl.when(step == 0)
+    def _():
+        copies = []
+        for which, whole in enumerate((both_one, down_one, stage, down_rows)):
+            copies += assemble(zs, pieces[which], whole, sem.at[which])
+        if linked:
+            greet(neighbours(zs, False, False))
+            for line in lines:
+                line.start()
+        both_sum[...] = jnp.zeros_like(both_sum)
+        down_sum[...] = jnp.zeros_like(down_sum)
+        if wide > n:
+            both_w[...] = jnp.zeros_like(both_w)
+            down_w[n:, :] = jnp.zeros((wide - n, D), down_w.dtype)
+        for copy in copies:
+            copy.wait()
+        both_w[:, :n] = stage[:, :n]
+        both_w[:, wide : wide + n] = stage[:, n:]
+
+    x, dy = x_ref[...], dy_ref[...]
+    hidden, d_both = swiglu(product(x, both_w[...]), product_nt(dy, down_w[...]))
+    dx_ref[...] = (product_nt(d_both_ref[...], both_one[...]) + product_nt(d_both, both_w[...])).astype(jnp.bfloat16)
+    out_ref[...] = (product(hidden_ref[...], down_one[...]) + product(hidden, down_w[...])).astype(jnp.bfloat16)
+    add_gradients(x, dy, hidden, d_both, both_sum, down_sum)
+
+    @pl.when(step == last)
+    def _():
+        stage[:, :n] = both_sum[:, :n].astype(jnp.bfloat16)
+        stage[:, n:] = both_sum[:, wide : wide + n].astype(jnp.bfloat16)
         down_w[...] = down_sum[...].astype(jnp.bfloat16)
         copies = [
-            pltpu.make_async_copy(both_w, g_both_ref, sem.at[0, 0]),
-            pltpu.make_async_copy(down_w, g_down_ref, sem.at[1, 0]),
+            pltpu.make_async_copy(stage, g_both_ref, sem.at[0, 0]), pltpu.make_async_copy(down_rows, g_down_ref, sem.at[1, 0])
         ]
         for copy in copies:
             copy.start()
         for copy in copies:
             copy.wait()
-
-
-def feed_forward(x, dy, both_pieces, down_pieces, zs):
-    count = x.shape[0]
-    spread_over = zs if len(both_pieces) > 1 else 1
-    n = down_pieces[0].shape[0] * spread_over
-    block = 256
-    low = jnp.bfloat16
-    tokens = pl.BlockSpec((block, D), lambda i: (i, 0))
+        for line in lines:
+            line.finish()
+
+
+def ffn_first(x, dy, both_pieces, down_pieces, zs):
+    count, n = len(both_pieces), down_pieces[0].shape[0] * (zs if len(down_pieces) > 1 else 1)
+    block, low, full = 256, jnp.bfloat16, jnp.float32
+    sem, shape = pltpu.SemaphoreType.DMA, jax.ShapeDtypeStruct
     anywhere = pl.BlockSpec(memory_space=pl.ANY)
+
+    def tokens(width):
+        return pl.BlockSpec((block, width), lambda i: (i, 0))
+
     return pl.pallas_call(
-        functools.partial(ffn_kernel, zs, len(both_pieces)),
-        grid=(count // block,),
-        in_specs=[tokens, tokens] + [anywhere] * (2 * len(both_pieces)),
-        out_specs=[tokens, tokens, anywhere, anywhere],
-        out_shape=[jax.ShapeDtypeStruct(x.shape, low)] * 2
-        + [jax.ShapeDtypeStruct((D, 2 * n), low), jax.ShapeDtypeStruct((n, D), low)],
+        functools.partial(ffn_first_kernel, zs, count),
+        grid=(x.shape[0] // block,),
+        in_specs=[tokens(D)] * 2 + [anywhere] * (2 * count),
+        out_specs=[tokens(n), tokens(2 * n)] + [anywhere] * 2,
+        out_shape=[shape((x.shape[0], n), low), shape((x.shape[0], 2 * n), low), shape((D, 2 * n), low), shape((n, D), low)],
         scratch_shapes=[
-            pltpu.VMEM((D, 2 * n), low),
-            pltpu.VMEM((n, D), low),
-            pltpu.VMEM((D, 2 * n), jnp.float32),
-            pltpu.VMEM((n, D), jnp.float32),
-            pltpu.SemaphoreType.DMA((2, zs)),
+            pltpu.VMEM((D, 2 * n), low), pltpu.VMEM((n, D), low), pltpu.VMEM((D, 2 * n), full), pltpu.VMEM((n, D), full),
+            sem((2, zs)),
         ],
-        compiler_params=pltpu.CompilerParams(vmem_limit_bytes=60 * MIB),
-        cost_estimate=pl.CostEstimate(flops=18 * count * D * n, bytes_accessed=60 * MIB, transcendentals=count * n),
+        compiler_params=pltpu.CompilerParams(vmem_limit_bytes=56 * MIB),
+        cost_estimate=LONG,
     )(x, dy, *both_pieces, *down_pieces)
 
 
-def spread_kernel(zs, rows, unit, gate_ref, up_ref, out):
-    for c in range(2):
-        for r in range(rows):
-            for n, weight in enumerate((gate_ref, up_ref)):
-                for z in range(zs):
-                    at = ((z * 2 + c) * rows + r) * unit
-                    to = (n * zs + z) * unit
-                    out[c, r, :, to : to + unit] = weight[:, at : at + unit]
+def ffn_second(x, dy, hidden, d_both, one, two, zs, parts=(), collective_id=None):
+    counts = (len(one[0]), len(two[0]))
+    wides = [down[0].shape[0] * (zs if len(down) > 1 else 1) for _, down in (one, two)]
+    n = wides[1]
+    wide = -(-n // 128) * 128
+    block, low, full = 256, jnp.bfloat16, jnp.float32
+    sem, shape = pltpu.SemaphoreType.DMA, jax.ShapeDtypeStruct
+    anywhere = pl.BlockSpec(memory_space=pl.ANY)
+
+    def tokens(width):
+        return pl.BlockSpec((block, width), lambda i: (i, 0))
+
+    linked = bool(parts)
+    params = dict(collective_id=collective_id, has_side_effects=True) if linked else {}
+    return pl.pallas_call(
+        functools.partial(ffn_second_kernel, zs, counts, linked),
+        grid=(x.shape[0] // block,),
+        in_specs=[tokens(D)] * 2 + [tokens(wides[0]), tokens(2 * wides[0])] + [anywhere] * (2 * sum(counts) + len(parts)),
+        out_specs=[tokens(D)] * 2 + [anywhere] * (2 + 2 * len(parts)),
+        out_shape=[shape(x.shape, low)] * 2 + [shape((D, 2 * n), low), shape((n, D), low)]
+        + [shape(part.shape[1:], low) for part in parts for _ in range(2)],
+        scratch_shapes=[
+            pltpu.VMEM((D, 2 * wides[0]), low), pltpu.VMEM((wides[0], D), low),
+            pltpu.VMEM((D, 2 * wide), low), pltpu.VMEM((wide, D), low),
+            pltpu.VMEM((D, 2 * wide), full), pltpu.VMEM((wide, D), full), pltpu.VMEM((D, 2 * n), low),
+            sem((4, zs)),
+        ] + [sem((4, 2))] * linked,
+        compiler_params=pltpu.CompilerParams(vmem_limit_bytes=56 * MIB, **params),
+        cost_estimate=LONG,
+    )(x, dy, hidden, d_both, *one[0], *one[1], *two[0], *two[1], *parts)
+
+
+def split_unit(unit):
+    return unit * 3 // 4 // 16 * 16
+
+
+def portions(unit):
+    first = split_unit(unit)
+    return (0, first), (first, unit - first)
+
+
+def spread_kernel(zs, rows, unit, gate_ref, up_ref, *out):
+    for (begin, size), ref in zip(portions(unit), out):
+        for c in range(2):
+            for r in range(rows):
+                for n, weight in enumerate((gate_ref, up_ref)):
+                    for z in range(zs):
+                        at = ((z * 2 + c) * rows + r) * unit + begin
+                        to = (n * zs + z) * size
+                        ref[c, r, :, to : to + size] = weight[:, at : at + size]
 
 
 def spread(gate, up, zs, rows):
@@ -750,28 +909,32 @@
     unit = part // (zs * 2 * rows)
     return pl.pallas_call(
         functools.partial(spread_kernel, zs, rows, unit),
-        out_shape=jax.ShapeDtypeStruct((2, rows, wide, 2 * zs * unit), gate.dtype),
+        out_shape=[jax.ShapeDtypeStruct((2, rows, wide, 2 * zs * size), gate.dtype) for _, size in portions(unit)],
     )(gate, up)
 
 
-def collect_kernel(zs, rows, unit, given, *outs):
+def collect_kernel(zs, rows, unit, *refs):
+    given, outs = refs[:2], refs[2:]
     for n, out in enumerate(outs):
-        for c in range(2):
-            for r in range(rows):
-                for z in range(zs):
-                    at = ((z * 2 + c) * rows + r) * unit
-                    to = (n * zs + z) * unit
-                    out[:, at : at + unit] = given[c, r, :, to : to + unit].astype(jnp.float32)
+        for (begin, size), ref in zip(portions(unit), given):
+            for c in range(2):
+                for r in range(rows):
+                    for z in range(zs):
+                        at = ((z * 2 + c) * rows + r) * unit + begin
+                        to = (n * zs + z) * size
+                        out[:, at : at + size] = ref[c, r, :, to : to + size].astype(jnp.float32)
 
 
 def collect(blocks, zs, rows, unit):
-    shape = jax.ShapeDtypeStruct((blocks.shape[2], unit * zs * 2 * rows), jnp.float32)
-    return pl.pallas_call(functools.partial(collect_kernel, zs, rows, unit), out_shape=[shape, shape])(blocks)
+    shape = jax.ShapeDtypeStruct((blocks[0].shape[2], unit * zs * 2 * rows), jnp.float32)
+    return pl.pallas_call(functools.partial(collect_kernel, zs, rows, unit), out_shape=[shape, shape])(*blocks)
 
 
 def forward_kernel(zs, micro, *refs):
-    order_ref, places_ref, first_ref, freq_ref, x_ref, pack_ref, both_ref, down_ref, out_ref, dy_ref = refs[:10]
-    packed, both_own, kv_all, out_all, dy_all, ffn_all = refs[10:16]
+    order_ref, places_ref, first_ref, freq_ref, x_ref, pack_ref, both_ref, down_ref, out_ref, dy_ref, rest_ref, last_ref = refs[:12]
+    refs = refs[2:]
+    packed, both_own, kv_all, out_all, dy_all, ffn_all, rest_own, rest_got, last_got = refs[10:19]
+    refs = refs[3:]
     steps = 2 * zs - 2
     both_got, down_got = refs[16 : 16 + steps], refs[16 + steps : 16 + 2 * steps]
     q_ref, attn_ref, attended_ref, middle_ref, gains_ref, cos_ref, sin_ref = refs[16 + 2 * steps : 23 + 2 * steps]
@@ -785,6 +948,9 @@
     greet(neighbours(zs, True, True))
 
     exchange = Exchange(both_ref, both_own, *more[:3])
+    rest = Exchange(rest_ref, rest_own, *more[3:6])
+    arounds = [Around(zs, lambda k: rest_own, rest_got, more[6].at[0]), Around(zs, lambda k: last_ref, last_got, more[6].at[1])]
+    more = more[:3] + more[7:]
     both_chain, down_chain = Chain(zs, both_own, both_got, more[3]), Chain(zs, down_ref, down_got, more[4])
     more = more[5:]
     weights = Gather(zs, True, True, pack_ref, packed, *more[:9])
@@ -797,6 +963,7 @@
     exchange.start()
     weights.begin(0)
     outs.launch()
+    rest.start()
 
     lane = lax.broadcasted_iota(jnp.int32, (half_len, 128), 1)
     for i in range(2 * micro):
@@ -811,41 +978,47 @@
 
     loads = {}
 
-    def load(k):
-        weights.complete(k)
-        zz = lax.rem(z - k + zs, zs)
-        loads[k] = pltpu.make_async_copy(packed.at[zz], staged.at[k % 2], sems.at[k % 2])
-        loads[k].start()
-
-    def project(k):
-        loads[k].wait()
-        zz = lax.rem(z - k + zs, zs)
+    def load(n):
+        weights.complete(n)
+        zz = lax.rem(z - weights.kth[n] + zs, zs)
+        loads[n] = pltpu.make_async_copy(packed.at[zz], staged.at[n % 2], sems.at[n % 2])
+        loads[n].start()
+
+    def project(n):
+        loads[n].wait()
+        zz = lax.rem(z - weights.kth[n] + zs, zs)
         at = pl.ds(pl.multiple_of(zz * rows, rows), rows)
-        block = staged[k % 2].reshape(rows, PACK)
+        block = staged[n % 2].reshape(rows, PACK)
         gains = block[:, QKV:].astype(jnp.float32).T[:8]
         gains_ref[:, at] = gains
         attn_in = (x_ref[:, at].astype(jnp.float32) * factor * gains[0:1]).astype(low)
         attn_ref[:, at] = attn_in
         value = product(attn_in, block[:, :QKV])
-        lin[...] = value if k == 0 else lin[...] + value
-
+        lin[...] = value if n == 0 else lin[...] + value
+
+    weights.arrive(1)
     weights.begin(1)
     weights.forward(0)
+    weights.arrive(2)
     weights.begin(2)
     weights.forward(1)
     weights.finish(0)
+    weights.arrive(3)
     weights.begin(3)
     down_chain.start(1)
     exchange.finish()
     both_chain.start(1)
+    outs.arrive(1)
     weights.forward(2)
     weights.finish(1)
     load(0)
+    outs.arrive(2)
     weights.forward(3)
     weights.finish(2)
     outs.begin(0)
     load(1)
     project(0)
+    outs.arrive(3)
     outs.begin(1)
     project(1)
     weights.finish(3)
@@ -876,7 +1049,11 @@
     down_chain.finish()
     both_chain.start(2)
     down_chain.start(2)
+    rest.finish()
+    for one in arounds:
+        one.start()
     for k in range(1, zs):
+        pairs.arrive(k)
         pairs.begin(k)
     outs.forward(1)
     outs.finish(0)
@@ -943,6 +1120,9 @@
     ffns.complete(0)
     both_chain.finish()
     down_chain.finish()
+    for one in arounds:
+        one.finish()
+    rest.end()
     exchange.end()
     for one in (weights, outs, pairs, dys, ffns):
         one.end()
@@ -952,7 +1132,7 @@
     return (order[:, None] * (span // 2) + jnp.arange(span // 2, dtype=jnp.int32)).reshape(1, -1)
 
 
-def forward(order, first, tokens, pack, both, down, w_out, dy, zs, collective_id):
+def forward(order, first, tokens, pack, both, rest, down, last, w_out, dy, zs, collective_id):
     many = tokens.shape[0]
     micro = first.shape[0]
     seq = 2 * zs
@@ -968,13 +1148,16 @@
         shape((zs, 2, 4) + w_out.shape, low),
         shape((2, 4) + dy.shape, low),
         shape((2, 4, many, D), low),
+        shape(rest.shape, low),
+        shape((zs - 1,) + rest.shape, low),
+        shape((zs - 1,) + last.shape, low),
     ] + [shape(both.shape, low)] * (2 * zs - 2) + [shape(down.shape, low)] * (2 * zs - 2)
     out_here = [shape((many, D), t) for t in (low, low, low, full)] + [shape((8, D), full)] + [shape((many, 128), full)] * 2
     sem = pltpu.SemaphoreType.DMA
     found = pl.pallas_call(
         functools.partial(forward_kernel, zs, micro),
         out_shape=out_any + out_here,
-        in_specs=[smem, here, smem] + [here] * 2 + [anywhere] * 5,
+        in_specs=[smem, here, smem] + [here] * 2 + [anywhere] * 7,
         out_specs=[anywhere] * len(out_any) + [here] * len(out_here),
         scratch_shapes=[
             pltpu.VMEM((2, 2, 4) + pack.shape, low),
@@ -986,20 +1169,21 @@
             pltpu.VMEM((zs, 2, 4) + w_out.shape, low),
             pltpu.VMEM((many, D), low),
             sem((4,)),
-        ] + EXCHANGE_SEMS + [sem((2 * zs - 2, 2))] * 2 + gather_sems(zs, True) * 3 + gather_sems(zs, False) * 2,
+        ] + EXCHANGE_SEMS * 2 + [sem((2, zs - 1, 2))] + [sem((2 * zs - 2, 2))] * 2 + gather_sems(zs, True) * 3 + gather_sems(zs, False) * 2,
         compiler_params=pltpu.CompilerParams(
             collective_id=collective_id, has_side_effects=True, vmem_limit_bytes=56 * MIB
         ),
         cost_estimate=LONG,
-    )(order, places_of(order, many // micro), first, freq.reshape(1, 128), tokens, pack, both, down, w_out, dy)
+    )(order, places_of(order, many // micro), first, freq.reshape(1, 128), tokens, pack, both, down, w_out, dy, rest, last)
     return found
 
 
 def back_kernel(zs, micro, *refs):
     (order_ref, places_ref, first_ref, dy_ref, middle_ref, gains_ref, q_ref, cos_ref, sin_ref) = refs[:9]
-    dx_part, out_part, both_part, down_part, out_all, kv_all = refs[9:15]
-    result_ref, d_middle_ref, dq_ref, dkv_ref, gain_ref, down_ref, both_up, both_down = refs[15:23]
-    out_w, kv_here, d_heads, chosen, window, bias, d_places, sems, got, held, d_sems, dl_sem, b_sems, *more = refs[23:]
+    dx_part, out_part, both_part, down_part, out_all, kv_all, rest_part, last_part, *come = refs[9:21]
+    result_ref, d_middle_ref, dq_ref, dkv_ref, gain_ref, down_ref, both_up, both_down, rest_in, last_in = refs[21:31]
+    out_w, kv_here, d_heads, chosen, window, bias, d_places, sems, got, held, d_sems, dl_sem, *more = refs[31:]
+    b_got, b_held, b_sems, bl_sem, r_sems, *more = more
     low, full = jnp.bfloat16, jnp.float32
     z, c, r = place()
     many = dy_ref.shape[0]
@@ -1017,27 +1201,40 @@
         "dx": Scatter(1, False, True, dx_part, take_d_ffn, *more[:SCATTER_REFS]),
         "out": Scatter(1, False, True, out_part, take_result, *more[SCATTER_REFS : 2 * SCATTER_REFS]),
     }
-    down = SumChain(zs, down_part, got, held, d_sems, dl_sem)
-    lines = [
-        Line(zs, 1, 0, 1, both_part.at[lax.rem(z + zs - 1, zs)], both_up, b_sems.at[0]),
-        Line(zs, -1, zs - 1, zs, both_part.at[lax.rem(z + 1, zs)], both_down, b_sems.at[1]),
+    down = SumChain(zs, down_part, [got.at[n] for n in range(2 * zs - 2)], held, d_sems, dl_sem)
+    none = [None] * (zs - 3)
+    both = SumChain(
+        zs, both_part, [b_got.at[0], both_up, *none, b_got.at[1], both_down, *none], b_held, b_sems, bl_sem
+    )
+    arounds = [
+        Around(zs, lambda k: rest_part.at[lax.rem(z + k, zs)], rest_in, r_sems.at[0]),
+        Around(zs, lambda k: last_part.at[lax.rem(z + k, zs)], last_in, r_sems.at[1]),
     ]
+    comes = [
+        pltpu.make_async_copy(src, dst, sems.at[2 + n])
+        for n, (src, dst) in enumerate(zip(come, (b_got.at[0], b_got.at[1], got.at[0], got.at[zs - 1])))
+    ]
+    for copy in comes:
+        copy.start()
+    both.fetch(2)
+    down.fetch(2)
     schedule = [(0, 3), (0, 1), (0, 2), (0, 0)]
     scatters["dx"].begin(schedule)
-    down.start(1)
-    for line in lines:
-        line.start()
+    for one in arounds:
+        one.start()
     loads = [pltpu.make_async_copy(out_all, out_w, sems.at[0]), pltpu.make_async_copy(kv_all, kv_here, sems.at[1])]
     for load in loads:
         load.start()
     scatters["dx"].stage_a(0)
+    for copy in comes:
+        copy.wait()
+    both.start(2)
+    down.start(2)
     scatters["out"].begin(schedule)
     scatters["dx"].stage_b(0)
     scatters["out"].stage_a(0)
     scatters["dx"].stage_c(0)
     scatters["out"].stage_b(0)
-    down.finish()
-    down.start(2)
 
     gain_ref[0:1, :] = jnp.zeros((1, D), full)
 
@@ -1101,6 +1298,7 @@
         return carry
 
     lax.fori_loop(0, micro, attend_some, 0)
+    both.finish()
     down.finish()
     down.start(3)
     lax.fori_loop(micro, 2 * micro, attend_some, 0)
@@ -1108,14 +1306,14 @@
     down.finish()
     down.total()
     down_ref[...] = held[0].astype(full)
-    for line in lines:
-        line.finish()
+    for one in arounds:
+        one.finish()
     for one in scatters.values():
         one.end()
 
 
 def back(order, first, dy, middle, gains, queries, cosine, sine, dx_part, out_part, both_part, down_part, out_all, kv_all,
-         zs, collective_id):
+         rest_part, last_part, come, zs, collective_id):
     many = dy.shape[0]
     micro = first.shape[0]
     span = many // micro
@@ -1130,9 +1328,10 @@
         out_shape=[
             shape((many, D), low), shape((many, D), full), shape((many, D), low), shape(kv_all.shape, low),
             shape((8, D), full), shape((unit, D), full), piece, piece,
+            shape((zs - 1,) + rest_part.shape[1:], low), shape((zs - 1,) + last_part.shape[1:], low),
         ],
-        in_specs=[smem, here, smem] + [here] * 6 + [anywhere] * 6,
-        out_specs=[here] * 6 + [anywhere] * 2,
+        in_specs=[smem, here, smem] + [here] * 6 + [anywhere] * 12,
+        out_specs=[here] * 6 + [anywhere] * 4,
         scratch_shapes=[
             pltpu.VMEM(out_all.shape, low),
             pltpu.VMEM(kv_all.shape, low),
@@ -1141,25 +1340,29 @@
             pltpu.VMEM((wide, 2 * KVW), low),
             pltpu.VMEM((wide, GROUP * span // 2), full),
             pltpu.VMEM((2 * wide, 2 * KVW), full),
-            sem((2,)),
+            sem((6,)),
             pltpu.VMEM((2 * zs - 2, unit, D), low),
             pltpu.VMEM((2, unit, D), low),
-            sem((2 * zs - 2, 2)), sem((2,)), sem((2, 2)),
+            sem((2 * zs - 2, 2)), sem((2,)),
+            pltpu.VMEM((2,) + piece.shape, low),
+            pltpu.VMEM((2,) + piece.shape, low),
+            sem((2 * zs - 2, 2)), sem((2,)), sem((2, zs - 1, 2)),
         ] + scatter_scratch(1, True, many, D, True) * 2,
         compiler_params=pltpu.CompilerParams(
             collective_id=collective_id, has_side_effects=True, vmem_limit_bytes=62 * MIB
         ),
         cost_estimate=LONG,
     )(order, places_of(order, span), first, dy, middle, gains, queries, cosine, sine, dx_part, out_part, both_part, down_part,
-      out_all, kv_all)
+      out_all, kv_all, rest_part, last_part, *come)
 
 
 def weights_kernel(zs, *refs):
     x_ref, attn_ref, d_middle_ref, d_attn_ref, gains_ref, gain_two_ref, cos_ref, sin_ref, dkv_ref = refs[:9]
-    packed, both_part, both_up, both_down, g_out, g_query = refs[9:15]
-    x_grad_ref, out_ref, query_ref, pack_ref, moved_ref = refs[15:20]
-    kv_w, d_kv, pack_g, sems, got, held, b_sems, bl_sem, *more = refs[20:]
-    exchange_sems, more = more[:3], more[3:]
+    packed, both_part, both_up, both_down, g_out, g_query, rest_part, last_part, rest_in, last_in = refs[9:19]
+    x_grad_ref, out_ref, query_ref, pack_ref, last_ref, moved_ref, rest_ref = refs[19:26]
+    kv_w, d_kv, pack_g, sems, got, held, b_sems, bl_sem, rest_here, last_here, *more = refs[26:]
+    exchange_sems, rest_sems, more = more[:3], more[3:6], more[6:]
+    z = place()[0]
     low, full = jnp.bfloat16, jnp.float32
     greet(neighbours(zs, True, True))
 
@@ -1185,15 +1388,24 @@
     items += [("pack", k) for k in range(2, zs)] + [("out", 0), ("query", 0), ("pack", 0)]
     rounds, schedules = scatter_plan(items)
 
-    chain = SumChain(zs, both_part, got, held, b_sems, bl_sem)
+    none = [None] * (zs - 3)
+    chain = SumChain(zs, both_part, [*none, got.at[0], got.at[1], *none, got.at[2], got.at[3]], held, b_sems, bl_sem)
     loads = [
         pltpu.make_async_copy(both_up, got.at[0], sems.at[0]),
-        pltpu.make_async_copy(both_down, got.at[zs - 1], sems.at[1]),
+        pltpu.make_async_copy(both_down, got.at[2], sems.at[1]),
         pltpu.make_async_copy(packed.at[:, :, :, :, pl.ds(D, 2 * KVW)], kv_w, sems.at[2]),
     ]
     for load in loads:
         load.start()
-    chain.fetch(2)
+    small = [
+        pltpu.make_async_copy(rest_part.at[z], rest_here.at[0], sems.at[3]),
+        pltpu.make_async_copy(last_part.at[z], last_here.at[0], sems.at[4]),
+        pltpu.make_async_copy(rest_in, rest_here.at[pl.ds(1, zs - 1)], sems.at[5]),
+        pltpu.make_async_copy(last_in, last_here.at[pl.ds(1, zs - 1)], sems.at[6]),
+    ]
+    for load in small:
+        load.start()
+    chain.fetch(zs - 1)
     pairs.begin([])
     scatters["out"].begin(schedules["out"])
     scatters["query"].begin(schedules["query"])
@@ -1201,7 +1413,13 @@
         pairs.stage_c(k)
     for load in loads:
         load.wait()
-    chain.start(2)
+    chain.start(zs - 1)
+    for load in small:
+        load.wait()
+    last_ref[...] = sum(last_here[n].astype(full) for n in range(zs))
+    rest_here[0] = sum(rest_here[n].astype(full) for n in range(zs)).astype(low)
+    rest = Exchange(rest_here.at[0], rest_ref, *rest_sems)
+    rest.start()
 
     def keys_and_norm():
         pairs.stage_c(0)
@@ -1227,24 +1445,22 @@
     for n, stages in enumerate(rounds):
         if n == 3:
             keys_and_norm()
-        if n == 6:
-            chain.finish()
-            chain.start(3)
-        if n == len(rounds) - 1:
+        if n == len(rounds) - 3:
             chain.finish()
             chain.total()
             exchange = Exchange(held.at[0], moved_ref, *exchange_sems)
             exchange.start()
         for stage in stages:
             run_stage(scatters, *stage)
-    exchange.finish()
-    exchange.end()
+    for one in (rest, exchange):
+        one.finish()
+        one.end()
     for one in (pairs, *scatters.values()):
         one.end()
 
 
 def weight_sums(x, attn_in, d_middle, d_attn, gains, gain_two, cosine, sine, d_kv, packed, both_part, both_up, both_down, g_out,
-                g_query, zs, collective_id):
+                g_query, rest_part, last_part, rest_in, last_in, zs, collective_id):
     many = x.shape[0]
     low, full = jnp.bfloat16, jnp.float32
     anywhere, here = (pl.BlockSpec(memory_space=m) for m in (pl.ANY, pltpu.VMEM))
@@ -1255,19 +1471,22 @@
     return pl.pallas_call(
         functools.partial(weights_kernel, zs),
         out_shape=[
-            shape((many, D), low), shape((wide, D), full), shape((wide, D), full), shape((wide, narrow), full), shape(block, low),
+            shape((many, D), low), shape((wide, D), full), shape((wide, D), full), shape((wide, narrow), full),
+            shape(last_part.shape[1:], full), shape(block, low), shape(rest_part.shape[1:], low),
         ],
-        in_specs=[here] * 9 + [anywhere] * 6,
-        out_specs=[here] * 4 + [anywhere],
+        in_specs=[here] * 9 + [anywhere] * 10,
+        out_specs=[here] * 5 + [anywhere] * 2,
         scratch_shapes=[
             pltpu.VMEM(packed.shape[:4] + (2 * KVW,), low),
             pltpu.VMEM((many, 2 * KVW), full),
             pltpu.VMEM((zs, 2, 4, wide, narrow), low),
-            sem((3,)),
-            pltpu.VMEM((2 * zs - 2,) + block, low),
+            sem((7,)),
+            pltpu.VMEM((4,) + block, low),
             pltpu.VMEM((2,) + block, low),
             sem((2 * zs - 2, 2)), sem((2,)),
-        ] + EXCHANGE_SEMS
+            pltpu.VMEM(rest_part.shape, low),
+            pltpu.VMEM(last_part.shape, low),
+        ] + EXCHANGE_SEMS * 2
         + scatter_scratch(zs, False, many, 2 * KVW, False)
         + scatter_scratch(zs, True, wide, D, True) * 2
         + scatter_scratch(zs, True, wide, narrow, False),
@@ -1276,7 +1495,7 @@
         ),
         cost_estimate=LONG,
     )(x, attn_in, d_middle, d_attn, gains, gain_two, cosine, sine, d_kv, packed, both_part, both_up, both_down, g_out,
-      g_query)
+      g_query, rest_part, last_part, rest_in, last_in)
 
 
 class Links:
@@ -1320,8 +1539,9 @@
     wide = w_gate.shape[0]
     unit = w_down.shape[0]
 
-    both = spread(w_gate, w_up, zs, rows)
-    flat = (2 * rows * wide, 2 * zs * unit)
+    both, rest = spread(w_gate, w_up, zs, rows)
+    cut = split_unit(unit)
+    flat, flat_rest = (2 * rows * wide, 2 * zs * cut), (2 * rows * wide, 2 * zs * (unit - cut))
     gains = jnp.pad(jnp.stack([gain_attn, gain_ffn], axis=1), ((0, 0), (0, 126)))
     pack = jnp.concatenate([w_query, w_key, w_value, gains], axis=1)
     dy_own = cotangent.reshape(many, D)
@@ -1331,15 +1551,19 @@
     slot_of = jnp.argmax(order[None, :] == jnp.arange(order.shape[0], dtype=jnp.int32)[:, None], axis=1).astype(jnp.int32)
     chained = links.kernels
     if chained:
-        found = forward(order, first, own_tokens, pack, both, w_down, w_out, dy_own, zs, 0)
-        packed, both_own, kv, out_w, dy, ffn_in = found[:6]
-        both_w = [b.reshape(flat) for b in (both_own, *found[6 : 4 + 2 * zs])]
-        down_w = [w_down, *found[4 + 2 * zs : 2 + 4 * zs]]
-        queries, attn_in, attended, middle, gains, cosine, sine = found[2 + 4 * zs :]
+        down_own, last_own = w_down[:cut], w_down[cut:]
+        found = forward(order, first, own_tokens, pack, both, rest, down_own, last_own, w_out, dy_own, zs, 0)
+        packed, both_own, kv, out_w, dy, ffn_in, rest_own, rest_got, last_got = found[:9]
+        both_w = [b.reshape(flat) for b in (both_own, *found[9 : 7 + 2 * zs])]
+        down_w = [down_own, *found[7 + 2 * zs : 5 + 4 * zs]]
+        rest_w = [rest_own.reshape(flat_rest), rest_got.reshape(zs - 1, *flat_rest)]
+        last_w = [last_own, last_got]
+        queries, attn_in, attended, middle, gains, cosine, sine = found[5 + 4 * zs :]
         packed = packed.reshape(D, PACK)
     else:
         both_w = [links.gather_z(links.exchange_xla(both).reshape(flat))]
-        down_w = [links.gather_z(w_down)]
+        rest_w = [links.gather_z(links.exchange_xla(rest).reshape(flat_rest))]
+        down_w, last_w = [links.gather_z(w_down[:cut])], [links.gather_z(w_down[cut:])]
         packed, dy = links.gather(pack, True, True).reshape(D, PACK), links.gather(dy_own, False, True)
         gain_one, gain_two = packed[:, QKV].astype(jnp.float32), packed[:, QKV + 1].astype(jnp.float32)
         mine = slot_places(order, half_len, lax.axis_index("seq") * span + jnp.arange(span, dtype=jnp.int32))
@@ -1360,29 +1584,39 @@
     dy = dy.reshape(2 * rows * many, D)
 
     ffn_in = ffn_in.reshape(2 * rows * many, D)
-    result_part, d_ffn_part, grad_both, grad_down = feed_forward(ffn_in, dy, both_w, down_w, zs)
     shards = (zs, 2, rows, wide)
-    grad_both = grad_both.reshape(*shards, 2 * zs * unit)
-    grad_down = grad_down.reshape(zs, unit, D)
+    if chained:
+        hidden, d_both, grad_both, grad_down = ffn_first(ffn_in, dy, both_w, down_w, zs)
+        grad_both, grad_down = grad_both.reshape(*shards, 2 * zs * cut), grad_down.reshape(zs, cut, D)
+        result_part, d_ffn_part, grad_rest, grad_last, *come = ffn_second(
+            ffn_in, dy, hidden, d_both, (both_w, down_w), (rest_w, last_w), zs, (grad_both, grad_down), 1
+        )
+    else:
+        hidden, d_both, grad_both, grad_down = ffn_first(ffn_in, dy, both_w, down_w, zs)
+        grad_both, grad_down = grad_both.reshape(*shards, 2 * zs * cut), grad_down.reshape(zs, cut, D)
+        result_part, d_ffn_part, grad_rest, grad_last = ffn_second(
+            ffn_in, dy, hidden, d_both, (both_w, down_w), (rest_w, last_w), zs
+        )
+    grad_rest, grad_last = grad_rest.reshape(*shards, 2 * zs * (unit - cut)), grad_last.reshape(zs, unit - cut, D)
     d_ffn_part, result_part = (part.reshape(2, rows, many, D) for part in (d_ffn_part, result_part))
     if chained:
         out_all, kv_all = out_w.reshape(*shards, D), kv.reshape(zs, 2, many, 2 * KVW)
-        result, d_middle, d_query, d_kv, gain_two_grad, grad_down, both_up, both_down = back(
+        result, d_middle, d_query, d_kv, gain_two_grad, grad_down, both_up, both_down, rest_in, last_in = back(
             order, first, dy_own, middle, gains, queries, cosine, sine, d_ffn_part, result_part, grad_both, grad_down,
-            out_all, kv_all, zs, 1,
+            out_all, kv_all, grad_rest, grad_last, come, zs, 2,
         )
         grad_out = product_tn(attended, d_middle.astype(low)).astype(low).reshape(*shards, D)
         grad_query = product_tn(attn_in, d_query).astype(low).reshape(*shards, D)
         d_attn = product_nt(d_query, packed[:, :D])
-        x_grad, grad_out, grad_query, pack_grad, grad_both = weight_sums(
+        x_grad, grad_out, grad_query, pack_grad, grad_last, grad_both, grad_rest = weight_sums(
             own_tokens, attn_in, d_middle, d_attn, gains, gain_two_grad, cosine, sine, d_kv, packed.reshape(*shards, PACK),
-            grad_both, both_up, both_down, grad_out, grad_query, zs, 2,
+            grad_both, both_up, both_down, grad_out, grad_query, grad_rest, grad_last, rest_in, last_in, zs, 3,
         )
     else:
         d_ffn_in = links.scatter(d_ffn_part, False, True)
         result = (middle + links.scatter(result_part, False, True)).astype(low)
-        grad_both = links.exchange_xla(links.scatter_z(grad_both)[0])
-        grad_down = links.scatter_z(grad_down)[0].astype(jnp.float32)
+        grad_both, grad_rest = (links.exchange_xla(links.scatter_z(grad)[0]) for grad in (grad_both, grad_rest))
+        grad_down, grad_last = (links.scatter_z(grad)[0].astype(jnp.float32) for grad in (grad_down, grad_last))
         factor_two = rms_factor(middle)
         d_part, grad_gain_two = norm_back(d_ffn_in, middle * factor_two, factor_two, gain_two)
         d_middle = dy_own.astype(jnp.float32) + d_part
@@ -1401,7 +1635,8 @@
         gains_grad = jnp.pad(jnp.stack([grad_gain_one, grad_gain_two], axis=1), ((0, 0), (0, 126)))
         pack_grad = jnp.concatenate([product_tn(attn_in, d_kv), gains_grad], axis=1).astype(low)
         pack_grad = links.scatter(pack_grad.reshape(*shards, 2 * KVW + 128), True, True)
-    grad_gate, grad_up = collect(grad_both, zs, rows, unit)
+    grad_gate, grad_up = collect((grad_both, grad_rest), zs, rows, unit)
+    grad_down = jnp.concatenate([grad_down, grad_last])
 
     return (
         result.reshape(tokens.shape),

time: 619 us -> 585 us (0.945)
  Pallas kernels: 575 us -> 541 us
    pallas_call x1, Pallas kernels: 162 us -> 112 us  [weight_sums(): pl.pallas_call(functools.partial(weights_kernel, zs), out_shape=[shape((m...]
    pallas_call x1 -> x2, Pallas kernels: 75.2 us -> 92.8 us  [the longest x1 54.2 us: ffn_second(): pl.pallas_call(functools.partial(ffn_second_kernel, zs, counts, linked),...]
where the time goes in v5:
time: 585 us; the launch traced here: 579 us
  Pallas kernels  541 us (92%)
  matrix products  19.1 us (3%)
  local copies, waits for them, and re-layouts  12.2 us (2%)
  other arithmetic  6.01 us (1%)
    pallas_call x1, Pallas kernels, forward(): pl.pallas_call(functools.partial(forward_kernel, zs, micro), out_shape=ou...  220 us
    pallas_call x1, Pallas kernels, weight_sums(): pl.pallas_call(functools.partial(weights_kernel, zs), out_shape=[shape((m...  112 us
    pallas_call x1, Pallas kernels, back(): pl.pallas_call(functools.partial(back_kernel, zs, micro), out_shape=[shap...  109 us
    pallas_call x1, Pallas kernels, ffn_second(): pl.pallas_call(functools.partial(ffn_second_kernel, zs, counts, linked),...  54.2 us
    pallas_call x1, Pallas kernels, ffn_first(): pl.pallas_call(functools.partial(ffn_first_kernel, zs, count), grid=(x.sh...  38.6 us

profile of v5, /device:TPU:8, one launch (start us, length us, event | category | flops | bytes accessed | tf_op | source)
XLA Modules:
  0.0 579.2 jit_solution(13537044440238073651)
XLA Ops:
  0.6 1.3 slice_reduce_fusion.2.refs_2_
  2.0 0.7 pad_maximum_fusion.1
  2.6 0.7 broadcast_multiply_fusion
  3.3 0.5 fusion.8.refs_3_
  3.8 0.1 iota_add_fusion
  3.9 0.7 add.48.refs_1_
  4.6 0.1 copy.32
  4.7 1.6 slice.26.refs_11_.refs_20_
  6.3 1.7 fusion.4.refs_5_
  8.0 1.9 slice.25.refs_7_.refs_9_.refs_11_
  9.9 3.4 shard_map.212
  13.3 220.4 %shard_map.213 = (bf16[4,2,4,64,2688]{4,3,2,1,0:T(8,128)(2,1)}, bf16[2,4,64,1024]{3,2,1,0:T(8,128)(2,1)}, bf16[4,2,256,512]{3,2,1,0:T(8,128)(2,1)}, bf16[4,2,4,6...) custom-call(s32[16]{0:T(128)} %refs_0_.3, ...), custom_call_target="tpu_custom_call" | custom-call | flops 49999998976 | bytes 157286400 | tf_op jit(solution)/shard_map/pallas_call | solution.py:1157
  233.7 38.6 %shard_map.214 = (bf16[2048,512]{1,0:T(8,128)(2,1)}, bf16[2048,1024]{1,0:T(8,128)(2,1)}, bf16[2048,1024]{1,0:T(8,128)(2,1)}, bf16[512,2048]{1,0:T(8,128)(2,1)}) custom-call(bf16[2048,2048]{1,0:T(8,128)(2,1)} %bitcast.47, bf16[2048,2048]{1,0:T(8,128)(2,1)} %bitcast.45, bf16[512,1024]{1,0:T(8,128)(2,1)} %bitcast.59, bf16[512,1024]{1,0:T(8,128)(2,1)} %bitcast.61, ...), custom_call_target="tpu_custom_call" | custom-call | flops 49999998976 | bytes 157286400 | tf_op jit(solution)/shard_map/pallas_call | solution.py:840
  272.3 54.2 %shard_map.215 = (bf16[2048,2048]{1,0:T(8,128)(2,1)}, bf16[2048,2048]{1,0:T(8,128)(2,1)}, bf16[2048,384]{1,0:T(8,128)(2,1)}, bf16[192,2048]{1,0:T(8,128)(2,1)}, ...) custom-call(bf16[2048,2048]{1,0:T(8,128)(2,1)} %bitcast.48, ...), custom_call_target="tpu_custom_call" | custom-call | flops 49999998976 | bytes 157286400 | tf_op jit(solution)/shard_map/pallas_call | solution.py:869
  326.5 108.8 %shard_map.216 = (bf16[256,2048]{1,0:T(8,128)(2,1)}, f32[256,2048]{1,0:T(8,128)}, bf16[256,2048]{1,0:T(8,128)(2,1)}, bf16[4,2,256,512]{3,2,1,0:T(8,128)(2,1)}, f...) custom-call(s32[16]{0:T(128)} %refs_0_.3, ...), custom_call_target="tpu_custom_call" | custom-call | flops 49999998976 | bytes 157286400 | tf_op jit(solution)/shard_map/pallas_call | solution.py:1326
  435.3 0.0 copy-start.2
  435.3 0.0 copy-start.3
  435.3 7.6 %fusion.refs_3_ = f32[256,2048]{1,0:T(8,128)} fusion(bf16[256,2048]{1,0:T(8,128)(2,1)} %get-tuple-element.114, bf16[2048,2688]{1,0:T(8,128)(2,1)} %bitcast.44), kind=kOutput, calls=%fused_computation | convolution fusion | flops 2147483648 | bytes 11534336 | tf_op jit(solution)/shard_map/dot_general | solution.py:31
  442.9 0.0 copy-done.2
  442.9 0.0 copy-done.3
  442.9 5.7 convolution_convert_fusion
  448.6 5.8 %convolution_convert_fusion.1 = bf16[2048,2048]{1,0:T(8,128)(2,1)} fusion(bf16[256,2048]{1,0:T(8,128)(2,1)S(1)} %copy-done.1, f32[256,2048]{1,0:T(8,128)S(1)} %copy-done), kind=kOutput, calls=%fused_computation.3 | convolution fusion | flops 2152202240 | bytes 11534336 | tf_op jit(solution)/shard_map/dot_general | solution.py:35
  454.4 112.0 %shard_map.217 = (bf16[256,2048]{1,0:T(8,128)(2,1)}, f32[64,2048]{1,0:T(8,128)}, f32[64,2048]{1,0:T(8,128)}, f32[64,640]{1,0:T(8,128)}, f32[48,2048]{1,0:T(8,128...) custom-call(bf16[256,2048]{1,0:T(8,128)(2,1)} %bitcast.41, ...), custom_call_target="tpu_custom_call" | custom-call | flops 49999998976 | bytes 157286400 | tf_op jit(solution)/shard_map/pallas_call | solution.py:1471
  566.5 1.5 slice_reduce_fusion
  568.0 1.5 fusion.9
  569.5 2.3 pad_maximum_fusion
  571.9 3.6 shard_map.218
  575.4 0.0 copy-done.4
  575.4 1.0 copy.39
  576.4 1.0 copy.40
  577.4 0.8 copy.41
  578.2 0.8 copy.42
  (13 shorter events, 0.0 us)
Async XLA Ops:
  435.3 7.6 %copy-start.2 = (bf16[256,2048]{1,0:T(8,128)(2,1)S(1)}, bf16[256,2048]{1,0:T(8,128)(2,1)}, u32[]{:S(2)}) copy-start(bf16[256,2048]{1,0:T(8,128)(2,1)} %get-tuple-element.112.refs_1_) | copy-start | bytes 3145732
  435.3 7.6 %copy-start.3 = (bf16[256,2048]{1,0:T(8,128)(2,1)S(1)}, bf16[256,2048]{1,0:T(8,128)(2,1)}, u32[]{:S(2)}) copy-start(bf16[256,2048]{1,0:T(8,128)(2,1)} %get-tuple-element.114) | copy-start | bytes 3145732
  442.9 5.7 copy-start
  442.9 5.7 copy-start.1
  454.4 115.1 %copy-start.6 = (f32[128,2048]{1,0:T(8,128)S(1)}, f32[128,2048]{1,0:T(8,128)}, u32[]{:S(2)}) copy-start(f32[128,2048]{1,0:T(8,128)} %get-tuple-element.131) | copy-start | bytes 3145732
  569.5 5.9 %copy-start.4 = (bf16[256,2048]{1,0:T(8,128)(2,1)S(1)}, bf16[256,2048]{1,0:T(8,128)(2,1)}, u32[]{:S(2)}) copy-start(bf16[256,2048]{1,0:T(8,128)(2,1)} %get-tuple-element.111) | copy-start | bytes 3145732
  571.9 4.5 copy-start.5
  575.4 2.0 copy-start.8
  575.4 2.7 copy-start.7

commit v6 on v5

--- a/solution.py
+++ b/solution.py
@@ -196,9 +196,16 @@
             src = self.part(src, j)
         return send(src, dst, self.h_ssem.at[k, j - 1], self.h_rsem.at[k, j - 1], (self.s, self.line[3 - j]))
 
+    def twin_copy(self, k, j, src):
+        dst = self.slot(k, 0, j) if self.z_flag else self.out.at[1, j]
+        return send(src, dst, self.c_ssem.at[k, j], self.c_rsem.at[k, j], self.twin)
+
     def to_twin(self, k, j, src):
-        dst = self.slot(k, 0, j) if self.z_flag else self.out.at[1, j]
-        self.start(send(src, dst, self.c_ssem.at[k, j], self.c_rsem.at[k, j], self.twin))
+        self.start(self.twin_copy(k, j, src))
+
+    def from_twin(self, k, j):
+        dst = self.slot(k, 1, j)
+        send(dst, dst, self.c_ssem.at[k, j], self.c_rsem.at[k, j], self.twin).wait_recv()
 
     def launch(self):
         self.local = pltpu.make_async_copy(self.own, self.slot(0, 0, 0), self.l_sem)
@@ -243,8 +250,14 @@
         if n == 0:
             self.local.wait()
         for j in range(4 if self.planes else 1):
-            dst = self.slot(k, 1, j)
-            send(dst, dst, self.c_ssem.at[k, j], self.c_rsem.at[k, j], self.twin).wait_recv()
+            self.from_twin(k, j)
+
+    def sent_all(self):
+        for j in (1, 2):
+            self.near(0, j, self.own).wait_send()
+            self.far(0, j, self.slot(0, 0, j)).wait_send()
+        for j in range(4):
+            self.twin_copy(0, j, self.slot(0, 0, j) if j else self.own).wait_send()
 
     def end(self):
         for goes, copy in self.sent:
@@ -502,6 +515,15 @@
     ahead = pltpu.roll(tensor, lanes - half, tensor.ndim - 1)
     behind = pltpu.roll(tensor, half, tensor.ndim - 1)
     return jnp.where(lax.rem(lane, HEAD_DIM) < half, ahead, behind)
+
+
+def first_of(my_block, half_blocks):
+    return jnp.where(my_block >= half_blocks, half_blocks, 0)
+
+
+def chosen_slots(places, first_block, half_len, wide):
+    wanted = first_block * half_len + lax.broadcasted_iota(jnp.int32, (wide, 2 * wide), 0)
+    return jnp.where(places == wanted, 1.0, 0.0).astype(jnp.bfloat16)
 
 
 def stack_heads(block, first):
@@ -736,21 +758,51 @@
         copy.wait()
 
 
-def ffn_first_kernel(zs, count, *refs):
+def ffn_first_kernel(zs, count, linked, *refs):
     x_ref, dy_ref = refs[:2]
     both_pieces, down_pieces = refs[2 : 2 + count], refs[2 + count : 2 + 2 * count]
-    hidden_ref, d_both_ref, g_both_ref, g_down_ref, both_w, down_w, both_sum, down_sum, sem = refs[2 + 2 * count :]
+    refs = refs[2 + 2 * count :]
+    if linked:
+        rest_own, last_own, x_out_ref, rest_got, last_got, *refs = refs
+    hidden_ref, d_both_ref, g_both_ref, g_down_ref, both_w, down_w, both_sum, down_sum, sem, *more = refs
     step, last = pl.program_id(0), pl.num_programs(0) - 1
+    gathered, arounds = None, []
+    if linked:
+        x_all, a_sems, *g_sems = more
+        gathered = Gather(zs, False, True, x_ref, x_all, *g_sems)
+        arounds = [
+            Around(zs, lambda k: rest_own, rest_got, a_sems.at[0]), Around(zs, lambda k: last_own, last_got, a_sems.at[1])
+        ]
 
     @pl.when(step == 0)
     def _():
         copies = assemble(zs, both_pieces, both_w, sem.at[0]) + assemble(zs, down_pieces, down_w, sem.at[1])
+        if linked:
+            greet(neighbours(zs, True, False))
+            gathered.launch()
+            gathered.begin(0)
+            for one in arounds:
+                one.start()
         both_sum[...] = jnp.zeros_like(both_sum)
         down_sum[...] = jnp.zeros_like(down_sum)
         for copy in copies:
             copy.wait()
-
-    x, dy = x_ref[...], dy_ref[...]
+        if linked:
+            gathered.local.wait()
+
+    if linked:
+        waits = [
+            lambda: gathered.from_twin(0, 0), lambda: gathered.forward(0), lambda: gathered.from_twin(0, 1), None,
+            lambda: gathered.from_twin(0, 2), lambda: gathered.finish(0), lambda: gathered.from_twin(0, 3),
+        ]
+        for n, wait in enumerate(waits):
+            if wait is not None:
+                pl.when(step == n + 1)(wait)
+        x = x_all[lax.rem(step, 2), lax.div(step, 2)]
+        x_out_ref[...] = x
+    else:
+        x = x_ref[...]
+    dy = dy_ref[...]
     hidden, d_both = swiglu(product(x, both_w[...]), product_nt(dy, down_w[...]))
     hidden_ref[...] = hidden
     d_both_ref[...] = d_both
@@ -759,6 +811,10 @@
     @pl.when(step == last)
     def _():
         put_gradients((both_sum, down_sum), (both_w, down_w), (g_both_ref, g_down_ref), sem)
+        for one in arounds:
+            one.finish()
+        if linked:
+            gathered.sent_all()
 
 
 def ffn_second_kernel(zs, counts, linked, *refs):
@@ -828,28 +884,39 @@
             line.finish()
 
 
-def ffn_first(x, dy, both_pieces, down_pieces, zs):
+def ffn_first(x, dy, both_pieces, down_pieces, zs, others=(), collective_id=None):
     count, n = len(both_pieces), down_pieces[0].shape[0] * (zs if len(down_pieces) > 1 else 1)
     block, low, full = 256, jnp.bfloat16, jnp.float32
     sem, shape = pltpu.SemaphoreType.DMA, jax.ShapeDtypeStruct
     anywhere = pl.BlockSpec(memory_space=pl.ANY)
+    linked = bool(others)
+    total = dy.shape[0]
 
     def tokens(width):
+        if linked:
+            return pl.BlockSpec((block, width), lambda i: (i % 2 * 4 + i // 2, 0))
         return pl.BlockSpec((block, width), lambda i: (i, 0))
 
+    extra_specs, extra_shapes, extra_scratch, params = [], [], [], {}
+    if linked:
+        extra_specs = [tokens(D)] + [anywhere] * 2
+        extra_shapes = [shape(dy.shape, low)] + [shape((zs - 1,) + other.shape, low) for other in others]
+        extra_scratch = [pltpu.VMEM((2, 4) + x.shape, low), sem((2, zs - 1, 2))] + gather_sems(zs, False)
+        params = dict(collective_id=collective_id, has_side_effects=True)
     return pl.pallas_call(
-        functools.partial(ffn_first_kernel, zs, count),
-        grid=(x.shape[0] // block,),
-        in_specs=[tokens(D)] * 2 + [anywhere] * (2 * count),
-        out_specs=[tokens(n), tokens(2 * n)] + [anywhere] * 2,
-        out_shape=[shape((x.shape[0], n), low), shape((x.shape[0], 2 * n), low), shape((D, 2 * n), low), shape((n, D), low)],
+        functools.partial(ffn_first_kernel, zs, count, linked),
+        grid=(total // block,),
+        in_specs=[anywhere if linked else tokens(D), tokens(D)] + [anywhere] * (2 * count + len(others)),
+        out_specs=extra_specs + [tokens(n), tokens(2 * n)] + [anywhere] * 2,
+        out_shape=extra_shapes
+        + [shape((total, n), low), shape((total, 2 * n), low), shape((D, 2 * n), low), shape((n, D), low)],
         scratch_shapes=[
             pltpu.VMEM((D, 2 * n), low), pltpu.VMEM((n, D), low), pltpu.VMEM((D, 2 * n), full), pltpu.VMEM((n, D), full),
             sem((2, zs)),
-        ],
-        compiler_params=pltpu.CompilerParams(vmem_limit_bytes=56 * MIB),
+        ] + extra_scratch,
+        compiler_params=pltpu.CompilerParams(vmem_limit_bytes=60 * MIB, **params),
         cost_estimate=LONG,
-    )(x, dy, *both_pieces, *down_pieces)
+    )(x, dy, *both_pieces, *down_pieces, *others)
 
 
 def ffn_second(x, dy, hidden, d_both, one, two, zs, parts=(), collective_id=None):
@@ -931,14 +998,13 @@
 
 
 def forward_kernel(zs, micro, *refs):
-    order_ref, places_ref, first_ref, freq_ref, x_ref, pack_ref, both_ref, down_ref, out_ref, dy_ref, rest_ref, last_ref = refs[:12]
-    refs = refs[2:]
-    packed, both_own, kv_all, out_all, dy_all, ffn_all, rest_own, rest_got, last_got = refs[10:19]
-    refs = refs[3:]
+    order_ref, places_ref, first_ref, freq_ref, x_ref, pack_ref, both_ref, down_ref, out_ref, dy_ref, rest_ref = refs[:11]
+    refs = refs[1:]
+    packed, both_own, kv_all, out_all, dy_all, rest_own = refs[10:16]
     steps = 2 * zs - 2
     both_got, down_got = refs[16 : 16 + steps], refs[16 + steps : 16 + 2 * steps]
-    q_ref, attn_ref, attended_ref, middle_ref, gains_ref, cos_ref, sin_ref = refs[16 + 2 * steps : 23 + 2 * steps]
-    (staged, lin, kv_own, kv_here, window, bias, out_w, ffn_own, sems, *more) = refs[23 + 2 * steps :]
+    q_ref, attn_ref, attended_ref, ffn_own, middle_ref, gains_ref, cos_ref, sin_ref = refs[16 + 2 * steps : 24 + 2 * steps]
+    (staged, lin, kv_own, kv_here, window, chosen, bias, out_w, sems, *more) = refs[24 + 2 * steps :]
     low = jnp.bfloat16
     z, c, r = place()
     many = x_ref.shape[0]
@@ -949,21 +1015,18 @@
 
     exchange = Exchange(both_ref, both_own, *more[:3])
     rest = Exchange(rest_ref, rest_own, *more[3:6])
-    arounds = [Around(zs, lambda k: rest_own, rest_got, more[6].at[0]), Around(zs, lambda k: last_ref, last_got, more[6].at[1])]
-    more = more[:3] + more[7:]
+    more = more[:3] + more[6:]
     both_chain, down_chain = Chain(zs, both_own, both_got, more[3]), Chain(zs, down_ref, down_got, more[4])
     more = more[5:]
     weights = Gather(zs, True, True, pack_ref, packed, *more[:9])
     outs = Gather(zs, True, True, out_ref, out_all, *more[9:18])
     pairs = Gather(zs, True, False, kv_own, kv_all, *more[18:27])
     dys = Gather(zs, False, True, dy_ref, dy_all, *more[27:36])
-    ffns = Gather(zs, False, True, ffn_own, ffn_all, *more[36:45])
 
     weights.launch()
     exchange.start()
     weights.begin(0)
     outs.launch()
-    rest.start()
 
     lane = lax.broadcasted_iota(jnp.int32, (half_len, 128), 1)
     for i in range(2 * micro):
@@ -975,6 +1038,11 @@
         sin_ref[i * half_len : (i + 1) * half_len, :] = jnp.where(lax.rem(lane, HEAD_DIM) < HEAD_DIM // 2, -sine, sine)
     x = x_ref[...].astype(jnp.float32)
     factor = rms_factor(x)
+    wide = window.shape[0]
+    half_blocks = wide // half_len
+    for half in range(2):
+        my_block = order_ref[(z * 2 + c) * 2 + half]
+        chosen[half] = chosen_slots(places_ref[...], first_of(my_block, half_blocks), half_len, wide)
 
     loads = {}
 
@@ -1022,6 +1090,7 @@
     outs.begin(1)
     project(1)
     weights.finish(3)
+    rest.start()
     dys.launch()
     dys.begin(0)
     load(2)
@@ -1049,9 +1118,6 @@
     down_chain.finish()
     both_chain.start(2)
     down_chain.start(2)
-    rest.finish()
-    for one in arounds:
-        one.start()
     for k in range(1, zs):
         pairs.arrive(k)
         pairs.begin(k)
@@ -1066,17 +1132,12 @@
     outs.finish(1)
     kv_load.wait()
 
-    wide = window.shape[0]
-    half_blocks = wide // half_len
-
     def attend_some(i, carry):
         m, half = lax.div(i, 2), lax.rem(i, 2)
         my_block = order_ref[(z * 2 + c) * 2 + half]
-        first_block = jnp.where(my_block >= half_blocks, half_blocks, 0)
-        wanted = first_block * half_len + lax.broadcasted_iota(jnp.int32, (wide, 2 * wide), 0)
-        chosen = jnp.where(places_ref[...] == wanted, 1.0, 0.0).astype(low)
+        first_block = first_of(my_block, half_blocks)
         at = pl.ds(pl.multiple_of(m * span, span), span)
-        window[...] = product(chosen, kv_here[:, :, at, :].reshape(2 * wide, 2 * KVW)).astype(low)
+        window[...] = product(chosen[half], kv_here[:, :, at, :].reshape(2 * wide, 2 * KVW)).astype(low)
         key_place = first_block * half_len + lax.broadcasted_iota(jnp.int32, (half_len, wide), 1)
         place_here = my_block * half_len + lax.broadcasted_iota(jnp.int32, (half_len, wide), 0)
         first = first_ref[m]
@@ -1103,28 +1164,22 @@
         outs.complete(k)
     out_load = pltpu.make_async_copy(out_all, out_w, sems.at[3])
     out_load.start()
-    dys.finish(0)
     out_load.wait()
     middle = x_ref[...].astype(jnp.float32) + product(attended_ref[...], out_w[...].reshape(D, D))
     middle_ref[...] = middle
     ffn_own[...] = (middle * rms_factor(middle) * gains_ref[1:2, :]).astype(low)
-    ffns.launch()
-    ffns.begin(0)
     both_chain.finish()
     down_chain.finish()
     both_chain.start(3)
     down_chain.start(3)
+    dys.finish(0)
     dys.complete(0)
-    ffns.forward(0)
-    ffns.finish(0)
-    ffns.complete(0)
+    rest.finish()
     both_chain.finish()
     down_chain.finish()
-    for one in arounds:
-        one.finish()
     rest.end()
     exchange.end()
-    for one in (weights, outs, pairs, dys, ffns):
+    for one in (weights, outs, pairs, dys):
         one.end()
 
 
@@ -1132,7 +1187,7 @@
     return (order[:, None] * (span // 2) + jnp.arange(span // 2, dtype=jnp.int32)).reshape(1, -1)
 
 
-def forward(order, first, tokens, pack, both, rest, down, last, w_out, dy, zs, collective_id):
+def forward(order, first, tokens, pack, both, rest, down, w_out, dy, zs, collective_id):
     many = tokens.shape[0]
     micro = first.shape[0]
     seq = 2 * zs
@@ -1147,17 +1202,14 @@
         shape((zs, 2, many, 2 * KVW), low),
         shape((zs, 2, 4) + w_out.shape, low),
         shape((2, 4) + dy.shape, low),
-        shape((2, 4, many, D), low),
         shape(rest.shape, low),
-        shape((zs - 1,) + rest.shape, low),
-        shape((zs - 1,) + last.shape, low),
     ] + [shape(both.shape, low)] * (2 * zs - 2) + [shape(down.shape, low)] * (2 * zs - 2)
-    out_here = [shape((many, D), t) for t in (low, low, low, full)] + [shape((8, D), full)] + [shape((many, 128), full)] * 2
+    out_here = [shape((many, D), t) for t in (low, low, low, low, full)] + [shape((8, D), full)] + [shape((many, 128), full)] * 2
     sem = pltpu.SemaphoreType.DMA
     found = pl.pallas_call(
         functools.partial(forward_kernel, zs, micro),
         out_shape=out_any + out_here,
-        in_specs=[smem, here, smem] + [here] * 2 + [anywhere] * 7,
+        in_specs=[smem, here, smem] + [here] * 2 + [anywhere] * 6,
         out_specs=[anywhere] * len(out_any) + [here] * len(out_here),
         scratch_shapes=[
             pltpu.VMEM((2, 2, 4) + pack.shape, low),
@@ -1165,16 +1217,16 @@
             pltpu.VMEM((many, 2 * KVW), low),
             pltpu.VMEM((zs, 2, many, 2 * KVW), low),
             pltpu.VMEM((wide, 2 * KVW), low),
+            pltpu.VMEM((2, wide, 2 * wide), low),
             pltpu.VMEM((many // micro // 2, wide), full),
             pltpu.VMEM((zs, 2, 4) + w_out.shape, low),
-            pltpu.VMEM((many, D), low),
             sem((4,)),
-        ] + EXCHANGE_SEMS * 2 + [sem((2, zs - 1, 2))] + [sem((2 * zs - 2, 2))] * 2 + gather_sems(zs, True) * 3 + gather_sems(zs, False) * 2,
+        ] + EXCHANGE_SEMS * 2 + [sem((2 * zs - 2, 2))] * 2 + gather_sems(zs, True) * 3 + gather_sems(zs, False),
         compiler_params=pltpu.CompilerParams(
             collective_id=collective_id, has_side_effects=True, vmem_limit_bytes=56 * MIB
         ),
         cost_estimate=LONG,
-    )(order, places_of(order, many // micro), first, freq.reshape(1, 128), tokens, pack, both, down, w_out, dy, rest, last)
+    )(order, places_of(order, many // micro), first, freq.reshape(1, 128), tokens, pack, both, down, w_out, dy, rest)
     return found
 
 
@@ -1356,6 +1408,30 @@
       out_all, kv_all, rest_part, last_part, *come)
 
 
+def products_kernel(attended_ref, attn_ref, d_middle_ref, dq_ref, packed_ref, out_ref, query_ref, d_attn_ref):
+    low = jnp.bfloat16
+    out_ref[...] = product_tn(attended_ref[...], d_middle_ref[...].astype(low)).astype(low)
+    query_ref[...] = product_tn(attn_ref[...], dq_ref[...]).astype(low)
+    d_attn_ref[...] = product_nt(dq_ref[...], packed_ref[...])
+
+
+def products(attended, attn_in, d_middle, d_query, packed):
+    many, block = attended.shape[0], 256
+    low, shape = jnp.bfloat16, jax.ShapeDtypeStruct
+    narrow = pl.BlockSpec((many, block), lambda i: (0, i))
+    tall = pl.BlockSpec((block, D), lambda i: (i, 0))
+    whole = pl.BlockSpec((many, D), lambda i: (0, 0))
+    return pl.pallas_call(
+        products_kernel,
+        grid=(D // block,),
+        in_specs=[narrow, narrow, whole, whole, tall],
+        out_specs=[tall, tall, narrow],
+        out_shape=[shape((D, D), low), shape((D, D), low), shape((many, D), jnp.float32)],
+        compiler_params=pltpu.CompilerParams(vmem_limit_bytes=32 * MIB),
+        cost_estimate=pl.CostEstimate(flops=6 * many * D * D, bytes_accessed=30 * MIB, transcendentals=0),
+    )(attended, attn_in, d_middle, d_query, packed)
+
+
 def weights_kernel(zs, *refs):
     x_ref, attn_ref, d_middle_ref, d_attn_ref, gains_ref, gain_two_ref, cos_ref, sin_ref, dkv_ref = refs[:9]
     packed, both_part, both_up, both_down, g_out, g_query, rest_part, last_part, rest_in, last_in = refs[9:19]
@@ -1552,13 +1628,12 @@
     chained = links.kernels
     if chained:
         down_own, last_own = w_down[:cut], w_down[cut:]
-        found = forward(order, first, own_tokens, pack, both, rest, down_own, last_own, w_out, dy_own, zs, 0)
-        packed, both_own, kv, out_w, dy, ffn_in, rest_own, rest_got, last_got = found[:9]
-        both_w = [b.reshape(flat) for b in (both_own, *found[9 : 7 + 2 * zs])]
-        down_w = [down_own, *found[7 + 2 * zs : 5 + 4 * zs]]
-        rest_w = [rest_own.reshape(flat_rest), rest_got.reshape(zs - 1, *flat_rest)]
-        last_w = [last_own, last_got]
-        queries, attn_in, attended, middle, gains, cosine, sine = found[5 + 4 * zs :]
+        found = forward(order, first, own_tokens, pack, both, rest, down_own, w_out, dy_own, zs, 0)
+        packed, both_own, kv, out_w, dy, rest_own = found[:6]
+        both_w = [b.reshape(flat) for b in (both_own, *found[6 : 4 + 2 * zs])]
+        down_w = [down_own, *found[4 + 2 * zs : 2 + 4 * zs]]
+        rest_own = rest_own.reshape(flat_rest)
+        queries, attn_in, attended, ffn_in, middle, gains, cosine, sine = found[2 + 4 * zs :]
         packed = packed.reshape(D, PACK)
     else:
         both_w = [links.gather_z(links.exchange_xla(both).reshape(flat))]
@@ -1578,18 +1653,20 @@
         kv, out_w = links.gather(kv_own, True, False), links.gather(w_out, True, True)
         queries, attended = attend(order, slot_of, first, lin, cosine, sine, kv.reshape(seq, many, 2 * KVW))
         middle = x + product(attended, out_w.reshape(D, D))
-        ffn_in = links.gather((middle * rms_factor(middle) * gain_two).astype(low), False, True)
+        ffn_in = links.gather((middle * rms_factor(middle) * gain_two).astype(low), False, True).reshape(2 * rows * many, D)
     kv = kv.reshape(seq, many, 2 * KVW)
     out_w = out_w.reshape(D, D)
     dy = dy.reshape(2 * rows * many, D)
 
-    ffn_in = ffn_in.reshape(2 * rows * many, D)
     shards = (zs, 2, rows, wide)
     if chained:
-        hidden, d_both, grad_both, grad_down = ffn_first(ffn_in, dy, both_w, down_w, zs)
+        ffn_in, rest_got, last_got, hidden, d_both, grad_both, grad_down = ffn_first(
+            ffn_in, dy, both_w, down_w, zs, (rest_own, last_own), 1
+        )
+        rest_w, last_w = [rest_own, rest_got], [last_own, last_got]
         grad_both, grad_down = grad_both.reshape(*shards, 2 * zs * cut), grad_down.reshape(zs, cut, D)
         result_part, d_ffn_part, grad_rest, grad_last, *come = ffn_second(
-            ffn_in, dy, hidden, d_both, (both_w, down_w), (rest_w, last_w), zs, (grad_both, grad_down), 1
+            ffn_in, dy, hidden, d_both, (both_w, down_w), (rest_w, last_w), zs, (grad_both, grad_down), 2
         )
     else:
         hidden, d_both, grad_both, grad_down = ffn_first(ffn_in, dy, both_w, down_w, zs)
@@ -1603,14 +1680,13 @@
         out_all, kv_all = out_w.reshape(*shards, D), kv.reshape(zs, 2, many, 2 * KVW)
         result, d_middle, d_query, d_kv, gain_two_grad, grad_down, both_up, both_down, rest_in, last_in = back(
             order, first, dy_own, middle, gains, queries, cosine, sine, d_ffn_part, result_part, grad_both, grad_down,
-            out_all, kv_all, grad_rest, grad_last, come, zs, 2,
+            out_all, kv_all, grad_rest, grad_last, come, zs, 3,
         )
-        grad_out = product_tn(attended, d_middle.astype(low)).astype(low).reshape(*shards, D)
-        grad_query = product_tn(attn_in, d_query).astype(low).reshape(*shards, D)
-        d_attn = product_nt(d_query, packed[:, :D])
+        grad_out, grad_query, d_attn = products(attended, attn_in, d_middle, d_query, packed)
+        grad_out, grad_query = grad_out.reshape(*shards, D), grad_query.reshape(*shards, D)
         x_grad, grad_out, grad_query, pack_grad, grad_last, grad_both, grad_rest = weight_sums(
             own_tokens, attn_in, d_middle, d_attn, gains, gain_two_grad, cosine, sine, d_kv, packed.reshape(*shards, PACK),
-            grad_both, both_up, both_down, grad_out, grad_query, grad_rest, grad_last, rest_in, last_in, zs, 3,
+            grad_both, both_up, both_down, grad_out, grad_query, grad_rest, grad_last, rest_in, last_in, zs, 4,
         )
     else:
         d_ffn_in = links.scatter(d_ffn_part, False, True)

time: 585 us -> 573 us (0.979)
  matrix products: 19.1 us -> 0 us
  local copies, waits for them, and re-layouts: 12.2 us -> 21 us
    pallas_call x1 -> x2, Pallas kernels: 38.6 us -> 76.1 us  [the longest x1 63.6 us: ffn_first(): pl.pallas_call(functools.partial(ffn_first_kernel, zs, count, linked), gr...]
    pallas_call x1, Pallas kernels: 220 us -> 183 us  [forward(): pl.pallas_call(functools.partial(forward_kernel, zs, micro), out_shape=ou...]
    dot_general x3 -> x0, matrix products: 19.1 us -> none  [the longest x2 11.5 us: product_tn(): lax.dot_general(left, right, (((0,), (0,)), ((), ())), preferred_element_...]
    unnamed x22 -> x26, local copies, waits for them, and re-layouts: 3.56 us -> 12.4 us
where the time goes in v6:
time: 573 us; the launch traced here: 565 us
  Pallas kernels  537 us (94%)
  local copies, waits for them, and re-layouts  21 us (4%)
  other arithmetic  6.01 us (1%)
    pallas_call x1, Pallas kernels, forward(): pl.pallas_call(functools.partial(forward_kernel, zs, micro), out_shape=ou...  183 us
    pallas_call x1, Pallas kernels, weight_sums(): pl.pallas_call(functools.partial(weights_kernel, zs), out_shape=[shape((m...  111 us
    pallas_call x1, Pallas kernels, back(): pl.pallas_call(functools.partial(back_kernel, zs, micro), out_shape=[shap...  107 us
    pallas_call x1, Pallas kernels, ffn_first(): pl.pallas_call(functools.partial(ffn_first_kernel, zs, count, linked), gr...  63.6 us
    pallas_call x1, Pallas kernels, ffn_second(): pl.pallas_call(functools.partial(ffn_second_kernel, zs, counts, linked),...  51.9 us
    pallas_call x1, Pallas kernels, products(): pl.pallas_call(products_kernel, grid=(D // block,), in_specs=[narrow, nar...  12.5 us
    unnamed x26, local copies, waits for them, and re-layouts  12.4 us

profile of v6, /device:TPU:8, one launch (start us, length us, event | category | flops | bytes accessed | tf_op | source)
XLA Modules:
  0.0 564.9 jit_solution(8697011002748474896)
XLA Ops:
  0.6 1.3 slice_reduce_fusion.2.refs_2_
  2.0 0.7 pad_maximum_fusion.1
  2.6 0.7 broadcast_multiply_fusion
  3.3 0.5 fusion.5.refs_3_
  3.8 0.1 iota_add_fusion
  3.9 0.7 add.48.refs_1_
  4.6 0.1 copy.32
  4.7 1.6 slice.23.refs_17_.refs_20_
  6.3 1.7 fusion.1.refs_5_
  8.0 1.9 slice.22.refs_7_.refs_9_.refs_11_
  9.9 3.4 shard_map.212
  13.3 183.3 %shard_map.213 = (bf16[4,2,4,64,2688]{4,3,2,1,0:T(8,128)(2,1)}, bf16[2,4,64,1024]{3,2,1,0:T(8,128)(2,1)}, bf16[4,2,256,512]{3,2,1,0:T(8,128)(2,1)}, bf16[4,2,4,6...) custom-call(s32[16]{0:T(128)} %refs_0_.3, ...), custom_call_target="tpu_custom_call" | custom-call | flops 49999998976 | bytes 157286400 | tf_op jit(solution)/shard_map/pallas_call | solution.py:1209
  196.6 63.6 %shard_map.214 = (bf16[2048,2048]{1,0:T(8,128)(2,1)}, bf16[3,512,384]{2,1,0:T(8,128)(2,1)}, bf16[3,48,2048]{2,1,0:T(8,128)(2,1)}, bf16[2048,512]{1,0:T(8,128)(2,...) custom-call(bf16[256,2048]{1,0:T(8,128)(2,1)} %get-tuple-element.83.refs_0_, ...), custom_call_target="tpu_custom_call" | custom-call | flops 49999998976 | bytes 157286400 | tf_op jit(solution)/shard_map/pallas_call | solution.py:906
  260.2 51.9 %shard_map.215 = (bf16[2048,2048]{1,0:T(8,128)(2,1)}, bf16[2048,2048]{1,0:T(8,128)(2,1)}, bf16[2048,384]{1,0:T(8,128)(2,1)}, bf16[192,2048]{1,0:T(8,128)(2,1)}, ...) custom-call(bf16[2048,2048]{1,0:T(8,128)(2,1)} %get-tuple-element.99, ...), custom_call_target="tpu_custom_call" | custom-call | flops 49999998976 | bytes 157286400 | tf_op jit(solution)/shard_map/pallas_call | solution.py:936
  312.1 0.0 copy-start.3
  312.1 107.3 %shard_map.216 = (bf16[256,2048]{1,0:T(8,128)(2,1)}, f32[256,2048]{1,0:T(8,128)}, bf16[256,2048]{1,0:T(8,128)(2,1)}, bf16[4,2,256,512]{3,2,1,0:T(8,128)(2,1)}, f...) custom-call(s32[16]{0:T(128)} %refs_0_.3, ...), custom_call_target="tpu_custom_call" | custom-call | flops 49999998976 | bytes 157286400 | tf_op jit(solution)/shard_map/pallas_call | solution.py:1378
  419.4 1.6 copy-done.1
  421.0 1.2 copy-done.4
  422.2 1.2 copy-done.5
  423.4 12.5 %shard_map.217 = (bf16[2048,2048]{1,0:T(8,128)(2,1)S(1)}, bf16[2048,2048]{1,0:T(8,128)(2,1)}, f32[256,2048]{1,0:T(8,128)S(1)}) custom-call(bf16[256,2048]{1,0:T(8,128)(2,1)S(1)} %copy-done.4, bf16[256,2048]{1,0:T(8,128)(2,1)S(1)} %copy-done.3, f32[256,2048]{1,0:T(8,128)S(1)} %copy-done.1, bf16[256,2048]{1,0:T(8,128)(2,1)S(1)} %copy-done.5, ...), custom_call_target="tpu_custom_call" | custom-call | flops 6442450944 | bytes 31457280 | tf_op jit(solution)/shard_map/pallas_call | solution.py:1424
  435.9 3.4 copy-done
  439.3 1.4 copy-done.2
  440.7 111.5 %shard_map.218 = (bf16[256,2048]{1,0:T(8,128)(2,1)}, f32[64,2048]{1,0:T(8,128)}, f32[64,2048]{1,0:T(8,128)}, f32[64,640]{1,0:T(8,128)}, f32[48,2048]{1,0:T(8,128...) custom-call(bf16[256,2048]{1,0:T(8,128)(2,1)} %bitcast.34, ...), custom_call_target="tpu_custom_call" | custom-call | flops 49999998976 | bytes 157286400 | tf_op jit(solution)/shard_map/pallas_call | solution.py:1547
  552.2 1.5 slice_reduce_fusion
  553.7 1.5 fusion.6
  555.3 0.0 copy-done.8
  555.3 2.3 pad_maximum_fusion
  557.6 3.6 shard_map.219
  561.2 1.0 copy.39
  562.1 1.0 copy.40
  563.1 0.8 copy.41
  563.9 0.8 copy.42
  (15 shorter events, 0.0 us)
Async XLA Ops:
  312.1 107.3 %copy-start.3 = (bf16[256,2048]{1,0:T(8,128)(2,1)S(1)}, bf16[256,2048]{1,0:T(8,128)(2,1)}, u32[]{:S(2)}) copy-start(bf16[256,2048]{1,0:T(8,128)(2,1)} %get-tuple-element.117.attn_ref.refs_1_) | copy-start | bytes 3145732
  419.4 1.6 copy-start.1
  421.0 1.2 copy-start.4
  422.2 1.2 copy-start.5
  435.9 3.4 copy-start
  439.3 1.4 copy-start.2
  440.7 114.6 %copy-start.8 = (f32[128,2048]{1,0:T(8,128)S(1)}, f32[128,2048]{1,0:T(8,128)}, u32[]{:S(2)}) copy-start(f32[128,2048]{1,0:T(8,128)} %get-tuple-element.139) | copy-start | bytes 3145732
  555.3 5.9 %copy-start.6 = (bf16[256,2048]{1,0:T(8,128)(2,1)S(1)}, bf16[256,2048]{1,0:T(8,128)(2,1)}, u32[]{:S(2)}) copy-start(bf16[256,2048]{1,0:T(8,128)(2,1)} %get-tuple-element.116) | copy-start | bytes 3145732
  557.6 4.5 copy-start.7
  561.2 2.0 copy-start.10
  561.2 2.7 copy-start.9

commit v7 on v6

--- a/solution.py
+++ b/solution.py
@@ -469,32 +469,37 @@
         ref = self.got[into]
         ref[...] = (ref[...].astype(jnp.float32) + self.held[more].astype(jnp.float32)).astype(ref.dtype)
 
-    def start(self, k):
-        zs, z, got = self.zs, self.z, self.got
+    def lines_of(self, k):
+        zs, got = self.zs, self.got
         up, down = k - 1, zs - 2 + k
-        self.lines = [
+        lines = [
             Line(zs, 1, 0, 1, self.own(-k), got[up], self.sems.at[up]),
             Line(zs, -1, zs - 1, zs, self.own(k), got[down], self.sems.at[down]),
         ]
+        if k > 1:
+            lines += [
+                Line(zs, 1, 1, k, got[up - 1], got[up], self.sems.at[up]),
+                Line(zs, -1, zs - k, zs - 1, got[down - 1], got[down], self.sems.at[down]),
+            ]
+        return lines
+
+    def start(self, k):
+        zs, z = self.zs, self.z
+        up, down = k - 1, zs - 2 + k
         if k > 1:
             for load in self.loads:
                 load.wait()
             pl.when((z >= 1) & (z < k))(functools.partial(self.add, up - 1, 0))
             pl.when((z >= zs - k) & (z < zs - 1))(functools.partial(self.add, down - 1, 1))
-            self.lines += [
-                Line(zs, 1, 1, k, got[up - 1], got[up], self.sems.at[up]),
-                Line(zs, -1, zs - k, zs - 1, got[down - 1], got[down], self.sems.at[down]),
-            ]
+        self.lines = self.lines_of(k)
         for line in self.lines:
             line.start()
-        if k < zs - 1 and self.got[up + 1] is not None:
-            self.fetch(k + 1)
-        elif k == zs - 1:
+        if k == zs - 1:
             self.loads = [pltpu.make_async_copy(self.own(0), self.held.at[0], self.l_sem.at[0])]
             self.loads[0].start()
 
-    def finish(self):
-        for line in self.lines:
+    def finish(self, k=None):
+        for line in self.lines if k is None else self.lines_of(k):
             line.finish()
 
     def total(self):
@@ -828,7 +833,7 @@
         g_both_one, g_down_one, *refs = refs
     out_ref, dx_ref, g_both_ref, g_down_ref, *refs = refs
     if linked:
-        *got, both_one, down_one, both_w, down_w, both_sum, down_sum, stage, sem, z_sem = refs
+        *got, both_one, down_one, both_w, down_w, both_sum, down_sum, stage, sem, z_sem, come, held, d_sems, dl_sem = refs
     else:
         got, (both_one, down_one, both_w, down_w, both_sum, down_sum, stage, sem) = [], refs
     n, wide = stage.shape[1] // 2, down_w.shape[0]
@@ -837,11 +842,12 @@
     lines = []
     if linked:
         z = lax.div(lax.axis_index("seq"), 2)
-        for at, parts in ((0, g_both_one), (2, g_down_one)):
-            lines += [
-                Line(zs, 1, 0, 1, parts.at[lax.rem(z + zs - 1, zs)], got[at], z_sem.at[at]),
-                Line(zs, -1, zs - 1, zs, parts.at[lax.rem(z + 1, zs)], got[at + 1], z_sem.at[at + 1]),
-            ]
+        lines = [
+            Line(zs, 1, 0, 1, g_both_one.at[lax.rem(z + zs - 1, zs)], got[0], z_sem.at[0]),
+            Line(zs, -1, zs - 1, zs, g_both_one.at[lax.rem(z + 1, zs)], got[1], z_sem.at[1]),
+        ]
+        none = [None] * (zs - 3)
+        down = SumChain(zs, g_down_one, [come.at[0], got[2], *none, come.at[1], got[3], *none], held, d_sems, dl_sem)
 
     @pl.when(step == 0)
     def _():
@@ -850,8 +856,7 @@
             copies += assemble(zs, pieces[which], whole, sem.at[which])
         if linked:
             greet(neighbours(zs, False, False))
-            for line in lines:
-                line.start()
+            down.start(1)
         both_sum[...] = jnp.zeros_like(both_sum)
         down_sum[...] = jnp.zeros_like(down_sum)
         if wide > n:
@@ -861,6 +866,16 @@
             copy.wait()
         both_w[:, :n] = stage[:, :n]
         both_w[:, wide : wide + n] = stage[:, n:]
+
+    if linked:
+
+        @pl.when(step == last - 5)
+        def _():
+            down.finish(1)
+            for line in lines:
+                line.start()
+            down.fetch(2)
+            down.start(2)
 
     x, dy = x_ref[...], dy_ref[...]
     hidden, d_both = swiglu(product(x, both_w[...]), product_nt(dy, down_w[...]))
@@ -882,6 +897,8 @@
             copy.wait()
         for line in lines:
             line.finish()
+        if linked:
+            down.finish(2)
 
 
 def ffn_first(x, dy, both_pieces, down_pieces, zs, others=(), collective_id=None):
@@ -932,6 +949,10 @@
         return pl.BlockSpec((block, width), lambda i: (i, 0))
 
     linked = bool(parts)
+    extra = []
+    if linked:
+        held = pltpu.VMEM((2,) + parts[1].shape[1:], low)
+        extra = [sem((2, 2)), held, held, sem((2 * zs - 2, 2)), sem((2,))]
     params = dict(collective_id=collective_id, has_side_effects=True) if linked else {}
     return pl.pallas_call(
         functools.partial(ffn_second_kernel, zs, counts, linked),
@@ -945,7 +966,7 @@
             pltpu.VMEM((D, 2 * wide), low), pltpu.VMEM((wide, D), low),
             pltpu.VMEM((D, 2 * wide), full), pltpu.VMEM((wide, D), full), pltpu.VMEM((D, 2 * n), low),
             sem((4, zs)),
-        ] + [sem((4, 2))] * linked,
+        ] + extra,
         compiler_params=pltpu.CompilerParams(vmem_limit_bytes=56 * MIB, **params),
         cost_estimate=LONG,
     )(x, dy, hidden, d_both, *one[0], *one[1], *two[0], *two[1], *parts)
@@ -960,7 +981,12 @@
     return (0, first), (first, unit - first)
 
 
-def spread_kernel(zs, rows, unit, gate_ref, up_ref, *out):
+def gain_columns(one, two, rows):
+    row = lax.broadcasted_iota(jnp.int32, (128, rows), 0)
+    return jnp.where(row == 0, one, jnp.where(row == 1, two, 0.0)).T
+
+
+def spread_kernel(zs, rows, unit, gate_ref, up_ref, query_ref, key_ref, value_ref, one_ref, two_ref, down_ref, *out):
     for (begin, size), ref in zip(portions(unit), out):
         for c in range(2):
             for r in range(rows):
@@ -969,20 +995,32 @@
                         at = ((z * 2 + c) * rows + r) * unit + begin
                         to = (n * zs + z) * size
                         ref[c, r, :, to : to + size] = weight[:, at : at + size]
-
-
-def spread(gate, up, zs, rows):
+    pack_ref, down_one, down_two = out[2:]
+    pack_ref[:, :D] = query_ref[...]
+    pack_ref[:, D : D + KVW] = key_ref[...]
+    pack_ref[:, D + KVW : QKV] = value_ref[...]
+    gains = gain_columns(one_ref[...].astype(jnp.float32), two_ref[...].astype(jnp.float32), pack_ref.shape[0])
+    pack_ref[:, QKV:] = gains.astype(pack_ref.dtype)
+    cut = down_one.shape[0]
+    down_one[...] = down_ref[:cut, :]
+    down_two[...] = down_ref[cut:, :]
+
+
+def spread(gate, up, query, key, value, one, two, down, zs, rows):
     wide, part = gate.shape
     unit = part // (zs * 2 * rows)
+    shape, low = jax.ShapeDtypeStruct, gate.dtype
     return pl.pallas_call(
         functools.partial(spread_kernel, zs, rows, unit),
-        out_shape=[jax.ShapeDtypeStruct((2, rows, wide, 2 * zs * size), gate.dtype) for _, size in portions(unit)],
-    )(gate, up)
+        out_shape=[shape((2, rows, wide, 2 * zs * size), low) for _, size in portions(unit)]
+        + [shape((wide, PACK), low)]
+        + [shape((size, D), low) for _, size in portions(unit)],
+    )(gate, up, query, key, value, one.reshape(1, -1), two.reshape(1, -1), down)
 
 
 def collect_kernel(zs, rows, unit, *refs):
-    given, outs = refs[:2], refs[2:]
-    for n, out in enumerate(outs):
+    given, (pack_ref, down_one, down_two), outs = refs[:2], refs[2:5], refs[5:]
+    for n, out in enumerate(outs[:2]):
         for (begin, size), ref in zip(portions(unit), given):
             for c in range(2):
                 for r in range(rows):
@@ -990,11 +1028,24 @@
                         at = ((z * 2 + c) * rows + r) * unit + begin
                         to = (n * zs + z) * size
                         out[:, at : at + size] = ref[c, r, :, to : to + size].astype(jnp.float32)
-
-
-def collect(blocks, zs, rows, unit):
-    shape = jax.ShapeDtypeStruct((blocks[0].shape[2], unit * zs * 2 * rows), jnp.float32)
-    return pl.pallas_call(functools.partial(collect_kernel, zs, rows, unit), out_shape=[shape, shape])(*blocks)
+    key_ref, value_ref, gains_ref, down_ref = outs[2:]
+    key_ref[...] = pack_ref[:, :KVW]
+    value_ref[...] = pack_ref[:, KVW : 2 * KVW]
+    gains_ref[...] = pack_ref[:, 2 * KVW :].T[:8]
+    cut = down_one.shape[0]
+    down_ref[:cut, :] = down_one[...]
+    down_ref[cut:, :] = down_two[...]
+
+
+def collect(blocks, pack, downs, zs, rows, unit):
+    wide = blocks[0].shape[2]
+    shape, full = jax.ShapeDtypeStruct, jnp.float32
+    whole = shape((wide, unit * zs * 2 * rows), full)
+    narrow = shape((wide, KVW), full)
+    return pl.pallas_call(
+        functools.partial(collect_kernel, zs, rows, unit),
+        out_shape=[whole, whole, narrow, narrow, shape((8, wide), full), shape((unit, D), full)],
+    )(*blocks, pack, *downs)
 
 
 def forward_kernel(zs, micro, *refs):
@@ -1253,8 +1304,8 @@
         "dx": Scatter(1, False, True, dx_part, take_d_ffn, *more[:SCATTER_REFS]),
         "out": Scatter(1, False, True, out_part, take_result, *more[SCATTER_REFS : 2 * SCATTER_REFS]),
     }
-    down = SumChain(zs, down_part, [got.at[n] for n in range(2 * zs - 2)], held, d_sems, dl_sem)
     none = [None] * (zs - 3)
+    down = SumChain(zs, down_part, [*none, got.at[0], got.at[1], *none, got.at[2], got.at[3]], held, d_sems, dl_sem)
     both = SumChain(
         zs, both_part, [b_got.at[0], both_up, *none, b_got.at[1], both_down, *none], b_held, b_sems, bl_sem
     )
@@ -1264,12 +1315,12 @@
     ]
     comes = [
         pltpu.make_async_copy(src, dst, sems.at[2 + n])
-        for n, (src, dst) in enumerate(zip(come, (b_got.at[0], b_got.at[1], got.at[0], got.at[zs - 1])))
+        for n, (src, dst) in enumerate(zip(come, (b_got.at[0], b_got.at[1], got.at[0], got.at[2])))
     ]
     for copy in comes:
         copy.start()
     both.fetch(2)
-    down.fetch(2)
+    down.fetch(zs - 1)
     schedule = [(0, 3), (0, 1), (0, 2), (0, 0)]
     scatters["dx"].begin(schedule)
     for one in arounds:
@@ -1281,7 +1332,7 @@
     for copy in comes:
         copy.wait()
     both.start(2)
-    down.start(2)
+    down.start(zs - 1)
     scatters["out"].begin(schedule)
     scatters["dx"].stage_b(0)
     scatters["out"].stage_a(0)
@@ -1349,12 +1400,9 @@
 
         return carry
 
-    lax.fori_loop(0, micro, attend_some, 0)
+    lax.fori_loop(0, 2 * micro, attend_some, 0)
+    scatters["out"].stage_c(0)
     both.finish()
-    down.finish()
-    down.start(3)
-    lax.fori_loop(micro, 2 * micro, attend_some, 0)
-    scatters["out"].stage_c(0)
     down.finish()
     down.total()
     down_ref[...] = held[0].astype(full)
@@ -1393,7 +1441,7 @@
             pltpu.VMEM((wide, GROUP * span // 2), full),
             pltpu.VMEM((2 * wide, 2 * KVW), full),
             sem((6,)),
-            pltpu.VMEM((2 * zs - 2, unit, D), low),
+            pltpu.VMEM((4, unit, D), low),
             pltpu.VMEM((2, unit, D), low),
             sem((2 * zs - 2, 2)), sem((2,)),
             pltpu.VMEM((2,) + piece.shape, low),
@@ -1427,7 +1475,7 @@
         in_specs=[narrow, narrow, whole, whole, tall],
         out_specs=[tall, tall, narrow],
         out_shape=[shape((D, D), low), shape((D, D), low), shape((many, D), jnp.float32)],
-        compiler_params=pltpu.CompilerParams(vmem_limit_bytes=32 * MIB),
+        compiler_params=pltpu.CompilerParams(vmem_limit_bytes=60 * MIB),
         cost_estimate=pl.CostEstimate(flops=6 * many * D * D, bytes_accessed=30 * MIB, transcendentals=0),
     )(attended, attn_in, d_middle, d_query, packed)
 
@@ -1615,11 +1663,11 @@
     wide = w_gate.shape[0]
     unit = w_down.shape[0]
 
-    both, rest = spread(w_gate, w_up, zs, rows)
+    both, rest, pack, down_own, last_own = spread(
+        w_gate, w_up, w_query, w_key, w_value, gain_attn, gain_ffn, w_down, zs, rows
+    )
     cut = split_unit(unit)
     flat, flat_rest = (2 * rows * wide, 2 * zs * cut), (2 * rows * wide, 2 * zs * (unit - cut))
-    gains = jnp.pad(jnp.stack([gain_attn, gain_ffn], axis=1), ((0, 0), (0, 126)))
-    pack = jnp.concatenate([w_query, w_key, w_value, gains], axis=1)
     dy_own = cotangent.reshape(many, D)
     own_tokens = tokens.reshape(many, D)
     x = own_tokens.astype(jnp.float32)
@@ -1627,7 +1675,6 @@
     slot_of = jnp.argmax(order[None, :] == jnp.arange(order.shape[0], dtype=jnp.int32)[:, None], axis=1).astype(jnp.int32)
     chained = links.kernels
     if chained:
-        down_own, last_own = w_down[:cut], w_down[cut:]
         found = forward(order, first, own_tokens, pack, both, rest, down_own, w_out, dy_own, zs, 0)
         packed, both_own, kv, out_w, dy, rest_own = found[:6]
         both_w = [b.reshape(flat) for b in (both_own, *found[6 : 4 + 2 * zs])]
@@ -1638,7 +1685,7 @@
     else:
         both_w = [links.gather_z(links.exchange_xla(both).reshape(flat))]
         rest_w = [links.gather_z(links.exchange_xla(rest).reshape(flat_rest))]
-        down_w, last_w = [links.gather_z(w_down[:cut])], [links.gather_z(w_down[cut:])]
+        down_w, last_w = [links.gather_z(down_own)], [links.gather_z(last_own)]
         packed, dy = links.gather(pack, True, True).reshape(D, PACK), links.gather(dy_own, False, True)
         gain_one, gain_two = packed[:, QKV].astype(jnp.float32), packed[:, QKV + 1].astype(jnp.float32)
         mine = slot_places(order, half_len, lax.axis_index("seq") * span + jnp.arange(span, dtype=jnp.int32))
@@ -1711,21 +1758,21 @@
         gains_grad = jnp.pad(jnp.stack([grad_gain_one, grad_gain_two], axis=1), ((0, 0), (0, 126)))
         pack_grad = jnp.concatenate([product_tn(attn_in, d_kv), gains_grad], axis=1).astype(low)
         pack_grad = links.scatter(pack_grad.reshape(*shards, 2 * KVW + 128), True, True)
-    grad_gate, grad_up = collect((grad_both, grad_rest), zs, rows, unit)
-    grad_down = jnp.concatenate([grad_down, grad_last])
-
+    grad_gate, grad_up, grad_key, grad_value, gains_grad, grad_down = collect(
+        (grad_both, grad_rest), pack_grad, (grad_down, grad_last), zs, rows, unit
+    )
     return (
         result.reshape(tokens.shape),
         x_grad.reshape(tokens.shape),
         grad_query,
-        pack_grad[:, :KVW],
-        pack_grad[:, KVW : 2 * KVW],
+        grad_key,
+        grad_value,
         grad_out,
         grad_gate,
         grad_up,
         grad_down,
-        pack_grad[:, 2 * KVW],
-        pack_grad[:, 2 * KVW + 1],
+        gains_grad[0],
+        gains_grad[1],
     )
 
 

time: 573 us -> 548 us (0.956)
  local copies, waits for them, and re-layouts: 21 us -> 6.82 us
    pallas_call x1, Pallas kernels: 107 us -> 94.1 us  [back(): pl.pallas_call(functools.partial(back_kernel, zs, micro), out_shape=[shap...]
    unnamed x26 -> x12, local copies, waits for them, and re-layouts: 12.4 us -> 3.54 us
    slice x4 -> x0, local copies, waits for them, and re-layouts: 6.56 us -> none  [the longest x2 3.5 us: on_device(): down_own, last_own = (w_down[:cut], w_down[cut:])]
where the time goes in v7:
time: 548 us; the launch traced here: 541 us
  Pallas kernels  532 us (97%)
  local copies, waits for them, and re-layouts  6.82 us (1%)
    pallas_call x1, Pallas kernels, forward(): pl.pallas_call(functools.partial(forward_kernel, zs, micro), out_shape=ou...  183 us
    pallas_call x1, Pallas kernels, weight_sums(): pl.pallas_call(functools.partial(weights_kernel, zs), out_shape=[shape((m...  111 us
    pallas_call x1, Pallas kernels, back(): pl.pallas_call(functools.partial(back_kernel, zs, micro), out_shape=[shap...  94.1 us
    pallas_call x1, Pallas kernels, ffn_first(): pl.pallas_call(functools.partial(ffn_first_kernel, zs, count, linked), gr...  63.6 us
    pallas_call x1, Pallas kernels, ffn_second(): pl.pallas_call(functools.partial(ffn_second_kernel, zs, counts, linked),...  55.3 us
    pallas_call x1, Pallas kernels, products(): pl.pallas_call(products_kernel, grid=(D // block,), in_specs=[narrow, nar...  16 us

profile of v7, /device:TPU:8, one launch (start us, length us, event | category | flops | bytes accessed | tf_op | source)
XLA Modules:
  0.0 541.0 jit_solution(13630608007662588278)
XLA Ops:
  0.6 1.3 slice_reduce_fusion.refs_2_
  2.0 0.7 broadcast_multiply_fusion
  2.6 0.5 fusion.3.refs_3_
  3.1 0.1 iota_add_fusion
  3.2 0.7 add.46.refs_1_
  3.9 4.1 shard_map.212
  8.0 183.4 %shard_map.213 = (bf16[4,2,4,64,2688]{4,3,2,1,0:T(8,128)(2,1)}, bf16[2,4,64,1024]{3,2,1,0:T(8,128)(2,1)}, bf16[4,2,256,512]{3,2,1,0:T(8,128)(2,1)}, bf16[4,2,4,6...) custom-call(s32[16]{0:T(128)} %refs_0_.3, ...), custom_call_target="tpu_custom_call" | custom-call | flops 49999998976 | bytes 157286400 | tf_op jit(solution)/shard_map/pallas_call | solution.py:1260
  191.4 63.6 %shard_map.214 = (bf16[2048,2048]{1,0:T(8,128)(2,1)}, bf16[3,512,384]{2,1,0:T(8,128)(2,1)}, bf16[3,48,2048]{2,1,0:T(8,128)(2,1)}, bf16[2048,512]{1,0:T(8,128)(2,...) custom-call(bf16[256,2048]{1,0:T(8,128)(2,1)} %get-tuple-element.92.refs_0_, ...), custom_call_target="tpu_custom_call" | custom-call | flops 49999998976 | bytes 157286400 | tf_op jit(solution)/shard_map/pallas_call | solution.py:923
  255.1 55.3 %shard_map.215 = (bf16[2048,2048]{1,0:T(8,128)(2,1)}, bf16[2048,2048]{1,0:T(8,128)(2,1)}, bf16[2048,384]{1,0:T(8,128)(2,1)}, bf16[192,2048]{1,0:T(8,128)(2,1)}, ...) custom-call(bf16[2048,2048]{1,0:T(8,128)(2,1)} %get-tuple-element.10, ...), custom_call_target="tpu_custom_call" | custom-call | flops 49999998976 | bytes 157286400 | tf_op jit(solution)/shard_map/pallas_call | solution.py:957
  310.3 94.1 %shard_map.216 = (bf16[256,2048]{1,0:T(8,128)(2,1)}, f32[256,2048]{1,0:T(8,128)}, bf16[256,2048]{1,0:T(8,128)(2,1)}, bf16[4,2,256,512]{3,2,1,0:T(8,128)(2,1)}, f...) custom-call(s32[16]{0:T(128)} %refs_0_.3, ...), custom_call_target="tpu_custom_call" | custom-call | flops 49999998976 | bytes 157286400 | tf_op jit(solution)/shard_map/pallas_call | solution.py:1426
  404.5 16.0 %shard_map.217 = (bf16[2048,2048]{1,0:T(8,128)(2,1)}, bf16[2048,2048]{1,0:T(8,128)(2,1)}, f32[256,2048]{1,0:T(8,128)}) custom-call(bf16[256,2048]{1,0:T(8,128)(2,1)} %get-tuple-element.129.attended_ref, bf16[256,2048]{1,0:T(8,128)(2,1)} %get-tuple-element.127.attn_ref.refs_1_, f32[256,2048]{1,0:T(8,128)} %get-tuple-element.128.d_middle_ref.refs_2_, ...), custom_call_target="tpu_custom_call" | custom-call | flops 6442450944 | bytes 31457280 | tf_op jit(solution)/shard_map/pallas_call | solution.py:1472
  420.5 110.8 %shard_map.218 = (bf16[256,2048]{1,0:T(8,128)(2,1)}, f32[64,2048]{1,0:T(8,128)}, f32[64,2048]{1,0:T(8,128)}, f32[64,640]{1,0:T(8,128)}, f32[48,2048]{1,0:T(8,128...) custom-call(bf16[256,2048]{1,0:T(8,128)(2,1)} %bitcast.39, ...), custom_call_target="tpu_custom_call" | custom-call | flops 49999998976 | bytes 157286400 | tf_op jit(solution)/shard_map/pallas_call | solution.py:1595
  531.3 0.0 copy-start
  531.3 0.0 copy-start.1
  531.3 4.6 shard_map.219
  535.9 1.3 slice_bitcast_fusion
  537.2 0.0 copy-done
  537.2 0.0 copy-start.3
  537.2 0.0 copy-start.2
  537.2 1.0 copy.32
  538.2 0.0 copy-done.1
  538.2 1.0 copy.33
  539.2 0.0 copy-done.3
  539.2 0.8 copy.34
  540.0 0.0 copy-done.2
  540.0 0.8 copy.35
Async XLA Ops:
  531.3 5.9 %copy-start = (bf16[256,2048]{1,0:T(8,128)(2,1)S(1)}, bf16[256,2048]{1,0:T(8,128)(2,1)}, u32[]{:S(2)}) copy-start(bf16[256,2048]{1,0:T(8,128)(2,1)} %get-tuple-element.126) | copy-start | bytes 3145732
  531.3 6.9 %copy-start.1 = (bf16[256,2048]{1,0:T(8,128)(2,1)S(1)}, bf16[256,2048]{1,0:T(8,128)(2,1)}, u32[]{:S(2)}) copy-start(bf16[256,2048]{1,0:T(8,128)(2,1)} %get-tuple-element.141) | copy-start | bytes 3145732
  537.2 2.0 copy-start.3
  537.2 2.8 copy-start.2

commit v8 on v7

--- a/solution.py
+++ b/solution.py
@@ -2,6 +2,7 @@
 
 import jax
 import jax.numpy as jnp
+import numpy as np
 from jax import lax
 from jax.experimental import pallas as pl
 from jax.experimental.pallas import tpu as pltpu
@@ -1028,10 +1029,12 @@
                         at = ((z * 2 + c) * rows + r) * unit + begin
                         to = (n * zs + z) * size
                         out[:, at : at + size] = ref[c, r, :, to : to + size].astype(jnp.float32)
-    key_ref, value_ref, gains_ref, down_ref = outs[2:]
+    key_ref, value_ref, one_ref, two_ref, down_ref = outs[2:]
     key_ref[...] = pack_ref[:, :KVW]
     value_ref[...] = pack_ref[:, KVW : 2 * KVW]
-    gains_ref[...] = pack_ref[:, 2 * KVW :].T[:8]
+    gains = pack_ref[:, 2 * KVW :].T
+    one_ref[...] = gains[0:1]
+    two_ref[...] = gains[1:2]
     cut = down_one.shape[0]
     down_ref[:cut, :] = down_one[...]
     down_ref[cut:, :] = down_two[...]
@@ -1044,7 +1047,7 @@
     narrow = shape((wide, KVW), full)
     return pl.pallas_call(
         functools.partial(collect_kernel, zs, rows, unit),
-        out_shape=[whole, whole, narrow, narrow, shape((8, wide), full), shape((unit, D), full)],
+        out_shape=[whole, whole, narrow, narrow, shape((1, wide), full), shape((1, wide), full), shape((unit, D), full)],
     )(*blocks, pack, *downs)
 
 
@@ -1082,7 +1085,7 @@
     lane = lax.broadcasted_iota(jnp.int32, (half_len, 128), 1)
     for i in range(2 * micro):
         place_here = order_ref[(z * 2 + c) * 2 + i % 2] * half_len + lax.broadcasted_iota(jnp.int32, (half_len, 128), 0)
-        start = jnp.where(place_here >= first_ref[i // 2], first_ref[i // 2], 0)
+        start = jnp.where(place_here >= first_ref[i // 2, 0], first_ref[i // 2, 0], 0)
         angle = (place_here - start).astype(jnp.float32) * freq_ref[...]
         cos_ref[i * half_len : (i + 1) * half_len, :] = jnp.cos(angle)
         sine = jnp.sin(angle)
@@ -1191,7 +1194,7 @@
         window[...] = product(chosen[half], kv_here[:, :, at, :].reshape(2 * wide, 2 * KVW)).astype(low)
         key_place = first_block * half_len + lax.broadcasted_iota(jnp.int32, (half_len, wide), 1)
         place_here = my_block * half_len + lax.broadcasted_iota(jnp.int32, (half_len, wide), 0)
-        first = first_ref[m]
+        first = first_ref[m, 0]
         start = jnp.where(place_here >= first, first, 0)
         bias[...] = jnp.where((key_place <= place_here) & (key_place >= start), 0.0, NEG_LARGE)
         here = pl.ds(pl.multiple_of(i * half_len, half_len), half_len)
@@ -1244,7 +1247,8 @@
     seq = 2 * zs
     wide = seq * (many // micro) // 2
     low, full = jnp.bfloat16, jnp.float32
-    freq = 10000.0 ** (-(jnp.arange(128, dtype=jnp.int32) % (HEAD_DIM // 2)).astype(full) / (HEAD_DIM // 2))
+    turns = np.arange(128) % (HEAD_DIM // 2) / (HEAD_DIM // 2)
+    freq = jnp.asarray((10000.0 ** -turns).astype(np.float32))
     anywhere, here, smem = (pl.BlockSpec(memory_space=m) for m in (pl.ANY, pltpu.VMEM, pltpu.SMEM))
     shape = jax.ShapeDtypeStruct
     out_any = [
@@ -1371,7 +1375,7 @@
         window[...] = product(chosen[...], kv_here[:, :, rows, :].reshape(2 * wide, 2 * KVW)).astype(low)
         key_place = first_block * half_len + lax.broadcasted_iota(jnp.int32, bias.shape, 0)
         place_here = my_block * half_len + lax.rem(lax.broadcasted_iota(jnp.int32, bias.shape, 1), half_len)
-        first = first_ref[m]
+        first = first_ref[m, 0]
         start = jnp.where(place_here >= first, first, 0)
         bias[...] = jnp.where((key_place <= place_here) & (key_place >= start), 0.0, NEG_LARGE)
         here = pl.ds(pl.multiple_of(i * half_len, half_len), half_len)
@@ -1464,7 +1468,7 @@
 
 
 def products(attended, attn_in, d_middle, d_query, packed):
-    many, block = attended.shape[0], 256
+    many, block = attended.shape[0], 512
     low, shape = jnp.bfloat16, jax.ShapeDtypeStruct
     narrow = pl.BlockSpec((many, block), lambda i: (0, i))
     tall = pl.BlockSpec((block, D), lambda i: (i, 0))
@@ -1675,7 +1679,7 @@
     slot_of = jnp.argmax(order[None, :] == jnp.arange(order.shape[0], dtype=jnp.int32)[:, None], axis=1).astype(jnp.int32)
     chained = links.kernels
     if chained:
-        found = forward(order, first, own_tokens, pack, both, rest, down_own, w_out, dy_own, zs, 0)
+        found = forward(order, lengths[:, 0], own_tokens, pack, both, rest, down_own, w_out, dy_own, zs, 0)
         packed, both_own, kv, out_w, dy, rest_own = found[:6]
         both_w = [b.reshape(flat) for b in (both_own, *found[6 : 4 + 2 * zs])]
         down_w = [down_own, *found[4 + 2 * zs : 2 + 4 * zs]]
@@ -1726,7 +1730,7 @@
     if chained:
         out_all, kv_all = out_w.reshape(*shards, D), kv.reshape(zs, 2, many, 2 * KVW)
         result, d_middle, d_query, d_kv, gain_two_grad, grad_down, both_up, both_down, rest_in, last_in = back(
-            order, first, dy_own, middle, gains, queries, cosine, sine, d_ffn_part, result_part, grad_both, grad_down,
+            order, lengths[:, 0], dy_own, middle, gains, queries, cosine, sine, d_ffn_part, result_part, grad_both, grad_down,
             out_all, kv_all, grad_rest, grad_last, come, zs, 3,
         )
         grad_out, grad_query, d_attn = products(attended, attn_in, d_middle, d_query, packed)
@@ -1758,7 +1762,7 @@
         gains_grad = jnp.pad(jnp.stack([grad_gain_one, grad_gain_two], axis=1), ((0, 0), (0, 126)))
         pack_grad = jnp.concatenate([product_tn(attn_in, d_kv), gains_grad], axis=1).astype(low)
         pack_grad = links.scatter(pack_grad.reshape(*shards, 2 * KVW + 128), True, True)
-    grad_gate, grad_up, grad_key, grad_value, gains_grad, grad_down = collect(
+    grad_gate, grad_up, grad_key, grad_value, grad_one, grad_two, grad_down = collect(
         (grad_both, grad_rest), pack_grad, (grad_down, grad_last), zs, rows, unit
     )
     return (
@@ -1771,8 +1775,8 @@
         grad_gate,
         grad_up,
         grad_down,
-        gains_grad[0],
-        gains_grad[1],
+        grad_one.reshape(-1),
+        grad_two.reshape(-1),
     )
 
 

time: 548 us -> 542 us (0.989)
  no operation moved by 1% of the time
where the time goes in v8:
time: 542 us; the launch traced here: 535 us
  Pallas kernels  529 us (98%)
    pallas_call x1, Pallas kernels, forward(): pl.pallas_call(functools.partial(forward_kernel, zs, micro), out_shape=ou...  183 us
    pallas_call x1, Pallas kernels, weight_sums(): pl.pallas_call(functools.partial(weights_kernel, zs), out_shape=[shape((m...  111 us
    pallas_call x1, Pallas kernels, back(): pl.pallas_call(functools.partial(back_kernel, zs, micro), out_shape=[shap...  94.2 us
    pallas_call x1, Pallas kernels, ffn_first(): pl.pallas_call(functools.partial(ffn_first_kernel, zs, count, linked), gr...  63.7 us
    pallas_call x1, Pallas kernels, ffn_second(): pl.pallas_call(functools.partial(ffn_second_kernel, zs, counts, linked),...  55.2 us
    pallas_call x1, Pallas kernels, products(): pl.pallas_call(products_kernel, grid=(D // block,), in_specs=[narrow, nar...  12.8 us

profile of v8, /device:TPU:8, one launch (start us, length us, event | category | flops | bytes accessed | tf_op | source)
XLA Modules:
  0.0 534.7 jit_solution(7751454799298242059)
XLA Ops:
  0.6 0.7 broadcast_multiply_fusion
  1.3 0.1 iota_add_fusion
  1.4 0.7 add.33.refs_1_
  2.0 4.1 shard_map.221
  6.2 183.3 %shard_map.222 = (bf16[4,2,4,64,2688]{4,3,2,1,0:T(8,128)(2,1)}, bf16[2,4,64,1024]{3,2,1,0:T(8,128)(2,1)}, bf16[4,2,256,512]{3,2,1,0:T(8,128)(2,1)}, bf16[4,2,4,6...) custom-call(s32[16]{0:T(128)} %refs_0_.3, ...), custom_call_target="tpu_custom_call" | custom-call | flops 49999998976 | bytes 157286400 | tf_op jit(solution)/shard_map/pallas_call | solution.py:1264
  189.5 63.7 %shard_map.223 = (bf16[2048,2048]{1,0:T(8,128)(2,1)}, bf16[3,512,384]{2,1,0:T(8,128)(2,1)}, bf16[3,48,2048]{2,1,0:T(8,128)(2,1)}, bf16[2048,512]{1,0:T(8,128)(2,...) custom-call(bf16[256,2048]{1,0:T(8,128)(2,1)} %get-tuple-element.93.refs_0_, ...), custom_call_target="tpu_custom_call" | custom-call | flops 49999998976 | bytes 157286400 | tf_op jit(solution)/shard_map/pallas_call | solution.py:924
  253.2 55.2 %shard_map.224 = (bf16[2048,2048]{1,0:T(8,128)(2,1)}, bf16[2048,2048]{1,0:T(8,128)(2,1)}, bf16[2048,384]{1,0:T(8,128)(2,1)}, bf16[192,2048]{1,0:T(8,128)(2,1)}, ...) custom-call(bf16[2048,2048]{1,0:T(8,128)(2,1)} %get-tuple-element.11, ...), custom_call_target="tpu_custom_call" | custom-call | flops 49999998976 | bytes 157286400 | tf_op jit(solution)/shard_map/pallas_call | solution.py:958
  308.4 94.2 %shard_map.225 = (bf16[256,2048]{1,0:T(8,128)(2,1)}, f32[256,2048]{1,0:T(8,128)}, bf16[256,2048]{1,0:T(8,128)(2,1)}, bf16[4,2,256,512]{3,2,1,0:T(8,128)(2,1)}, f...) custom-call(s32[16]{0:T(128)} %refs_0_.3, ...), custom_call_target="tpu_custom_call" | custom-call | flops 49999998976 | bytes 157286400 | tf_op jit(solution)/shard_map/pallas_call | solution.py:1430
  402.6 12.8 %shard_map.226 = (bf16[2048,2048]{1,0:T(8,128)(2,1)}, bf16[2048,2048]{1,0:T(8,128)(2,1)}, f32[256,2048]{1,0:T(8,128)}) custom-call(bf16[256,2048]{1,0:T(8,128)(2,1)} %get-tuple-element.130.attended_ref, bf16[256,2048]{1,0:T(8,128)(2,1)} %get-tuple-element.128.attn_ref.refs_1_, f32[256,2048]{1,0:T(8,128)} %get-tuple-element.129.d_middle_ref.refs_2_, ...), custom_call_target="tpu_custom_call" | custom-call | flops 6442450944 | bytes 31457280 | tf_op jit(solution)/shard_map/pallas_call | solution.py:1476
  415.4 110.8 %shard_map.227 = (bf16[256,2048]{1,0:T(8,128)(2,1)}, f32[64,2048]{1,0:T(8,128)}, f32[64,2048]{1,0:T(8,128)}, f32[64,640]{1,0:T(8,128)}, f32[48,2048]{1,0:T(8,128...) custom-call(bf16[256,2048]{1,0:T(8,128)(2,1)} %bitcast.38, ...), custom_call_target="tpu_custom_call" | custom-call | flops 49999998976 | bytes 157286400 | tf_op jit(solution)/shard_map/pallas_call | solution.py:1599
  526.2 0.0 copy-start
  526.2 0.0 copy-start.1
  526.2 4.6 shard_map.228
  530.9 0.0 copy-done
  530.9 0.0 copy-start.3
  530.9 0.0 copy-start.2
  530.9 1.0 copy.31
  531.9 0.0 copy-done.1
  531.9 1.0 copy.32
  532.8 0.0 copy-done.3
  532.8 0.8 copy.33
  533.6 0.0 copy-done.2
  533.6 0.8 copy.34
Async XLA Ops:
  526.2 4.7 copy-start
  526.2 5.6 %copy-start.1 = (bf16[256,2048]{1,0:T(8,128)(2,1)S(1)}, bf16[256,2048]{1,0:T(8,128)(2,1)}, u32[]{:S(2)}) copy-start(bf16[256,2048]{1,0:T(8,128)(2,1)} %get-tuple-element.142) | copy-start | bytes 3145732
  530.9 2.0 copy-start.3
  530.9 2.8 copy-start.2

commit v9 on v8

--- a/solution.py
+++ b/solution.py
@@ -1573,7 +1573,7 @@
     for n, stages in enumerate(rounds):
         if n == 3:
             keys_and_norm()
-        if n == len(rounds) - 3:
+        if n == len(rounds) - 2:
             chain.finish()
             chain.total()
             exchange = Exchange(held.at[0], moved_ref, *exchange_sems)

time: 542 us -> 541 us (level)
  no operation moved by 1% of the time
where the time goes in v9:
time: 541 us; the launch traced here: 534 us
  Pallas kernels  528 us (98%)
    pallas_call x1, Pallas kernels, forward(): pl.pallas_call(functools.partial(forward_kernel, zs, micro), out_shape=ou...  183 us
    pallas_call x1, Pallas kernels, weight_sums(): pl.pallas_call(functools.partial(weights_kernel, zs), out_shape=[shape((m...  110 us
    pallas_call x1, Pallas kernels, back(): pl.pallas_call(functools.partial(back_kernel, zs, micro), out_shape=[shap...  94.2 us
    pallas_call x1, Pallas kernels, ffn_first(): pl.pallas_call(functools.partial(ffn_first_kernel, zs, count, linked), gr...  63.7 us
    pallas_call x1, Pallas kernels, ffn_second(): pl.pallas_call(functools.partial(ffn_second_kernel, zs, counts, linked),...  55.2 us
    pallas_call x1, Pallas kernels, products(): pl.pallas_call(products_kernel, grid=(D // block,), in_specs=[narrow, nar...  12.8 us

profile of v9, /device:TPU:8, one launch (start us, length us, event | category | flops | bytes accessed | tf_op | source)
XLA Modules:
  0.0 534.2 jit_solution(14820528447004337523)
XLA Ops:
  0.6 0.7 broadcast_multiply_fusion
  1.3 0.1 iota_add_fusion
  1.4 0.7 add.33.refs_1_
  2.0 4.1 shard_map.221
  6.2 183.3 %shard_map.222 = (bf16[4,2,4,64,2688]{4,3,2,1,0:T(8,128)(2,1)}, bf16[2,4,64,1024]{3,2,1,0:T(8,128)(2,1)}, bf16[4,2,256,512]{3,2,1,0:T(8,128)(2,1)}, bf16[4,2,4,6...) custom-call(s32[16]{0:T(128)} %refs_0_.3, ...), custom_call_target="tpu_custom_call" | custom-call | flops 49999998976 | bytes 157286400 | tf_op jit(solution)/shard_map/pallas_call | solution.py:1264
  189.5 63.7 %shard_map.223 = (bf16[2048,2048]{1,0:T(8,128)(2,1)}, bf16[3,512,384]{2,1,0:T(8,128)(2,1)}, bf16[3,48,2048]{2,1,0:T(8,128)(2,1)}, bf16[2048,512]{1,0:T(8,128)(2,...) custom-call(bf16[256,2048]{1,0:T(8,128)(2,1)} %get-tuple-element.93.refs_0_, ...), custom_call_target="tpu_custom_call" | custom-call | flops 49999998976 | bytes 157286400 | tf_op jit(solution)/shard_map/pallas_call | solution.py:924
  253.2 55.2 %shard_map.224 = (bf16[2048,2048]{1,0:T(8,128)(2,1)}, bf16[2048,2048]{1,0:T(8,128)(2,1)}, bf16[2048,384]{1,0:T(8,128)(2,1)}, bf16[192,2048]{1,0:T(8,128)(2,1)}, ...) custom-call(bf16[2048,2048]{1,0:T(8,128)(2,1)} %get-tuple-element.11, ...), custom_call_target="tpu_custom_call" | custom-call | flops 49999998976 | bytes 157286400 | tf_op jit(solution)/shard_map/pallas_call | solution.py:958
  308.4 94.2 %shard_map.225 = (bf16[256,2048]{1,0:T(8,128)(2,1)}, f32[256,2048]{1,0:T(8,128)}, bf16[256,2048]{1,0:T(8,128)(2,1)}, bf16[4,2,256,512]{3,2,1,0:T(8,128)(2,1)}, f...) custom-call(s32[16]{0:T(128)} %refs_0_.3, ...), custom_call_target="tpu_custom_call" | custom-call | flops 49999998976 | bytes 157286400 | tf_op jit(solution)/shard_map/pallas_call | solution.py:1430
  402.6 12.8 %shard_map.226 = (bf16[2048,2048]{1,0:T(8,128)(2,1)}, bf16[2048,2048]{1,0:T(8,128)(2,1)}, f32[256,2048]{1,0:T(8,128)}) custom-call(bf16[256,2048]{1,0:T(8,128)(2,1)} %get-tuple-element.130.attended_ref, bf16[256,2048]{1,0:T(8,128)(2,1)} %get-tuple-element.128.attn_ref.refs_1_, f32[256,2048]{1,0:T(8,128)} %get-tuple-element.129.d_middle_ref.refs_2_, ...), custom_call_target="tpu_custom_call" | custom-call | flops 6442450944 | bytes 31457280 | tf_op jit(solution)/shard_map/pallas_call | solution.py:1476
  415.4 110.4 %shard_map.227 = (bf16[256,2048]{1,0:T(8,128)(2,1)}, f32[64,2048]{1,0:T(8,128)}, f32[64,2048]{1,0:T(8,128)}, f32[64,640]{1,0:T(8,128)}, f32[48,2048]{1,0:T(8,128...) custom-call(bf16[256,2048]{1,0:T(8,128)(2,1)} %bitcast.38, ...), custom_call_target="tpu_custom_call" | custom-call | flops 49999998976 | bytes 157286400 | tf_op jit(solution)/shard_map/pallas_call | solution.py:1599
  525.8 0.0 copy-start
  525.8 0.0 copy-start.1
  525.8 4.6 shard_map.228
  530.5 0.0 copy-done
  530.5 0.0 copy-start.3
  530.5 0.0 copy-start.2
  530.5 1.0 copy.31
  531.4 0.0 copy-done.1
  531.4 1.0 copy.32
  532.4 0.0 copy-done.3
  532.4 0.8 copy.33
  533.2 0.0 copy-done.2
  533.2 0.8 copy.34
Async XLA Ops:
  525.8 4.7 copy-start
  525.8 5.6 %copy-start.1 = (bf16[256,2048]{1,0:T(8,128)(2,1)S(1)}, bf16[256,2048]{1,0:T(8,128)(2,1)}, u32[]{:S(2)}) copy-start(bf16[256,2048]{1,0:T(8,128)(2,1)} %get-tuple-element.142) | copy-start | bytes 3145732
  530.5 2.0 copy-start.3
  530.5 2.8 copy-start.2
